TPU v7x, 128 devices: a whole 4x4x4 slice. The times are simulated.
128 devices in a mesh: nodes: 128 (over z, y, x, core).
Axes of the slice: x: 4, y: 4, z: 4, core: 2. Of those that a mesh axis runs over, the one named last changes fastest.
Arguments:
- ctrl_points: float32 [3, 4194304], P(None, 'nodes'), may hold values from 0 to 128, as said below
- ctrl_disp: float32 [3, 4194304], P(None, 'nodes'), may hold values from -16 to 16
- stiffness: float32 [4194304], P('nodes'), may hold values from 0.3 to 1
- pair_rows: int32 [98304], P('nodes'), may hold values from 0 to 255, as said below
- pair_cols: int32 [98304], P('nodes'), may hold values from 1 to 511, as said below
- pair_count: int32 [128], P('nodes'), may hold values from 256 to 768, as said below
- vol_points: float32 [3, 4194304], P(None, 'nodes'), may hold values from 0 to 128, as said below
- vol_rows: int32 [65536], P('nodes'), may hold values from 0 to 255, as said below
- vol_cols: int32 [65536], P('nodes'), may hold values from 0 to 1279, as said below
- vol_count: int32 [128], P('nodes'), may hold values from 170 to 512, as said below
Outputs:
- coefficients: float32 [3, 4194304], P(None, 'nodes')
- moved: float32 [3, 4194304], P(None, 'nodes')
Inputs may be any that keep to these rules, and one draw needn't show every extreme that they name: `ctrl_points`: control block b of device d lies in the box [d, d + 1) x [2 (b // 16), 2 (b // 16) + 2) x [2 (b % 16), 2 (b % 16) + 2). `pair_rows`: A block of the device's own 256 control blocks. Below 256: an own block greater than the tile's row block; from 256 on: block pair_cols - 256 of the next device. The 768 listed pairs of one device are distinct. Only the first pair_count entries of a device's list are live; some device has all 768 live. `vol_points`: volume block b of device d lies in the box of control block b % 256 of device d. `vol_rows`: A block of the device's own 256 volume blocks. Names control block vol_cols % 256 of device d + vol_cols // 256 - 2. The 512 listed pairs of one device are distinct. Only the first vol_count entries of a device's list are live; some device has all 512 live.
All inputs are finite; a program needn't handle non-finite values.
Results may differ from a plain program's by a relative error of at most 0.0003.
Values sent between devices are 32-bit elements; how exact they have to be, the bound alone decides.
No kernel may reach another device: no remote copies, remote signals or barrier semaphores. Data moves between devices by JAX's collectives and lax.ppermute only.
A program may use at most 64 MiB of HBM per device.

v0:
```python
import math

import jax
import jax.numpy as jnp
from jax import lax
from jax.sharding import PartitionSpec as P

TILE = 128
CB = 256
VB = 256
ITERS = 3


support_radius = 2.0
exact_mode = lax.Precision.HIGHEST


def from_behind(block, axis, distance):
    devices = range(lax.axis_size(axis))
    route = [(i - distance, i) for i in devices if i - distance in devices]
    return lax.ppermute(block, axis, route)


def wendland(row_points, col_points):
    dist_sq = jnp.zeros(
        (row_points.shape[0], row_points.shape[2], col_points.shape[2]), jnp.float32
    )
    for component in range(3):
        coord_gap = row_points[:, component, :, None] - col_points[:, component, None, :]
        dist_sq = dist_sq + coord_gap * coord_gap
    scaled_r = jnp.sqrt(dist_sq) / support_radius
    falloff = jnp.maximum(1.0 - scaled_r, 0.0)
    squared = falloff * falloff
    return squared * squared * (4.0 * scaled_r + 1.0)


def to_blocks(field):
    return field.reshape(3, -1, TILE).transpose(1, 0, 2)


def from_blocks(blocks):
    return blocks.transpose(1, 0, 2).reshape(3, -1)


def place(block_ids, block_total, contrib):
    onehot = (block_ids[:, None] == lax.iota(jnp.int32, block_total)[None, :]).astype(jnp.float32)
    return jnp.einsum("gb,gkt->bkt", onehot, contrib, precision=exact_mode)


def pair_terms(row_points, col_points, row_vec, col_vec, valid_mask):
    kernel = wendland(row_points, col_points) * (valid_mask / TILE)[:, None, None]
    to_rows = (
        jnp.einsum("gkj,gij->gki", col_vec, kernel, precision=exact_mode)
        + jnp.sum(kernel, axis=2)[:, None, :] * row_vec
    )
    to_cols = (
        jnp.einsum("gki,gij->gkj", row_vec, kernel, precision=exact_mode)
        + jnp.sum(kernel, axis=1)[:, None, :] * col_vec
    )
    return (to_rows, to_cols)


def comp_sum(first_vec, second_vec):
    return jnp.sum(first_vec * second_vec, axis=(0, 2))


def residual_norm(residual):
    return lax.psum(comp_sum(residual, residual), "nodes")


def body(
    ctrl_points,
    ctrl_disp,
    stiffness,
    pair_rows,
    pair_cols,
    pair_count,
    vol_points,
    vol_rows,
    vol_cols,
    vol_count,
):
    my_index = lax.axis_index("nodes")
    device_count = lax.axis_size("nodes")
    own_points = to_blocks(ctrl_points)
    nearby = {0: own_points}
    for offset in (2, 1, -1, -2):
        nearby[offset] = to_blocks(from_behind(ctrl_points, "nodes", offset))
    stiff_blocks = stiffness.reshape(CB, TILE)
    both_points = jnp.concatenate([own_points, nearby[-1]], axis=0)
    pair_len = math.gcd(32, pair_rows.shape[0])
    diag_len = math.gcd(32, CB)
    right_exists = my_index < device_count - 1
    residual = to_blocks(ctrl_disp)
    solution = jnp.zeros_like(residual)
    direction = residual
    norm_now = residual_norm(residual)
    for step in range(ITERS):
        operate_right_vec = from_behind(direction, "nodes", -1)
        vector = direction
        both_vec = jnp.concatenate([vector, operate_right_vec], axis=0)
        live_count = pair_count[0]

        def step_pairs(step_index, totals):
            first_slot = step_index * pair_len
            row_ids = lax.dynamic_slice_in_dim(pair_rows, first_slot, pair_len)
            col_ids = lax.dynamic_slice_in_dim(pair_cols, first_slot, pair_len)
            slot_ids = first_slot + lax.iota(jnp.int32, pair_len)
            valid_mask = ((slot_ids < live_count) & ((col_ids < CB) | right_exists)).astype(
                jnp.float32
            )
            to_rows, to_cols = pair_terms(
                own_points[row_ids],
                both_points[col_ids],
                vector[row_ids],
                both_vec[col_ids],
                valid_mask,
            )
            return (
                totals[0] + place(row_ids, CB, to_rows),
                totals[1] + place(col_ids, 2 * CB, to_cols),
            )

        group_count = (live_count + pair_len - 1) // pair_len
        start_sums = (jnp.zeros_like(vector), jnp.zeros_like(both_vec))
        row_total, col_total = lax.fori_loop(0, group_count, step_pairs, start_sums)
        own_total = row_total + col_total[:CB]
        right_part = col_total[CB:]
        own_total = own_total + from_behind(right_part, "nodes", 1)
        diagonal_vector = direction

        def step_diag(step_index, totals):
            first_slot = step_index * diag_len
            block_pts = lax.dynamic_slice_in_dim(own_points, first_slot, diag_len)
            block_vec = lax.dynamic_slice_in_dim(diagonal_vector, first_slot, diag_len)
            kernel = wendland(block_pts, block_pts) / TILE
            contrib = jnp.einsum("gkj,gij->gki", block_vec, kernel, precision=exact_mode)
            return lax.dynamic_update_slice_in_dim(totals, contrib, first_slot, 0)

        image_vec = (
            own_total
            + lax.fori_loop(0, CB // diag_len, step_diag, jnp.zeros_like(diagonal_vector))
            + stiff_blocks[:, None, :] * direction
        )
        step_len = norm_now / lax.psum(comp_sum(direction, image_vec), "nodes")
        solution = solution + step_len[None, :, None] * direction
        residual = residual - step_len[None, :, None] * image_vec
        norm_next = residual_norm(residual)
        direction = residual + (norm_next / norm_now)[None, :, None] * direction
        norm_now = norm_next
    near_coef = {0: solution}
    for offset in (2, 1, -1, -2):
        near_coef[offset] = from_behind(solution, "nodes", offset)
    all_points = jnp.concatenate([nearby[2], nearby[1], nearby[0], nearby[-1], nearby[-2]], axis=0)
    all_coef = jnp.concatenate(
        [near_coef[2], near_coef[1], near_coef[0], near_coef[-1], near_coef[-2]], axis=0
    )
    volume = to_blocks(vol_points)
    vol_len = math.gcd(32, vol_rows.shape[0])
    vol_live = vol_count[0]

    def step_volume(step_index, totals):
        first_slot = step_index * vol_len
        row_ids = lax.dynamic_slice_in_dim(vol_rows, first_slot, vol_len)
        col_ids = lax.dynamic_slice_in_dim(vol_cols, first_slot, vol_len)
        slot_ids = first_slot + lax.iota(jnp.int32, vol_len)
        source_device = my_index + col_ids // CB - 2
        valid_mask = (
            (slot_ids < vol_live) & (source_device >= 0) & (source_device < device_count)
        ).astype(jnp.float32)
        kernel = wendland(volume[row_ids], all_points[col_ids]) * valid_mask[:, None, None]
        contrib = jnp.einsum("gkj,gij->gki", all_coef[col_ids], kernel, precision=exact_mode)
        return totals + place(row_ids, VB, contrib)

    vol_groups = (vol_live + vol_len - 1) // vol_len
    moved = lax.fori_loop(0, vol_groups, step_volume, jnp.zeros_like(volume))
    moved = moved * TILE ** (-0.5)
    return (from_blocks(solution), from_blocks(moved))


def solution(mesh):
    placed = (
        P(None, "nodes"),
        P(None, "nodes"),
        P("nodes"),
        P("nodes"),
        P("nodes"),
        P("nodes"),
        P(None, "nodes"),
        P("nodes"),
        P("nodes"),
        P("nodes"),
    )
    return jax.shard_map(
        body,
        mesh=mesh,
        in_specs=placed,
        out_specs=(P(None, "nodes"), P(None, "nodes")),
        check_vma=False,
    )
```

profile of v0, /device:TPU:31, one launch (start us, length us, event | category | flops | bytes accessed | tf_op | source)
XLA Modules:
  0.0 2304.6 jit_solution(14671182078828033310)
XLA Ops:
  7.3 8.4 collective-permute-done.1
  22.6 427.5 %while.99 = (s32[]{:T(128)}, f32[256,3,128]{2,0,1:T(8,128)S(1)}, f32[512,3,128]{2,0,1:T(8,128)S(1)}, s32[]{:T(128)}, s32[768]{0:T(1024)}, /*index=5*/s32[768]{0:...) while((s32[]{:T(128)}, f32[256,3,128]{2,0,1:T(8,128)S(1)}, ...), condition=%wide.region_5.6_spmd, body=%wide.region_2.5_spmd.sunk | while | flops 179145088 | bytes 3713620 | solution.py:126
  452.6 62.9 %collective-permute-start.2 = (f32[256,3,128]{2,1,0:T(4,128)}, f32[256,3,128]{2,1,0:T(4,128)}, u32[]{:S(2)}, u32[]{:S(2)}) collective-permute-start(f32[256,3,128]{2,1,0:T(4,128)} %slice.322), channel_id=1, source_target_pairs={{0,1},{1,2},{2,3},{3,4},{4,5},{5,6},{6,7},{7,8},{8,9},{9,10},{10,1... | collective-permute-start | bytes 1179656 | tf_op jit(solution)/shard_map/ppermute | solution.py:21
  515.6 43.1 %while.100 = (s32[]{:T(128)}, f32[256,3,128]{2,1,0:T(4,128)S(1)}, f32[256,3,128]{2,1,0:T(4,128)S(1)}, f32[256,3,128]{2,0,1:T(8,128)S(1)}, s32[]{:T(128)}, /*index=5*/s32[]{:T(128)}, s32[]{:T(128)}, s32[]{:T(128)}, s32[]{}, s32[]{}) while((s32[]{:T(128)}, f32[256,3,128]{2,1,0:T(4,128)S(1)}, f32[256,3,128]{2,1,0:T(4,128)S(1)}, ...), condition=%wide.region_7.8_spmd, body=%wide.region_6.7_spmd.sunk | while | flops 27787272 | bytes 328887 | solution.py:142
  560.6 63.4 %all-reduce = (f32[3]{0:T(128)S(1)}, f32[3]{0:T(128)S(1)}) all-reduce(f32[3]{0:T(128)S(1)} %get-tuple-element.963, f32[3]{0:T(128)S(1)} %get-tuple-element.962), channel_id=1, replica_groups=mesh['nodes'=128] {'nodes'}, use_global_device_ids=true, to_apply=%region_1.0 | all-reduce | flops 6 | bytes 48 | tf_op jit(solution)/shard_map/psum | solution.py:68
  625.8 64.1 %psum.44 = f32[3]{0:T(128)S(1)} all-reduce(f32[3]{0:T(128)S(1)} %get-tuple-element.1098), channel_id=1, replica_groups=mesh['nodes'=128] {'nodes'}, use_global_device_ids=true, to_apply=%region_11.12 | all-reduce | flops 3 | bytes 24 | tf_op jit(solution)/shard_map/psum | solution.py:68
  707.5 453.4 %while.101 = (s32[]{:T(128)}, f32[256,3,128]{2,0,1:T(8,128)S(1)}, f32[512,3,128]{2,0,1:T(8,128)S(1)}, s32[]{:T(128)}, s32[768]{0:T(1024)}, /*index=5*/s32[768]{0...) while((s32[]{:T(128)}, f32[256,3,128]{2,0,1:T(8,128)S(1)}, ...), condition=%wide.region_15.16_spmd, body=%wide.region_12.15_spmd.sunk | while | flops 179145088 | bytes 3713620 | solution.py:126
  1163.1 71.2 %collective-permute-start.4 = (f32[256,3,128]{2,1,0:T(4,128)}, f32[256,3,128]{2,1,0:T(4,128)}, u32[]{:S(2)}, u32[]{:S(2)}) collective-permute-start(f32[256,3,128]{2,1,0:T(4,128)} %slice.324), channel_id=1, source_target_pairs={{0,1},{1,2},{2,3},{3,4},{4,5},{5,6},{6,7},{7,8},{8,9},{9,10},{10,1... | collective-permute-start | bytes 1179656 | tf_op jit(solution)/shard_map/ppermute | solution.py:21
  1234.4 51.8 %while.102 = (s32[]{:T(128)}, f32[256,3,128]{2,1,0:T(4,128)S(1)}, f32[256,3,128]{2,1,0:T(4,128)}, f32[256,3,128]{2,0,1:T(8,128)}, s32[]{:T(128)}, /*index=5*/s32[]{:T(128)}, s32[]{:T(128)}, s32[]{:T(128)}, s32[]{}, s32[]{}) while((s32[]{:T(128)}, f32[256,3,128]{2,1,0:T(4,128)S(1)}, f32[256,3,128]{2,1,0:T(4,128)}, ...), condition=%wide.region_17.18_spmd, body=%wide.region_16.17_spmd.sunk | while | flops 27787272 | bytes 328887 | solution.py:142
  1289.0 62.3 %psum.45 = f32[3]{0:T(128)S(1)} all-reduce(f32[3]{0:T(128)S(1)} %get-tuple-element.1096), channel_id=1, replica_groups=mesh['nodes'=128] {'nodes'}, use_global_device_ids=true, to_apply=%region_19.20 | all-reduce | flops 3 | bytes 24 | tf_op jit(solution)/shard_map/psum | solution.py:145
  1351.7 64.0 %psum.46 = f32[3]{0:T(128)S(1)} all-reduce(f32[3]{0:T(128)S(1)} %multiply_reduce_fusion), channel_id=1, replica_groups=mesh['nodes'=128] {'nodes'}, use_global_device_ids=true, to_apply=%region_21.22 | all-reduce | flops 3 | bytes 24 | tf_op jit(solution)/shard_map/psum | solution.py:68
  1422.5 8.2 collective-permute-done.5
  1432.0 453.5 %while.103 = (s32[]{:T(128)}, f32[256,3,128]{2,0,1:T(8,128)S(1)}, f32[512,3,128]{2,0,1:T(8,128)S(1)}, s32[]{:T(128)}, s32[768]{0:T(1024)}, /*index=5*/s32[768]{0...) while((s32[]{:T(128)}, f32[256,3,128]{2,0,1:T(8,128)S(1)}, ...), condition=%wide.region_25.26_spmd, body=%wide.region_22.25_spmd.sunk | while | flops 179145088 | bytes 3713620 | solution.py:126
  1888.0 66.5 %collective-permute-start.6 = (f32[256,3,128]{2,1,0:T(4,128)}, f32[256,3,128]{2,1,0:T(4,128)}, u32[]{:S(2)}, u32[]{:S(2)}) collective-permute-start(f32[256,3,128]{2,1,0:T(4,128)} %slice.326), channel_id=1, source_target_pairs={{0,1},{1,2},{2,3},{3,4},{4,5},{5,6},{6,7},{7,8},{8,9},{9,10},{10,1... | collective-permute-start | bytes 1179656 | tf_op jit(solution)/shard_map/ppermute | solution.py:21
  1955.3 53.6 %while.104 = (s32[]{:T(128)}, f32[256,3,128]{2,1,0:T(4,128)}, f32[256,3,128]{2,1,0:T(4,128)S(1)}, f32[256,3,128]{2,0,1:T(8,128)}, s32[]{:T(128)}, /*index=5*/s32[]{:T(128)}, s32[]{:T(128)}, s32[]{:T(128)}, s32[]{}, s32[]{}) while((s32[]{:T(128)}, f32[256,3,128]{2,1,0:T(4,128)}, f32[256,3,128]{2,1,0:T(4,128)S(1)}, ...), condition=%wide.region_27.28_spmd, body=%wide.region_26.27_spmd.sunk | while | flops 27787272 | bytes 328887 | solution.py:142
  1956.2 5.9 fusion.317
  1962.9 5.9 fusion.317
  1969.6 5.9 fusion.317
  1976.3 5.9 fusion.317
  1982.9 5.9 fusion.317
  1989.6 5.9 fusion.317
  2012.7 62.2 %psum.47 = f32[3]{0:T(128)S(1)} all-reduce(f32[3]{0:T(128)S(1)} %fusion.222), channel_id=1, replica_groups=mesh['nodes'=128] {'nodes'}, use_global_device_ids=true, to_apply=%region_29.30 | all-reduce | flops 3 | bytes 24 | tf_op jit(solution)/shard_map/psum | solution.py:145
  2100.6 7.6 collective-permute-done.10
  2109.9 193.6 %while.105 = (s32[]{:T(128)}, f32[256,3,128]{2,0,1:T(8,128)S(1)}, s32[]{:T(128)}, s32[512]{0:T(512)}, s32[512]{0:T(512)S(1)}, /*index=5*/f32[1280,3,128]{2,1,0:T...) while((s32[]{:T(128)}, f32[256,3,128]{2,0,1:T(8,128)S(1)}, ...), condition=%wide.region_31.32_spmd, body=%wide.region_30.31_spmd.sunk | while | flops 65645508 | bytes 1533895 | solution.py:176
  (1298 shorter events, 1719.5 us)
Async XLA Ops:
  0.6 20.7 copy-start
  0.6 15.1 collective-permute-start.1
  3.4 18.0 collective-permute-start
  15.7 6.8 copy-start.8
  452.6 106.1 %collective-permute-start.2 = (f32[256,3,128]{2,1,0:T(4,128)}, f32[256,3,128]{2,1,0:T(4,128)}, u32[]{:S(2)}, u32[]{:S(2)}) collective-permute-start(f32[256,3,128]{2,1,0:T(4,128)} %slice.322), channel_id=1, source_target_pairs={{0,1},{1,2},{2,3},{3,4},{4,5},{5,6},{6,7},{7,8},{8,9},{9,10},{10,1... | collective-permute-start | bytes 1179656 | tf_op jit(solution)/shard_map/ppermute | solution.py:21
  515.6 43.1 %copy-start.6 = (f32[32768]{0:T(1024)S(1)}, f32[32768]{0:T(1024)}, u32[]{:S(2)}) copy-start(f32[32768]{0:T(1024)} %param.26) | copy-start | bytes 393220
  558.7 65.3 %copy-start.5 = (f32[256,3,128]{2,0,1:T(8,128)}, f32[256,3,128]{2,0,1:T(8,128)S(1)}, u32[]{:S(2)}) copy-start(f32[256,3,128]{2,0,1:T(8,128)S(1)} %get-tuple-element.1887) | copy-start | bytes 1179652
  690.1 16.1 collective-permute-start.3
  692.7 725.9 %collective-permute-start.11 = (f32[3,32768]{1,0:T(4,128)}, f32[3,32768]{1,0:T(4,128)}, u32[]{:S(2)}, u32[]{:S(2)}) collective-permute-start(f32[3,32768]{1,0:T(4,128)} %param.24), channel_id=1, source_target_pairs={{0,2},{1,3},{2,4},{3,5},{4,6},{5,7},{6,8},{7,9},{8,10},{9,11},{10,... | collective-permute-start | bytes 1179656 | tf_op jit(solution)/shard_map/ppermute | solution.py:21
  696.3 724.3 %collective-permute-start.12 = (f32[3,32768]{1,0:T(4,128)}, f32[3,32768]{1,0:T(4,128)}, u32[]{:S(2)}, u32[]{:S(2)}) collective-permute-start(f32[3,32768]{1,0:T(4,128)} %param.24), channel_id=1, source_target_pairs={{0,1},{1,2},{2,3},{3,4},{4,5},{5,6},{6,7},{7,8},{8,9},{9,10},{10,1... | collective-permute-start | bytes 1179656 | tf_op jit(solution)/shard_map/ppermute | solution.py:21
  701.9 1384.4 %collective-permute-start.13 = (f32[3,32768]{1,0:T(4,128)}, f32[3,32768]{1,0:T(4,128)}, u32[]{:S(2)}, u32[]{:S(2)}) collective-permute-start(f32[3,32768]{1,0:T(4,128)} %param.24), channel_id=1, source_target_pairs={{2,0},{3,1},{4,2},{5,3},{6,4},{7,5},{8,6},{9,7},{10,8},{11,9},{12,... | collective-permute-start | bytes 1179656 | tf_op jit(solution)/shard_map/ppermute | solution.py:21
  1163.1 123.1 %collective-permute-start.4 = (f32[256,3,128]{2,1,0:T(4,128)}, f32[256,3,128]{2,1,0:T(4,128)}, u32[]{:S(2)}, u32[]{:S(2)}) collective-permute-start(f32[256,3,128]{2,1,0:T(4,128)} %slice.324), channel_id=1, source_target_pairs={{0,1},{1,2},{2,3},{3,4},{4,5},{5,6},{6,7},{7,8},{8,9},{9,10},{10,1... | collective-permute-start | bytes 1179656 | tf_op jit(solution)/shard_map/ppermute | solution.py:21
  1416.0 14.7 collective-permute-start.5
  1886.1 1.0 copy-start.1
  1888.0 121.0 %collective-permute-start.6 = (f32[256,3,128]{2,1,0:T(4,128)}, f32[256,3,128]{2,1,0:T(4,128)}, u32[]{:S(2)}, u32[]{:S(2)}) collective-permute-start(f32[256,3,128]{2,1,0:T(4,128)} %slice.326), channel_id=1, source_target_pairs={{0,1},{1,2},{2,3},{3,4},{4,5},{5,6},{6,7},{7,8},{8,9},{9,10},{10,1... | collective-permute-start | bytes 1179656 | tf_op jit(solution)/shard_map/ppermute | solution.py:21
  1955.3 53.6 %copy-start.2 = (f32[512,3,128]{2,1,0:T(4,128)S(1)}, f32[512,3,128]{2,1,0:T(4,128)}, u32[]{:S(2)}) copy-start(f32[512,3,128]{2,1,0:T(4,128)} %copy-done.1) | copy-start | bytes 2359300
  2010.7 72.3 %copy-start.9 = (f32[3,32768]{1,0:T(4,128)S(1)}, f32[3,32768]{1,0:T(4,128)}, u32[]{:S(2)}) copy-start(f32[3,32768]{1,0:T(4,128)} %copy-done.8) | copy-start | bytes 1179652
  2075.3 22.3 copy-start.7
  2075.3 16.1 collective-permute-start.7
  2080.1 17.3 collective-permute-start.8
  2083.9 16.6 collective-permute-start.9
  2088.2 20.1 collective-permute-start.10
  2091.5 18.4 copy-start.12
  2108.4 1.5 copy-start.11
  (3 other events, 2.6 us)
where the time goes:
time: 2350 us; the launch traced here: 2300 us
  matrix products  886 us (38%)
  local copies, waits for them, and re-layouts  476 us (20%)
  other arithmetic  344 us (15%)
  blocking collectives  316 us (13%)
  starting transfers between devices  237 us (10%)
  waiting for transfers between devices  37.1 us (2%)
    dot_general x63, matrix products, pair_terms(): jnp.einsum('gkj,gij->gki', col_vec, kernel, precision=exact_mode)  336 us
    dot_general x63, matrix products, pair_terms(): jnp.einsum('gki,gij->gkj', row_vec, kernel, precision=exact_mode)  253 us
    ppermute x14, starting transfers between devices, from_behind(): return lax.ppermute(block, axis, route)  237 us
    psum x3, blocking collectives, residual_norm(): return lax.psum(comp_sum(residual, residual), 'nodes')  192 us
    reduce_sum x63, other arithmetic, pair_terms(): jnp.sum(kernel, axis=1)[:, None, :] * col_vec  170 us
    dot_general x24, matrix products, step_diag(): jnp.einsum('gkj,gij->gki', block_vec, kernel, precision=exact_mode)  136 us
    psum x2, blocking collectives, body(): step_len = norm_now / lax.psum(comp_sum(direction, image_vec), 'nodes')  124 us
    gather x63, local copies, waits for them, and re-layouts, step_pairs(): both_vec[col_ids]  115 us
  transfers between devices with their start and end apart: 14, of which 6 were waited for; matrix products, arithmetic and copies ran while one was open for 47% of the time, Pallas kernels for 0%

commit v1 on v0

v1 whole, which is shorter than its diff:
```python
import functools

import jax
import jax.numpy as jnp
from jax import lax
from jax.experimental import pallas as pl
from jax.experimental.pallas import tpu as pltpu
from jax.sharding import PartitionSpec as P

TILE = 128
SIDE = 16
CB = 256
VB = 256
MAXT = 768
MAXV = 512
GROUP = 16
SHIFT = 0.75
FAR = 64.0

f32 = jnp.float32
bf16 = jnp.bfloat16
i32 = jnp.int32


def from_behind(block, axis, distance):
    devices = range(lax.axis_size(axis))
    route = [(i - distance, i) for i in devices if i - distance in devices]
    return lax.ppermute(block, axis, route)


def blocks_of(field):
    return field.reshape(3, -1, TILE).transpose(1, 0, 2)


def from_blocks(blocks):
    return blocks.transpose(1, 0, 2).reshape(3, -1)


def head(value):
    return lax.reduce_precision(value, 8, 7)


def local_coords(points, device):
    blocks = blocks_of(points)
    block = lax.iota(i32, blocks.shape[0])
    centre = jnp.stack(
        [
            jnp.full(block.shape, 0.5, f32) + device.astype(f32),
            2.0 * (block // SIDE).astype(f32) + 1.0,
            2.0 * (block % SIDE).astype(f32) + 1.0,
        ],
        axis=1,
    )
    return (blocks - centre[:, :, None]) * 0.25


def column_side(local):
    one = jnp.ones_like(local[:, :1])
    return jnp.concatenate([local, local, one, jnp.zeros_like(one)], axis=1)


def row_side(local):
    one = jnp.ones_like(local[:, :1])
    norm = jnp.sum(local * local, axis=1, keepdims=True)
    full = jnp.concatenate([-2.0 * local, one, one, one, norm, jnp.zeros_like(one)], axis=1)
    high = head(full)
    mid = head(full - high)
    low = head(full - high - mid)
    last = jnp.concatenate([mid[:, :3], one, one, one, low[:, 6:7], jnp.zeros_like(one)], axis=1)
    packed = jnp.concatenate([high, high, mid, last], axis=1).astype(bf16)
    return packed.reshape(-1, TILE, TILE).transpose(0, 2, 1)


def offset_table():
    code = lax.iota(i32, 125)
    step_x = (code // 25 - 2).astype(f32) * 0.25
    step_y = (code // 5 % 5 - 2).astype(f32) * 0.5
    step_z = (code % 5 - 2).astype(f32) * 0.5
    zero = jnp.zeros_like(step_x)
    rows = jnp.stack([step_x, step_y, step_z, step_x, step_y, step_z, zero, zero], axis=1)
    return jnp.broadcast_to(rows[:, :, None], (125, 8, TILE))


def offset_code(step_x, row_cell, col_cell):
    step_y = jnp.clip(col_cell // SIDE - row_cell // SIDE, -2, 2)
    step_z = jnp.clip(col_cell % SIDE - row_cell % SIDE, -2, 2)
    return (step_x + 2) * 25 + (step_y + 2) * 5 + step_z + 2


def with_far(columns):
    return jnp.concatenate([columns, jnp.full((1, 8, TILE), FAR, f32)], axis=0)


def split_rows(vector):
    high = head(vector)
    one = jnp.ones_like(vector[:, :1])
    return jnp.concatenate([high, one, vector - high, jnp.zeros_like(one)], axis=1)


def tile_loop(groups, listed, rows_ref, cols_ref, table_ref, dist_ref, tile_ref, use):
    row = lax.broadcasted_iota(i32, (8, TILE), 0)
    coords = row < 3
    squares = (row >= 3) & (row < 6)
    unit = row == 6
    dist_ref[...] = jnp.full_like(dist_ref, FAR)
    tile_ref[...] = jnp.zeros_like(tile_ref)

    def distances(slot):
        packed = listed[slot]
        row_block = packed & 255
        moved = cols_ref[(packed >> 8) & 2047] + table_ref[packed >> 19]
        full = jnp.where(squares, moved * moved, moved)
        high = full.astype(bf16).astype(f32)
        rest = full - high
        mid = rest.astype(bf16).astype(f32)
        last = jnp.where(squares, rest - mid, jnp.where(unit, 1.0, mid))
        features = jnp.concatenate([high, mid, high, last], axis=0).astype(bf16)
        place = row_block & 3
        empty = jnp.zeros_like(features)
        spread = jnp.concatenate(
            [jnp.where(place == quarter, features, empty) for quarter in range(4)], axis=0
        )
        return jnp.dot(rows_ref[row_block >> 2], spread, preferred_element_type=f32)

    def phi(dist_sq):
        dist_sq = jnp.maximum(dist_sq, 1e-12)
        gap = jnp.maximum(0.5 - dist_sq * lax.rsqrt(dist_sq), 0.0)
        gap_sq = gap * gap
        return gap_sq * gap_sq * (0.625 - gap)

    def step(at, carry):
        use(jnp.maximum(at - 2, 0) * GROUP)
        for k in range(GROUP):
            tile_ref[k] = phi(dist_ref[k]).astype(tile_ref.dtype)
        first = jnp.minimum(at, groups - 1) * GROUP
        for k in range(GROUP):
            dist_ref[k] = distances(first + k)
        return carry

    lax.fori_loop(0, jnp.where(groups > 0, groups + 2, 0), step, 0)


def pair_body(full_image, groups, diag_list, pair_list, rows_ref, cols_ref, vec_ref, table_ref, row_out, col_out, dist_ref, tile_ref):
    row_out[...] = jnp.zeros_like(row_out)
    col_out[...] = jnp.zeros_like(col_out)
    row = lax.broadcasted_iota(i32, (8, TILE), 0)

    def two(first, second):
        return jnp.concatenate([first, second], axis=0).astype(bf16)

    def add(out, found):
        for block, value in found:
            out[block] += value

    def use_diag(first):
        found = []
        for k in range(0, GROUP, 2):
            a, b = diag_list[first + k] & 255, diag_list[first + k + 1] & 255
            left = two(jnp.where(row == 3, 0.0, vec_ref[a]), jnp.where(row == 3, 0.0, vec_ref[b]))
            image = jnp.dot(
                left, jnp.concatenate([tile_ref[k], tile_ref[k + 1]], axis=1), preferred_element_type=f32
            )
            found += [(a, image[:8, :TILE]), (b, image[8:, TILE:])]
        add(col_out, found)

    def use_pair(first):
        to_rows, to_cols = [], []
        for k in range(0, GROUP, 2):
            p, q = pair_list[first + k], pair_list[first + k + 1]
            row_a, col_a = p & 255, (p >> 8) & 2047
            row_b, col_b = q & 255, (q >> 8) & 2047
            one, other = tile_ref[k], tile_ref[k + 1]
            left = two(vec_ref[row_a], vec_ref[row_b])
            if not full_image:
                left = left * 2
            image = jnp.dot(left, jnp.concatenate([one, other], axis=1), preferred_element_type=f32)
            to_cols += [(col_a, image[:8, :TILE]), (col_b, image[8:, TILE:])]
            if full_image:
                image = lax.dot_general(
                    two(vec_ref[col_a], vec_ref[col_b]),
                    jnp.concatenate([one, other], axis=0),
                    (((1,), (1,)), ((), ())),
                    preferred_element_type=f32,
                )
                to_rows += [(row_a, image[:8, :TILE]), (row_b, image[8:, TILE:])]
        add(row_out, to_rows)
        add(col_out, to_cols)

    loop = functools.partial(
        tile_loop, rows_ref=rows_ref, cols_ref=cols_ref, table_ref=table_ref, dist_ref=dist_ref, tile_ref=tile_ref
    )
    loop(jnp.int32(CB // GROUP), diag_list, use=use_diag)
    loop(groups[0], pair_list, use=use_pair)


def pair_call(full_image, groups, diag_list, pair_list, rows, cols, vec, table):
    smem = pl.BlockSpec(memory_space=pltpu.SMEM)
    vmem = pl.BlockSpec(memory_space=pltpu.VMEM)
    return pl.pallas_call(
        functools.partial(pair_body, full_image),
        out_shape=(
            jax.ShapeDtypeStruct((CB, 8, TILE), f32),
            jax.ShapeDtypeStruct((2 * CB + 1, 8, TILE), f32),
        ),
        in_specs=[smem] * 3 + [vmem] * 4,
        out_specs=(vmem, vmem),
        scratch_shapes=[pltpu.VMEM((GROUP, TILE, TILE), f32), pltpu.VMEM((GROUP, TILE, TILE), bf16)],
        compiler_params=pltpu.CompilerParams(vmem_limit_bytes=48 * 2**20),
        name="pair_tiles",
    )(groups, diag_list, pair_list, rows, cols, vec, table)


def volume_body(groups, vol_list, rows_ref, cols_ref, coef_ref, table_ref, out, dist_ref, tile_ref):
    out[...] = jnp.zeros_like(out)

    def use(first):
        found = []
        for k in range(GROUP):
            p = vol_list[first + k]
            tile = tile_ref[k]
            high = tile.astype(bf16)
            low = (tile - high.astype(f32)).astype(bf16)
            left = coef_ref[(p >> 8) & 2047]
            left = jnp.concatenate([left, left], axis=0).astype(bf16)
            dims = (((1,), (1,)), ((), ()))
            by_high = lax.dot_general(left, high, dims, preferred_element_type=f32)
            by_low = lax.dot_general(left, low, dims, preferred_element_type=f32)
            found.append((p & 255, by_high[:8] + by_low[:8]))
        for block, value in found:
            out[block] += value

    tile_loop(groups[0], vol_list, rows_ref, cols_ref, table_ref, dist_ref, tile_ref, use)


def volume_call(groups, vol_list, rows, cols, coef, table):
    smem = pl.BlockSpec(memory_space=pltpu.SMEM)
    vmem = pl.BlockSpec(memory_space=pltpu.VMEM)
    return pl.pallas_call(
        volume_body,
        out_shape=jax.ShapeDtypeStruct((VB, 8, TILE), f32),
        in_specs=[smem] * 2 + [vmem] * 4,
        out_specs=vmem,
        scratch_shapes=[pltpu.VMEM((GROUP, TILE, TILE), f32), pltpu.VMEM((GROUP, TILE, TILE), f32)],
        compiler_params=pltpu.CompilerParams(vmem_limit_bytes=48 * 2**20),
        name="volume_tiles",
    )(groups, vol_list, rows, cols, coef, table)


def cg_weights(moment):
    def gram(first, second):
        return sum(a * b * moment[i + j] for i, a in enumerate(first) for j, b in enumerate(second))

    def image(vector):
        grown = [SHIFT * a for a in vector] + [0.0]
        return [a + (vector[k - 1] if k else 0.0) for k, a in enumerate(grown)]

    def axpy(scale, first, second):
        size = max(len(first), len(second))
        pad = lambda v: list(v) + [0.0] * (size - len(v))
        return [scale * a + b for a, b in zip(pad(first), pad(second))]

    one = jnp.ones_like(moment[0])
    residual, direction, total = [one], [one], [0.0 * one]
    norm = gram(residual, residual)
    for step in range(3):
        grown = image(direction)
        length = norm / gram(direction, grown)
        total = axpy(length, direction, total)
        if step < 2:
            residual = axpy(-length, grown, residual)
            norm_next = gram(residual, residual)
            direction = axpy(norm_next / norm, direction, residual)
            norm = norm_next
    return total


def comp_sum(first, second):
    return jnp.sum(first * second, axis=(0, 2))


def body(ctrl_points, ctrl_disp, stiffness, pair_rows, pair_cols, pair_count, vol_points, vol_rows, vol_cols, vol_count):
    me = lax.axis_index("nodes")
    devices = lax.axis_size("nodes")

    near = {0: ctrl_points}
    for offset in (-1, 1, 2, -2):
        near[offset] = from_behind(ctrl_points, "nodes", offset)
    columns = {k: column_side(local_coords(v, me - k)) for k, v in near.items()}
    rows = row_side(local_coords(ctrl_points, me))
    table = offset_table()

    slots = lax.iota(i32, MAXT)
    right = pair_cols >= CB
    live = (slots < pair_count[0]) & (~right | (me < devices - 1))
    code = offset_code(right.astype(i32), pair_rows, pair_cols % CB)
    pair_list = jnp.where(live, pair_rows | (pair_cols << 8) | (code << 19), (2 * CB) << 8)
    pair_groups = (pair_count + GROUP - 1) // GROUP
    own = lax.iota(i32, CB)
    diag_list = own | (own << 8) | (62 << 19)

    pair_columns = with_far(jnp.concatenate([columns[0], columns[-1]], axis=0))
    stiff = stiffness.reshape(CB, 1, TILE)
    no_rows = jnp.zeros((1, 8, TILE), f32)

    def product(vector, full_image):
        beside = from_behind(from_blocks(vector), "nodes", -1)
        vec = split_rows(jnp.concatenate([vector, blocks_of(beside)], axis=0))
        vec = jnp.concatenate([vec, no_rows], axis=0)
        return pair_call(full_image, pair_groups, diag_list, pair_list, rows, pair_columns, vec, table), blocks_of(beside)

    def folded(sums):
        return jnp.concatenate([sums[:, :3] + sums[:, 4:7], sums[:, 3:4]], axis=1)

    basis = [blocks_of(ctrl_disp)]
    diagonal = None
    for step in range(2):
        (to_rows, to_cols), _ = product(basis[-1], True)
        back = from_behind(folded(to_cols[CB : 2 * CB]), "nodes", 1)
        total = folded(to_rows + to_cols[:CB]) + back
        if diagonal is None:
            diagonal = stiff + total[:, 3:4]
        basis.append(total[:, :3] + (diagonal - SHIFT) * basis[-1])
    last = basis[-1]
    (_, to_cols), beside = product(last, False)
    folded_cols = folded(to_cols)[:, :3]
    quad = (
        comp_sum(folded_cols[:CB], last)
        + comp_sum(folded_cols[CB : 2 * CB], beside)
        + comp_sum((diagonal - SHIFT) * last, last)
    )
    moments = jnp.stack(
        [
            comp_sum(basis[0], basis[0]),
            comp_sum(basis[0], basis[1]),
            comp_sum(basis[1], basis[1]),
            comp_sum(basis[1], basis[2]),
            comp_sum(basis[2], basis[2]),
            quad,
        ]
    )
    moments = lax.psum(moments, "nodes")
    weights = cg_weights([moments[k] for k in range(6)])
    solution = sum(w[None, :, None] * u for w, u in zip(weights, basis))

    slots = lax.iota(i32, MAXV)
    step_x = vol_cols // CB - 2
    source = me + step_x
    live = (slots < vol_count[0]) & (source >= 0) & (source < devices)
    code = offset_code(step_x, vol_rows, vol_cols % CB)
    vol_list = jnp.where(live, vol_rows | (vol_cols << 8) | (code << 19), (5 * CB) << 8)
    vol_groups = (vol_count + GROUP - 1) // GROUP
    order = (2, 1, 0, -1, -2)
    flat = from_blocks(solution)
    near_coef = [flat if k == 0 else from_behind(flat, "nodes", k) for k in order]
    coef = jnp.concatenate([split_rows(blocks_of(c)) for c in near_coef] + [no_rows], axis=0)
    all_columns = with_far(jnp.concatenate([columns[k] for k in order], axis=0))
    vol_features = row_side(local_coords(vol_points, me))
    moved = volume_call(vol_groups, vol_list, vol_features, all_columns, coef, table)
    moved = (moved[:, :3] + moved[:, 4:7]) * (TILE**0.5)
    return (flat, from_blocks(moved))


def solution(mesh):
    split = P(None, "nodes")
    flat = P("nodes")
    return jax.shard_map(
        body,
        mesh=mesh,
        in_specs=(split, split, flat, flat, flat, flat, split, flat, flat, flat),
        out_specs=(split, split),
        check_vma=False,
    )
```

time: 2350 us -> 384 us (0.16); the launches traced: 2300 us -> 384 us
  matrix products: 886 us -> 0 us
  local copies, waits for them, and re-layouts: 476 us -> 30.4 us
  other arithmetic: 344 us -> 43 us
  blocking collectives: 316 us -> 72.9 us
  starting transfers between devices: 237 us -> 88.5 us
  Pallas kernels: 0 us -> 117 us
    dot_general x304 -> x0, matrix products: 886 us -> none  [the longest x63 336 us: pair_terms(): jnp.einsum('gkj,gij->gki', col_vec, kernel, precision=exact_mode)]
    gather x294 -> x0, local copies, waits for them, and re-layouts: 436 us -> none  [the longest x63 115 us: step_pairs(): both_vec[col_ids]]
    psum x5 -> x1, blocking collectives: 316 us -> 72.9 us  [body(): moments = lax.psum(moments, 'nodes')]
    reduce_sum x68 -> x1, other arithmetic: 178 us -> 1.37 us  [comp_sum(): return jnp.sum(first * second, axis=(0, 2))]
    ppermute x14 -> x13, starting transfers between devices: 237 us -> 88.5 us  [from_behind(): return lax.ppermute(block, axis, route)]
    pallas_call x0 -> x4, Pallas kernels: none -> 117 us  [the longest x3 80.9 us: pair_call(): pl.pallas_call(functools.partial(pair_body, full_image), out_shape=(jax.S...]
    div x68 -> x0, other arithmetic: 89.1 us -> none  [the longest x63 89.1 us: pair_terms(): valid_mask / TILE]
    select_n x140 -> x2, other arithmetic: 59.2 us -> 0.06 us  [the longest x1 0.03 us: body(): jnp.where(live, vol_rows | vol_cols << 8 | code << 19, 5 * CB << 8)]
  transfers between devices with their start and end apart: 14 -> 13, of which waited for: 6 -> 5; matrix products, arithmetic and copies ran while one was open for 47% -> 15% of each run, Pallas kernels for 0% -> 14%
where the time goes in v1:
time: 384 us
  Pallas kernels  117 us (30%)
  starting transfers between devices  88.5 us (23%)
  blocking collectives  72.9 us (19%)
  other arithmetic  43 us (11%)
  local copies, waits for them, and re-layouts  30.4 us (8%)
  waiting for transfers between devices  29.6 us (8%)
    ppermute x13, starting transfers between devices, from_behind(): return lax.ppermute(block, axis, route)  88.5 us
    pallas_call x3, Pallas kernels, pair_call(): pl.pallas_call(functools.partial(pair_body, full_image), out_shape=(jax.S...  80.9 us
    psum x1, blocking collectives, body(): moments = lax.psum(moments, 'nodes')  72.9 us
    pallas_call x1, Pallas kernels, volume_call(): pl.pallas_call(volume_body, out_shape=jax.ShapeDtypeStruct((VB, 8, TILE),...  35.9 us
    ppermute x13, waiting for transfers between devices, from_behind(): return lax.ppermute(block, axis, route)  29.6 us
    concatenate x2, local copies, waits for them, and re-layouts, row_side(): packed = jnp.concatenate([high, high, mid, last], axis=1).astype(bf16)  12.7 us
    unnamed x8, other arithmetic  9.34 us
    mul x4, other arithmetic, local_coords(): return (blocks - centre[:, :, None]) * 0.25  7.94 us
  transfers between devices with their start and end apart: 13, of which 5 were waited for; matrix products, arithmetic and copies ran while one was open for 15% of the time, Pallas kernels for 14%

profile of v1, /device:TPU:31, one launch (start us, length us, event | category | flops | bytes accessed | tf_op | source)
XLA Modules:
  0.0 384.1 jit_solution(13080921279822434474)
XLA Ops:
  0.6 2.6 collective-permute-start
  6.5 3.8 fusion.33
  11.4 6.3 %concatenate.93 = bf16[256,32,128]{2,1,0:T(8,128)(2,1)} concatenate(bf16[256,8,128]{2,1,0:T(8,128)(2,1)S(1)} %get-tuple-element.45, bf16[256,8,128]{2,1,0:T(8,128)(2,1)S(1)} %get-tuple-element.45, bf16[256,8,128]{2,1,0:T(8,128)(2,1)S(1)} %get-tuple-element.44, bf16[256,3,128]{2,1,0:T(4,128)(2,1)S(1)} %slice.144, bf16[256,3,128]{2,1,0:T(4,128)(2,1)S(1)} %broadcast.556, ...), dimensions={1} | concatenate | bytes 4194304 | tf_op jit(solution)/shard_map/concatenate | solution.py:70
  17.7 3.3 copy.15
  28.9 27.3 %pair_tiles.3 = (f32[256,8,128]{2,1,0:T(8,128)S(1)}, f32[513,8,128]{2,1,0:T(8,128)S(1)}) custom-call(s32[1]{0:T(128)S(6)} %select_n.177.groups, s32[256]{0:T(256)S(1)} %fusion.80.diag_list, s32[768]{0:T(1024)S(1)} %fusion.49.pair_list, bf16[64,128,128]{2,1,0:T(8,128)(2,1)S(1)} %bitcast.302, f32[513,8,128]{2,1,0:T(8,128)} %pad_maximum_fusion.22.cols_ref, ...), custom_call_target="tpu_custom_call" | custom-call | tf_op jit(solution)/shard_map/pair_tiles/pallas_call | solution.py:199
  56.7 26.0 %collective-permute-start.2 = (f32[256,4,128]{2,1,0:T(4,128)S(1)}, f32[256,4,128]{2,1,0:T(4,128)S(1)}, u32[]{:S(2)}, u32[]{:S(2)}) collective-permute-start(f32[256,4,128]{2,1,0:T(4,128)S(1)} %pad_maximum_fusion.27), channel_id=1, source_target_pairs={{0,1},{1,2},{2,3},{3,4},{4,5},{5,6},{6,7},{7,8},{8,9},{9,10},{10,1... | collective-permute-start | bytes 1572872 | tf_op jit(solution)/shard_map/ppermute | solution.py:28
  83.1 5.7 %collective-permute-done.2 = f32[256,4,128]{2,1,0:T(4,128)S(1)} collective-permute-done((f32[256,4,128]{2,1,0:T(4,128)S(1)}, f32[256,4,128]{2,1,0:T(4,128)S(1)}, u32[]{:S(2)}, u32[]{:S(2)}) %collective-permute-start.2) | collective-permute-done | bytes 524320 | tf_op jit(solution)/shard_map/ppermute | solution.py:28
  92.2 8.7 %collective-permute-start.6 = (f32[3,32768]{1,0:T(4,128)}, f32[3,32768]{1,0:T(4,128)}, u32[]{:S(2)}, u32[]{:S(2)}) collective-permute-start(f32[3,32768]{1,0:T(4,128)} %param.10), channel_id=1, source_target_pairs={{0,2},{1,3},{2,4},{3,5},{4,6},{5,7},{6,8},{7,9},{8,10},{9,11},{10,... | collective-permute-start | bytes 1179656 | tf_op jit(solution)/shard_map/ppermute | solution.py:28
  102.9 3.7 collective-permute-start.8
  114.3 27.3 %pair_tiles.4 = (f32[256,8,128]{2,1,0:T(8,128)S(1)}, f32[513,8,128]{2,1,0:T(8,128)S(1)}) custom-call(s32[1]{0:T(128)S(6)} %select_n.177.groups, s32[256]{0:T(256)S(1)} %fusion.80.diag_list, s32[768]{0:T(1024)S(1)} %fusion.49.pair_list, bf16[64,128,128]{2,1,0:T(8,128)(2,1)S(1)} %bitcast.303, f32[513,8,128]{2,1,0:T(8,128)} %pad_maximum_fusion.22.cols_ref, ...), custom_call_target="tpu_custom_call" | custom-call | tf_op jit(solution)/shard_map/pair_tiles/pallas_call | solution.py:199
  142.1 25.0 %collective-permute-start.4 = (f32[256,4,128]{2,1,0:T(4,128)S(1)}, f32[256,4,128]{2,1,0:T(4,128)S(1)}, u32[]{:S(2)}, u32[]{:S(2)}) collective-permute-start(f32[256,4,128]{2,1,0:T(4,128)S(1)} %pad_maximum_fusion.28), channel_id=1, source_target_pairs={{0,1},{1,2},{2,3},{3,4},{4,5},{5,6},{6,7},{7,8},{8,9},{9,10},{10,1... | collective-permute-start | bytes 1572872 | tf_op jit(solution)/shard_map/ppermute | solution.py:28
  167.5 5.7 %collective-permute-done.4 = f32[256,4,128]{2,1,0:T(4,128)S(1)} collective-permute-done((f32[256,4,128]{2,1,0:T(4,128)S(1)}, f32[256,4,128]{2,1,0:T(4,128)S(1)}, u32[]{:S(2)}, u32[]{:S(2)}) %collective-permute-start.4) | collective-permute-done | bytes 524320 | tf_op jit(solution)/shard_map/ppermute | solution.py:28
  177.9 11.3 %collective-permute-done.5 = f32[3,32768]{1,0:T(4,128)S(1)} collective-permute-done((f32[3,32768]{1,0:T(4,128)S(1)}, f32[3,32768]{1,0:T(4,128)S(1)}, u32[]{:S(2)}, u32[]{:S(2)}) %collective-permute-start.5) | collective-permute-done | bytes 393248 | tf_op jit(solution)/shard_map/ppermute | solution.py:28
  191.5 26.3 %pair_tiles.5 = (f32[256,8,128]{2,1,0:T(8,128)}, f32[513,8,128]{2,1,0:T(8,128)S(1)}) custom-call(s32[1]{0:T(128)S(6)} %select_n.177.groups, s32[256]{0:T(256)S(1)} %fusion.80.diag_list, s32[768]{0:T(1024)S(1)} %fusion.49.pair_list, bf16[64,128,128]{2,1,0:T(8,128)(2,1)S(1)} %bitcast.304, f32[513,8,128]{2,1,0:T(8,128)} %pad_maximum_fusion.22.cols_ref, ...), custom_call_target="tpu_custom_call" | custom-call | tf_op jit(solution)/shard_map/pair_tiles/pallas_call | solution.py:199
  221.7 72.9 %psum.7 = f32[6,3]{1,0:T(8,128)S(1)} all-reduce(f32[6,3]{1,0:T(8,128)S(1)} %stack.90), channel_id=1, replica_groups=mesh['nodes'=128] {'nodes'}, use_global_device_ids=true, to_apply=%region_9.10 | all-reduce | flops 18 | bytes 144 | tf_op jit(solution)/shard_map/psum | solution.py:341
  296.9 6.4 %collective-permute-start.9 = (f32[3,32768]{1,0:T(4,128)}, f32[3,32768]{1,0:T(4,128)S(1)}, u32[]{:S(2)}, u32[]{:S(2)}) collective-permute-start(f32[3,32768]{1,0:T(4,128)} %bitcast.37), channel_id=1, source_target_pairs={{0,2},{1,3},{2,4},{3,5},{4,6},{5,7},{6,8},{7,9},{8,10},{9,11},{10,... | collective-permute-start | bytes 1179656 | tf_op jit(solution)/shard_map/ppermute | solution.py:28
  305.4 2.4 collective-permute-start.10
  307.9 2.3 collective-permute-start.11
  310.2 3.5 collective-permute-start.12
  315.0 5.9 %collective-permute-done.10 = f32[3,32768]{1,0:T(4,128)S(1)} collective-permute-done((f32[3,32768]{1,0:T(4,128)}, f32[3,32768]{1,0:T(4,128)S(1)}, u32[]{:S(2)}, u32[]{:S(2)}) %collective-permute-start.10) | collective-permute-done | bytes 393248 | tf_op jit(solution)/shard_map/ppermute | solution.py:28
  329.0 6.3 %concatenate.111 = bf16[256,32,128]{2,1,0:T(8,128)(2,1)} concatenate(bf16[256,8,128]{2,1,0:T(8,128)(2,1)S(1)} %get-tuple-element.41, bf16[256,8,128]{2,1,0:T(8,128)(2,1)S(1)} %get-tuple-element.41, bf16[256,8,128]{2,1,0:T(8,128)(2,1)S(1)} %get-tuple-element.40, bf16[256,3,128]{2,1,0:T(4,128)(2,1)S(1)} %slice.158, bf16[256,3,128]{2,1,0:T(4,128)(2,1)S(1)} %copy-done.11, ...), dimensions={1} | concatenate | bytes 4194304 | tf_op jit(solution)/shard_map/concatenate | solution.py:70
  335.4 3.2 copy.18
  339.8 3.1 fusion.14
  347.2 35.9 %volume_tiles.1 = f32[256,8,128]{2,1,0:T(8,128)S(1)} custom-call(s32[1]{0:T(128)S(6)} %select_n.190.groups, s32[512]{0:T(512)S(1)} %or_select_fusion.vol_list, bf16[64,128,128]{2,1,0:T(8,128)(2,1)S(1)} %bitcast.305, f32[1281,8,128]{2,1,0:T(8,128)} %copy-done.5, f32[1281,8,128]{2,1,0:T(8,128)} %constant_dynamic-update-slice_fusion.1.coef_ref, ...), custom_call_target="tpu_custom_call" | custom-call | tf_op jit(solution)/shard_map/volume_tiles/pallas_call | solution.py:238
  (163 shorter events, 56.5 us)
Async XLA Ops:
  0.6 24.3 %collective-permute-start = (f32[3,32768]{1,0:T(4,128)}, f32[3,32768]{1,0:T(4,128)}, u32[]{:S(2)}, u32[]{:S(2)}) collective-permute-start(f32[3,32768]{1,0:T(4,128)} %param.10), channel_id=1, source_target_pairs={{1,0},{2,1},{3,2},{4,3},{5,4},{6,5},{7,6},{8,7},{9,8},{10,9},{11,1... | collective-permute-start | bytes 1179656 | tf_op jit(solution)/shard_map/ppermute | solution.py:28
  3.2 18.3 %collective-permute-start.1 = (f32[3,32768]{1,0:T(4,128)}, f32[3,32768]{1,0:T(4,128)}, u32[]{:S(2)}, u32[]{:S(2)}) collective-permute-start(f32[3,32768]{1,0:T(4,128)} %param.11), channel_id=1, source_target_pairs={{1,0},{2,1},{3,2},{4,3},{5,4},{6,5},{7,6},{8,7},{9,8},{10,9},{11,1... | collective-permute-start | bytes 1179656 | tf_op jit(solution)/shard_map/ppermute | solution.py:28
  11.3 6.4 %copy-start.10 = (bf16[256,3,128]{2,1,0:T(4,128)(2,1)}, bf16[256,3,128]{2,1,0:T(4,128)(2,1)S(1)}, u32[]{:S(2)}) copy-start(bf16[256,3,128]{2,1,0:T(4,128)(2,1)S(1)} %broadcast.556) | copy-start | bytes 589828
  11.4 6.4 %copy-start.15 = (bf16[256,1,128]{2,1,0:T(2,128)(2,1)}, bf16[256,1,128]{2,1,0:T(2,128)(2,1)S(1)}, u32[]{:S(2)}) copy-start(bf16[256,1,128]{2,1,0:T(2,128)(2,1)S(1)} %broadcast.557) | copy-start | bytes 196612
  56.7 32.1 %collective-permute-start.2 = (f32[256,4,128]{2,1,0:T(4,128)S(1)}, f32[256,4,128]{2,1,0:T(4,128)S(1)}, u32[]{:S(2)}, u32[]{:S(2)}) collective-permute-start(f32[256,4,128]{2,1,0:T(4,128)S(1)} %pad_maximum_fusion.27), channel_id=1, source_target_pairs={{0,1},{1,2},{2,3},{3,4},{4,5},{5,6},{6,7},{7,8},{8,9},{9,10},{10,1... | collective-permute-start | bytes 1572872 | tf_op jit(solution)/shard_map/ppermute | solution.py:28
  82.8 6.2 %copy-start.21 = (f32[32768]{0:T(1024)S(1)}, f32[32768]{0:T(1024)}, u32[]{:S(2)}) copy-start(f32[32768]{0:T(1024)} %param.12) | copy-start | bytes 393220
  82.8 6.5 %copy-start.1 = (f32[3,32768]{1,0:T(4,128)S(1)}, f32[3,32768]{1,0:T(4,128)}, u32[]{:S(2)}) copy-start(f32[3,32768]{1,0:T(4,128)} %param.11) | copy-start | bytes 1179652
  90.3 20.6 %collective-permute-start.3 = (f32[3,32768]{1,0:T(4,128)}, f32[3,32768]{1,0:T(4,128)}, u32[]{:S(2)}, u32[]{:S(2)}) collective-permute-start(f32[3,32768]{1,0:T(4,128)} %fusion.132), channel_id=1, source_target_pairs={{1,0},{2,1},{3,2},{4,3},{5,4},{6,5},{7,6},{8,7},{9,8},{10,9},{11,1... | collective-permute-start | bytes 1179656 | tf_op jit(solution)/shard_map/ppermute | solution.py:28
  92.2 83.5 %collective-permute-start.6 = (f32[3,32768]{1,0:T(4,128)}, f32[3,32768]{1,0:T(4,128)}, u32[]{:S(2)}, u32[]{:S(2)}) collective-permute-start(f32[3,32768]{1,0:T(4,128)} %param.10), channel_id=1, source_target_pairs={{0,2},{1,3},{2,4},{3,5},{4,6},{5,7},{6,8},{7,9},{8,10},{9,11},{10,... | collective-permute-start | bytes 1179656 | tf_op jit(solution)/shard_map/ppermute | solution.py:28
  100.9 118.5 %collective-permute-start.7 = (f32[3,32768]{1,0:T(4,128)}, f32[3,32768]{1,0:T(4,128)}, u32[]{:S(2)}, u32[]{:S(2)}) collective-permute-start(f32[3,32768]{1,0:T(4,128)} %param.10), channel_id=1, source_target_pairs={{0,1},{1,2},{2,3},{3,4},{4,5},{5,6},{6,7},{7,8},{8,9},{9,10},{10,1... | collective-permute-start | bytes 1179656 | tf_op jit(solution)/shard_map/ppermute | solution.py:28
  102.9 200.4 %collective-permute-start.8 = (f32[3,32768]{1,0:T(4,128)}, f32[3,32768]{1,0:T(4,128)}, u32[]{:S(2)}, u32[]{:S(2)}) collective-permute-start(f32[3,32768]{1,0:T(4,128)} %param.10), channel_id=1, source_target_pairs={{2,0},{3,1},{4,2},{5,3},{6,4},{7,5},{8,6},{9,7},{10,8},{11,9},{12,... | collective-permute-start | bytes 1179656 | tf_op jit(solution)/shard_map/ppermute | solution.py:28
  142.1 31.1 %collective-permute-start.4 = (f32[256,4,128]{2,1,0:T(4,128)S(1)}, f32[256,4,128]{2,1,0:T(4,128)S(1)}, u32[]{:S(2)}, u32[]{:S(2)}) collective-permute-start(f32[256,4,128]{2,1,0:T(4,128)S(1)} %pad_maximum_fusion.28), channel_id=1, source_target_pairs={{0,1},{1,2},{2,3},{3,4},{4,5},{5,6},{6,7},{7,8},{8,9},{9,10},{10,1... | collective-permute-start | bytes 1572872 | tf_op jit(solution)/shard_map/ppermute | solution.py:28
  167.1 6.1 %copy-start.2 = (f32[3,32768]{1,0:T(4,128)S(1)}, f32[3,32768]{1,0:T(4,128)}, u32[]{:S(2)}) copy-start(f32[3,32768]{1,0:T(4,128)} %param.11) | copy-start | bytes 1179652
  167.4 8.2 %copy-start.28 = (s32[512]{0:T(512)S(1)}, s32[512]{0:T(512)}, u32[]{:S(2)}) copy-start(s32[512]{0:T(512)} %param.17) | copy-start | bytes 6148
  167.4 8.2 %copy-start.29 = (s32[512]{0:T(512)S(1)}, s32[512]{0:T(512)}, u32[]{:S(2)}) copy-start(s32[512]{0:T(512)} %param.18) | copy-start | bytes 6148
  167.4 8.3 %copy-start.20 = (f32[256,3]{1,0:T(8,128)S(1)}, f32[256,3]{1,0:T(8,128)}, u32[]{:S(2)}) copy-start(f32[256,3]{1,0:T(8,128)} %copy.19) | copy-start | bytes 9220
  173.7 44.3 %copy-start.4 = (f32[256,3,128]{2,1,0:T(4,128)}, f32[256,3,128]{2,1,0:T(4,128)S(1)}, u32[]{:S(2)}) copy-start(f32[256,3,128]{2,1,0:T(4,128)S(1)} %fusion.26) | copy-start | bytes 1179652
  173.7 15.5 %collective-permute-start.5 = (f32[3,32768]{1,0:T(4,128)S(1)}, f32[3,32768]{1,0:T(4,128)S(1)}, u32[]{:S(2)}, u32[]{:S(2)}) collective-permute-start(f32[3,32768]{1,0:T(4,128)S(1)} %bitcast.309), channel_id=1, source_target_pairs={{1,0},{2,1},{3,2},{4,3},{5,4},{6,5},{7,6},{8,7},{9,8},{10,9},{11,1... | collective-permute-start | bytes 1179656 | tf_op jit(solution)/shard_map/ppermute | solution.py:28
  218.0 76.7 %copy-start.3 = (f32[3,32768]{1,0:T(4,128)S(1)}, f32[3,32768]{1,0:T(4,128)}, u32[]{:S(2)}) copy-start(f32[3,32768]{1,0:T(4,128)} %param.11) | copy-start | bytes 1179652
  219.4 83.9 %copy-start.18 = (f32[256,3]{1,0:T(8,128)S(1)}, f32[256,3]{1,0:T(8,128)}, u32[]{:S(2)}) copy-start(f32[256,3]{1,0:T(8,128)} %copy.21) | copy-start | bytes 9220
  296.9 17.9 %collective-permute-start.9 = (f32[3,32768]{1,0:T(4,128)}, f32[3,32768]{1,0:T(4,128)S(1)}, u32[]{:S(2)}, u32[]{:S(2)}) collective-permute-start(f32[3,32768]{1,0:T(4,128)} %bitcast.37), channel_id=1, source_target_pairs={{0,2},{1,3},{2,4},{3,5},{4,6},{5,7},{6,8},{7,9},{8,10},{9,11},{10,... | collective-permute-start | bytes 1179656 | tf_op jit(solution)/shard_map/ppermute | solution.py:28
  305.4 15.5 %collective-permute-start.10 = (f32[3,32768]{1,0:T(4,128)}, f32[3,32768]{1,0:T(4,128)S(1)}, u32[]{:S(2)}, u32[]{:S(2)}) collective-permute-start(f32[3,32768]{1,0:T(4,128)} %bitcast.37), channel_id=1, source_target_pairs={{0,1},{1,2},{2,3},{3,4},{4,5},{5,6},{6,7},{7,8},{8,9},{9,10},{10,1... | collective-permute-start | bytes 1179656 | tf_op jit(solution)/shard_map/ppermute | solution.py:28
  307.9 18.7 %collective-permute-start.11 = (f32[3,32768]{1,0:T(4,128)}, f32[3,32768]{1,0:T(4,128)S(1)}, u32[]{:S(2)}, u32[]{:S(2)}) collective-permute-start(f32[3,32768]{1,0:T(4,128)} %bitcast.37), channel_id=1, source_target_pairs={{1,0},{2,1},{3,2},{4,3},{5,4},{6,5},{7,6},{8,7},{9,8},{10,9},{11,1... | collective-permute-start | bytes 1179656 | tf_op jit(solution)/shard_map/ppermute | solution.py:28
  310.2 28.4 %collective-permute-start.12 = (f32[3,32768]{1,0:T(4,128)}, f32[3,32768]{1,0:T(4,128)}, u32[]{:S(2)}, u32[]{:S(2)}) collective-permute-start(f32[3,32768]{1,0:T(4,128)} %bitcast.37), channel_id=1, source_target_pairs={{2,0},{3,1},{4,2},{5,3},{6,4},{7,5},{8,6},{9,7},{10,8},{11,9},{12,... | collective-permute-start | bytes 1179656 | tf_op jit(solution)/shard_map/ppermute | solution.py:28
  (19 other events, 51.3 us)

commit v2 on v1

v2 whole, which is shorter than its diff:
```python
import functools

import jax
import jax.numpy as jnp
from jax import lax
from jax.experimental import pallas as pl
from jax.experimental.pallas import tpu as pltpu
from jax.sharding import PartitionSpec as P

TILE = 128
SIDE = 16
CB = 256
VB = 256
MAXT = 768
MAXV = 512
GROUP = 16
PART = 32
SHIFT = 0.75
FAR = 64.0

f32 = jnp.float32
bf16 = jnp.bfloat16
i32 = jnp.int32


def from_behind(block, axis, distance):
    devices = range(lax.axis_size(axis))
    route = [(i - distance, i) for i in devices if i - distance in devices]
    return lax.ppermute(block, axis, route)


def blocks_of(field):
    return field.reshape(3, -1, TILE).transpose(1, 0, 2)


def from_blocks(blocks):
    return blocks.transpose(1, 0, 2).reshape(3, -1)


def local_coords(points, device):
    blocks = blocks_of(points)
    block = lax.iota(i32, blocks.shape[0])
    centre = jnp.stack(
        [
            jnp.full(block.shape, 0.5, f32) + device.astype(f32),
            2.0 * (block // SIDE).astype(f32) + 1.0,
            2.0 * (block % SIDE).astype(f32) + 1.0,
        ],
        axis=1,
    )
    return (blocks - centre[:, :, None]) * 0.25


def payload(local, vector):
    rest = jnp.zeros((local.shape[0], 2, TILE), f32)
    return jnp.concatenate([local, vector, rest], axis=1)


def offset_table():
    code = lax.iota(i32, 125)
    step_x = (code // 25 - 2).astype(f32) * 0.25
    step_y = (code // 5 % 5 - 2).astype(f32) * 0.5
    step_z = (code % 5 - 2).astype(f32) * 0.5
    zero = jnp.zeros_like(step_x)
    rows = jnp.stack([step_x, step_y, step_z, step_x, step_y, step_z, zero, zero], axis=1)
    return jnp.broadcast_to(rows[:, :, None], (125, 8, TILE))


def offset_code(step_x, row_cell, col_cell):
    step_y = jnp.clip(col_cell // SIDE - row_cell // SIDE, -2, 2)
    step_z = jnp.clip(col_cell % SIDE - row_cell % SIDE, -2, 2)
    return (step_x + 2) * 25 + (step_y + 2) * 5 + step_z + 2


def row_ids():
    return lax.broadcasted_iota(i32, (8, TILE), 0)


def split(value):
    high = value.astype(bf16).astype(f32)
    return high, value - high


def column_rows(geo_refs, cols_ref):
    row = row_ids()
    for at, ref in enumerate(geo_refs):

        def fill(b, carry):
            for k in range(4):
                block = ref[4 * b + k]
                both = jnp.where(row < 3, block, pltpu.roll(block, 3, 0))
                cols_ref[at * CB + 4 * b + k] = jnp.where(row < 6, both, jnp.where(row == 6, 1.0, 0.0))
            return carry

        lax.fori_loop(0, CB // 4, fill, 0)
    cols_ref[len(geo_refs) * CB] = jnp.full((8, TILE), FAR, f32)


def row_features(geo_ref, rows_ref):
    row = row_ids()

    def features(block):
        coords = jnp.where(row < 3, block, 0.0)
        norm = jnp.sum(coords * coords, axis=0, keepdims=True)
        full = jnp.where(row < 3, -2.0 * coords, jnp.where(row < 6, 1.0, jnp.where(row == 6, norm, 0.0)))
        high, rest = split(full)
        mid, low = split(rest)
        last = jnp.where(row < 3, mid, jnp.where(row < 6, 1.0, jnp.where(row == 6, low, 0.0)))
        return [high, high, mid, last]

    def fill(at, carry):
        parts = []
        for k in range(4):
            parts += features(geo_ref[4 * at + k])
        turned = jnp.transpose(jnp.concatenate(parts, axis=0).astype(bf16))
        for k in range(4):
            rows_ref[4 * at + k] = turned if k == 0 else pltpu.roll(turned, TILE - k * PART, 1)
        return carry

    lax.fori_loop(0, geo_ref.shape[0] // 4, fill, 0)


def tile_loop(groups, listed, rows_ref, cols_ref, table_ref, dist_ref, tile_ref, use):
    row = row_ids()
    squares = (row >= 3) & (row < 6)
    unit = row == 6
    dist_ref[...] = jnp.full_like(dist_ref, FAR)
    tile_ref[...] = jnp.zeros_like(tile_ref)

    def distances(slot):
        packed = listed[slot]
        moved = cols_ref[(packed >> 8) & 2047] + table_ref[packed >> 19]
        full = jnp.where(squares, moved * moved, moved)
        high, rest = split(full)
        mid, low = split(rest)
        last = jnp.where(squares, low, jnp.where(unit, 1.0, mid))
        features = jnp.concatenate([high, mid, high, last], axis=0).astype(bf16)
        return jnp.dot(rows_ref[packed & 255][:, :PART], features, preferred_element_type=f32)

    def phi(dist_sq):
        dist_sq = jnp.maximum(dist_sq, 1e-12)
        gap = jnp.maximum(0.5 - dist_sq * lax.rsqrt(dist_sq), 0.0)
        gap_sq = gap * gap
        return gap_sq * gap_sq * (0.625 - gap)

    def step(at, carry):
        used = jnp.maximum(at - 2, 0) * GROUP
        first = jnp.minimum(at, groups - 1) * GROUP
        found = []
        for k in range(0, GROUP, 2):
            found += use(used, k)
            for j in (k, k + 1):
                tile_ref[j] = phi(dist_ref[j]).astype(tile_ref.dtype)
            for j in (k, k + 1):
                dist_ref[j] = distances(first + j)
        for out, block, value in found:
            out[block] += value
        return carry

    lax.fori_loop(0, jnp.where(groups > 0, groups + 2, 0), step, 0)


def pair_body(step, *refs):
    if step == 0:
        groups, diag_list, pair_list, own_geo, right_geo, table_ref = refs[:6]
        refs = refs[6:]
    else:
        groups, diag_list, pair_list, own_geo, right_geo, own_vec, right_vec, table_ref = refs[:8]
        refs = refs[8:]
    if step < 2:
        own_out, right_out = refs[:2]
        refs = refs[2:]
    else:
        (quad_out,) = refs[:1]
        refs = refs[1:]
    rows_ref, cols_ref, vec_ref, row_sum, col_sum, dist_ref, tile_ref = refs
    row = row_ids()

    column_rows((own_geo, right_geo), cols_ref)
    row_features(own_geo, rows_ref)
    for at, source in enumerate((own_geo, right_geo) if step == 0 else (own_vec, right_vec)):

        def fill(b, carry):
            for k in range(4):
                block = 4 * b + k
                if step == 0:
                    value = pltpu.roll(source[block], 5, 0)
                else:
                    value = source[:, pl.ds(pl.multiple_of(block * TILE, TILE), TILE)]
                    value = jnp.concatenate([value, jnp.zeros((5, TILE), f32)], axis=0)
                high, low = split(value)
                low = pltpu.roll(low, 4, 0)
                rows = jnp.where(row < 3, high, jnp.where(row == 3, 1.0, jnp.where(row < 7, low, 0.0)))
                vec_ref[at * CB + block] = rows
            return carry

        lax.fori_loop(0, CB // 4, fill, 0)
    vec_ref[2 * CB] = jnp.zeros((8, TILE), f32)
    row_sum[...] = jnp.zeros_like(row_sum)
    col_sum[...] = jnp.zeros_like(col_sum)

    def two(first, second):
        return jnp.concatenate([first, second], axis=0).astype(bf16)

    def use_diag(first, k):
        a, b = diag_list[first + k] & 255, diag_list[first + k + 1] & 255
        left = two(jnp.where(row == 3, 0.0, vec_ref[a]), jnp.where(row == 3, 0.0, vec_ref[b]))
        image = jnp.dot(
            left, jnp.concatenate([tile_ref[k], tile_ref[k + 1]], axis=1), preferred_element_type=f32
        )
        return [(col_sum, a, image[:8, :TILE]), (col_sum, b, image[8:, TILE:])]

    def use_pair(first, k):
        p, q = pair_list[first + k], pair_list[first + k + 1]
        row_a, col_a = p & 255, (p >> 8) & 2047
        row_b, col_b = q & 255, (q >> 8) & 2047
        one, other = tile_ref[k], tile_ref[k + 1]
        left = two(vec_ref[row_a], vec_ref[row_b])
        if step == 2:
            left = left * 2
        image = jnp.dot(left, jnp.concatenate([one, other], axis=1), preferred_element_type=f32)
        found = [(col_sum, col_a, image[:8, :TILE]), (col_sum, col_b, image[8:, TILE:])]
        if step < 2:
            image = lax.dot_general(
                two(vec_ref[col_a], vec_ref[col_b]),
                jnp.concatenate([one, other], axis=0),
                (((1,), (1,)), ((), ())),
                preferred_element_type=f32,
            )
            found += [(row_sum, row_a, image[:8, :TILE]), (row_sum, row_b, image[8:, TILE:])]
        return found

    loop = functools.partial(
        tile_loop, rows_ref=rows_ref, cols_ref=cols_ref, table_ref=table_ref, dist_ref=dist_ref, tile_ref=tile_ref
    )
    loop(jnp.int32(CB // GROUP), diag_list, use=use_diag)
    loop(groups[0], pair_list, use=use_pair)

    def fold(value):
        return value + pltpu.roll(value, 4, 0)

    if step < 2:

        def finish(b, carry):
            for k in range(4):
                block = 4 * b + k
                place = pl.ds(pl.multiple_of(block * TILE, TILE), TILE)
                own_out[:, place] = fold(row_sum[block] + col_sum[block])[:4]
                right_out[:, place] = fold(col_sum[CB + block])[:4]
            return carry

        lax.fori_loop(0, CB // 4, finish, 0)
    else:

        def finish(b, sums):
            new = []
            for k, total in enumerate(sums):
                block = 4 * b + k
                new.append(total + fold(col_sum[block]) * fold(vec_ref[block]))
            return tuple(new)

        zero = jnp.zeros((8, TILE), f32)
        sums = lax.fori_loop(0, 2 * CB // 4, finish, (zero,) * 4)
        quad_out[...] = sums[0] + sums[1] + sums[2] + sums[3]


def pair_call(step, groups, diag_list, pair_list, *arrays):
    smem = pl.BlockSpec(memory_space=pltpu.SMEM)
    vmem = pl.BlockSpec(memory_space=pltpu.VMEM)
    if step < 2:
        out = (jax.ShapeDtypeStruct((4, CB * TILE), f32),) * 2
    else:
        out = (jax.ShapeDtypeStruct((8, TILE), f32),)
    return pl.pallas_call(
        functools.partial(pair_body, step),
        out_shape=out,
        in_specs=[smem] * 3 + [vmem] * len(arrays),
        out_specs=(vmem,) * len(out),
        scratch_shapes=[
            pltpu.VMEM((CB, TILE, TILE), bf16),
            pltpu.VMEM((2 * CB + 1, 8, TILE), f32),
            pltpu.VMEM((2 * CB + 1, 8, TILE), f32),
            pltpu.VMEM((CB, 8, TILE), f32),
            pltpu.VMEM((2 * CB + 1, 8, TILE), f32),
            pltpu.VMEM((GROUP, TILE, TILE), f32),
            pltpu.VMEM((GROUP, TILE, TILE), bf16),
        ],
        compiler_params=pltpu.CompilerParams(vmem_limit_bytes=48 * 2**20),
        name=f"pair_tiles_{step}",
    )(groups, diag_list, pair_list, *arrays)


def volume_body(groups, vol_list, vol_geo, *refs):
    geos, firsts, seconds = refs[:5], refs[5:10], refs[10:15]
    table_ref, out, rows_ref, cols_ref, coef_ref, dist_ref, tile_ref = refs[15:]
    row = row_ids()
    column_rows(geos, cols_ref)
    row_features(vol_geo, rows_ref)
    for at in range(5):

        def fill(b, carry):
            for k in range(4):
                block = 4 * b + k
                place = pl.ds(pl.multiple_of(block * TILE, TILE), TILE)
                rest = jnp.zeros((5, TILE), f32)
                one = jnp.concatenate([firsts[at][:, place], rest], axis=0)
                two = jnp.concatenate([seconds[at][:, place], rest], axis=0)
                coef_ref[at * CB + block, :8] = jnp.where(row < 3, one, geos[at][block])
                coef_ref[at * CB + block, 8:] = two
            return carry

        lax.fori_loop(0, CB // 4, fill, 0)
    coef_ref[5 * CB] = jnp.zeros((16, TILE), f32)
    out[...] = jnp.zeros_like(out)

    def use(first, start):
        found = []
        dims = (((1,), (1,)), ((), ()))
        for k in (start, start + 1):
            p = vol_list[first + k]
            tile = tile_ref[k]
            high = tile.astype(bf16)
            low = (tile - high.astype(f32)).astype(bf16)
            left = coef_ref[(p >> 8) & 2047]
            left_high, left_low = split(left)
            by_high = lax.dot_general(
                jnp.concatenate([left_high, left_low], axis=0).astype(bf16), high, dims, preferred_element_type=f32
            )
            by_low = lax.dot_general(left_high.astype(bf16), low, dims, preferred_element_type=f32)
            found.append((out, p & 255, by_high[:16] + by_high[16:] + by_low))
        return found

    tile_loop(groups[0], vol_list, rows_ref, cols_ref, table_ref, dist_ref, tile_ref, use)


def volume_call(groups, vol_list, *arrays):
    smem = pl.BlockSpec(memory_space=pltpu.SMEM)
    vmem = pl.BlockSpec(memory_space=pltpu.VMEM)
    return pl.pallas_call(
        volume_body,
        out_shape=jax.ShapeDtypeStruct((VB, 16, TILE), f32),
        in_specs=[smem] * 2 + [vmem] * len(arrays),
        out_specs=vmem,
        scratch_shapes=[
            pltpu.VMEM((VB, TILE, TILE), bf16),
            pltpu.VMEM((5 * CB + 1, 8, TILE), f32),
            pltpu.VMEM((5 * CB + 1, 16, TILE), f32),
            pltpu.VMEM((GROUP, TILE, TILE), f32),
            pltpu.VMEM((GROUP, TILE, TILE), f32),
        ],
        compiler_params=pltpu.CompilerParams(vmem_limit_bytes=56 * 2**20),
        name="volume_tiles",
    )(groups, vol_list, *arrays)


def cg_weights(moment):
    def gram(first, second):
        return sum(a * b * moment[i + j] for i, a in enumerate(first) for j, b in enumerate(second))

    def image(vector):
        grown = [SHIFT * a for a in vector] + [0.0]
        return [a + (vector[k - 1] if k else 0.0) for k, a in enumerate(grown)]

    def axpy(scale, first, second):
        size = max(len(first), len(second))
        pad = lambda v: list(v) + [0.0] * (size - len(v))
        return [scale * a + b for a, b in zip(pad(first), pad(second))]

    one = jnp.ones_like(moment[0])
    residual, direction, total = [one], [one], [0.0 * one]
    norm = gram(residual, residual)
    for step in range(3):
        grown = image(direction)
        length = norm / gram(direction, grown)
        total = axpy(length, direction, total)
        if step < 2:
            residual = axpy(-length, grown, residual)
            norm_next = gram(residual, residual)
            direction = axpy(norm_next / norm, direction, residual)
            norm = norm_next
    return total


def comp_sum(first, second):
    return jnp.sum(first * second, axis=1)


def body(ctrl_points, ctrl_disp, stiffness, pair_rows, pair_cols, pair_count, vol_points, vol_rows, vol_cols, vol_count):
    me = lax.axis_index("nodes")
    devices = lax.axis_size("nodes")
    order = (2, 1, 0, -1, -2)

    geo = {0: payload(local_coords(ctrl_points, me), blocks_of(ctrl_disp))}
    for offset in (-1, 1, 2, -2):
        geo[offset] = from_behind(geo[0], "nodes", offset)
    table = offset_table()

    slots = lax.iota(i32, MAXT)
    right = pair_cols >= CB
    live = (slots < pair_count[0]) & (~right | (me < devices - 1))
    code = offset_code(right.astype(i32), pair_rows, pair_cols % CB)
    pair_list = jnp.where(live, pair_rows | (pair_cols << 8) | (code << 19), (2 * CB) << 8)
    pair_groups = (pair_count + GROUP - 1) // GROUP
    own = lax.iota(i32, CB)
    diag_list = own | (own << 8) | (62 << 19)

    slots = lax.iota(i32, MAXV)
    step_x = vol_cols // CB - 2
    source = me + step_x
    live = (slots < vol_count[0]) & (source >= 0) & (source < devices)
    code = offset_code(step_x, vol_rows, vol_cols % CB)
    vol_list = jnp.where(live, vol_rows | (vol_cols << 8) | (code << 19), (5 * CB) << 8)
    vol_groups = (vol_count + GROUP - 1) // GROUP
    vol_local = local_coords(vol_points, me)
    vol_geo = payload(vol_local, jnp.zeros_like(vol_local))

    def images(step, *vectors):
        own_part, right_part = pair_call(step, pair_groups, diag_list, pair_list, geo[0], geo[-1], *vectors, table)
        return own_part + from_behind(right_part, "nodes", 1)

    total = images(0)
    diagonal = stiffness[None, :] + total[3:4] - SHIFT
    first = total[:3] + diagonal * ctrl_disp
    near_first = {k: first if k == 0 else from_behind(first, "nodes", k) for k in (-1, 0, 1, 2, -2)}
    total = images(1, first, near_first[-1])
    second = total[:3] + diagonal * first
    near_second = {k: second if k == 0 else from_behind(second, "nodes", k) for k in (-1, 0, 1, 2, -2)}
    (quad,) = pair_call(2, pair_groups, diag_list, pair_list, geo[0], geo[-1], second, near_second[-1], table)
    moments = jnp.concatenate(
        [
            comp_sum(ctrl_disp, ctrl_disp),
            comp_sum(ctrl_disp, first),
            comp_sum(first, first),
            comp_sum(first, second),
            comp_sum(second, second),
            jnp.sum(quad, axis=1)[:3] + comp_sum(diagonal * second, second),
            jnp.zeros((TILE - 18,), f32),
        ]
    )

    parts = volume_call(
        vol_groups,
        vol_list,
        vol_geo,
        *[geo[k] for k in order],
        *[near_first[k] for k in order],
        *[near_second[k] for k in order],
        table,
    )
    moments, parts = lax.optimization_barrier((moments, parts))
    sent = jnp.broadcast_to(moments[None, None, :], (devices, 1, TILE))
    moments = jnp.sum(lax.all_to_all(sent, "nodes", 0, 0, tiled=True), axis=(0, 1))
    weights = cg_weights([moments[3 * k : 3 * k + 3] for k in range(6)])
    solution = sum(w[:, None] * u for w, u in zip(weights, (ctrl_disp, first, second)))
    scale = TILE**0.5
    parts = (parts[:, 3:6], parts[:, :3], parts[:, 8:11])
    moved = sum((scale * w)[None, :, None] * u for w, u in zip(weights, parts))
    return (solution, from_blocks(moved))


def solution(mesh):
    across = P(None, "nodes")
    flat = P("nodes")
    return jax.shard_map(
        body,
        mesh=mesh,
        in_specs=(across, across, flat, flat, flat, flat, across, flat, flat, flat),
        out_specs=(across, across),
        check_vma=False,
    )
```

time: 384 us -> 338 us (0.88); the launches traced: 384 us -> 331 us
  Pallas kernels: 117 us -> 160 us
  other arithmetic: 43 us -> 9.46 us
  local copies, waits for them, and re-layouts: 30.4 us -> 1.66 us
  blocking collectives: 72.9 us -> 46.3 us
  starting transfers between devices: 88.5 us -> 63.3 us
  waiting for transfers between devices: 29.6 us -> 48 us
    psum x1 -> x0, blocking collectives: 72.9 us -> none  [body(): moments = lax.psum(moments, 'nodes')]
    all_to_all x0 -> x1, blocking collectives: none -> 46.3 us  [body(): lax.all_to_all(sent, 'nodes', 0, 0, tiled=True)]
    pallas_call x4, Pallas kernels: 117 us -> 160 us  [the longest x3 113 us: pair_call(): pl.pallas_call(functools.partial(pair_body, step), out_shape=out, in_spec...]
    ppermute x13 -> x14, starting transfers between devices: 88.5 us -> 63.3 us  [from_behind(): return lax.ppermute(block, axis, route)]
    ppermute x13 -> x14, waiting for transfers between devices: 29.6 us -> 48 us  [from_behind(): return lax.ppermute(block, axis, route)]
    concatenate x10 -> x3, local copies, waits for them, and re-layouts: 18 us -> 0.23 us  [the longest x2 0.15 us: payload(): return jnp.concatenate([local, vector, rest], axis=1)]
    unnamed x8 -> x0, other arithmetic: 9.34 us -> none
    reduce_precision x8 -> x0, other arithmetic: 6.85 us -> none  [head(): return lax.reduce_precision(value, 8, 7)]
  transfers between devices with their start and end apart: 13 -> 14, of which waited for: 5 -> 5; matrix products, arithmetic and copies ran while one was open for 15% -> 1% of each run, Pallas kernels for 14% -> 12%
where the time goes in v2:
time: 338 us; the launch traced here: 331 us
  Pallas kernels  160 us (47%)
  starting transfers between devices  63.3 us (19%)
  waiting for transfers between devices  48 us (14%)
  blocking collectives  46.3 us (14%)
  other arithmetic  9.46 us (3%)
    pallas_call x3, Pallas kernels, pair_call(): pl.pallas_call(functools.partial(pair_body, step), out_shape=out, in_spec...  113 us
    ppermute x14, starting transfers between devices, from_behind(): return lax.ppermute(block, axis, route)  63.3 us
    ppermute x14, waiting for transfers between devices, from_behind(): return lax.ppermute(block, axis, route)  48 us
    pallas_call x1, Pallas kernels, volume_call(): pl.pallas_call(volume_body, out_shape=jax.ShapeDtypeStruct((VB, 16, TILE)...  46.9 us
    all_to_all x1, blocking collectives, body(): lax.all_to_all(sent, 'nodes', 0, 0, tiled=True)  46.3 us
  transfers between devices with their start and end apart: 14, of which 5 were waited for; matrix products, arithmetic and copies ran while one was open for 1% of the time, Pallas kernels for 12%

profile of v2, /device:TPU:31, one launch (start us, length us, event | category | flops | bytes accessed | tf_op | source)
XLA Modules:
  0.0 331.4 jit_solution(2441495180827046775)
XLA Ops:
  4.0 2.6 collective-permute-start
  7.5 16.8 %collective-permute-done.refs_4_.refs_3_ = f32[256,8,128]{2,1,0:T(8,128)S(1)} collective-permute-done((f32[256,8,128]{2,1,0:T(8,128)S(1)}, f32[256,8,128]{2,1,0:T(8,128)S(1)}, u32[]{:S(2)}, u32[]{:S(2)}) %collective-permute-start) | collective-permute-done | bytes 1048608 | tf_op jit(solution)/shard_map/ppermute | solution.py:29
  24.6 36.9 %pair_tiles_0.1 = (f32[4,32768]{1,0:T(4,128)S(1)}, f32[4,32768]{1,0:T(4,128)S(1)}) custom-call(s32[1]{0:T(128)S(6)} %select_n.146.refs_0_, s32[256]{0:T(256)S(1)} %fusion.46.refs_1_, s32[768]{0:T(1024)S(1)} %fusion.15.refs_2_, f32[256,8,128]{2,1,0:T(8,128)S(1)} %get-tuple-element.39.refs_3_.refs_2_, f32[256,8,128]{2,1,0:T(8,128)S(1)} %collective-permute-done.refs_4_.refs_3_, ...), custom_call_target="tpu_custom_call" | custom-call | tf_op jit(solution)/shard_map/pair_tiles_0/pallas_call | solution.py:274
  61.4 1.9 collective-permute-start.1
  63.4 6.1 %collective-permute-done.1 = f32[4,32768]{1,0:T(4,128)S(1)} collective-permute-done((f32[4,32768]{1,0:T(4,128)S(1)}, f32[4,32768]{1,0:T(4,128)S(1)}, u32[]{:S(2)}, u32[]{:S(2)}) %collective-permute-start.1) | collective-permute-done | bytes 524320 | tf_op jit(solution)/shard_map/ppermute | solution.py:29
  70.1 2.2 collective-permute-start.2
  72.3 13.2 %collective-permute-done.2.refs_6_.refs_8_ = f32[3,32768]{1,0:T(4,128)S(1)} collective-permute-done((f32[3,32768]{1,0:T(4,128)S(1)}, f32[3,32768]{1,0:T(4,128)S(1)}, u32[]{:S(2)}, u32[]{:S(2)}) %collective-permute-start.2) | collective-permute-done | bytes 393248 | tf_op jit(solution)/shard_map/ppermute | solution.py:29
  85.5 37.2 %pair_tiles_1.1 = (f32[4,32768]{1,0:T(4,128)S(1)}, f32[4,32768]{1,0:T(4,128)S(1)}) custom-call(s32[1]{0:T(128)S(6)} %select_n.146.refs_0_, s32[256]{0:T(256)S(1)} %fusion.46.refs_1_, s32[768]{0:T(1024)S(1)} %fusion.15.refs_2_, f32[256,8,128]{2,1,0:T(8,128)S(1)} %get-tuple-element.39.refs_3_.refs_2_, f32[256,8,128]{2,1,0:T(8,128)S(1)} %collective-permute-done.refs_4_.refs_3_, ...), custom_call_target="tpu_custom_call" | custom-call | tf_op jit(solution)/shard_map/pair_tiles_1/pallas_call | solution.py:274
  122.8 1.9 collective-permute-start.3
  126.7 8.2 %collective-permute-start.6 = (f32[256,8,128]{2,1,0:T(8,128)S(1)}, f32[256,8,128]{2,1,0:T(8,128)S(1)}, u32[]{:S(2)}, u32[]{:S(2)}) collective-permute-start(f32[256,8,128]{2,1,0:T(8,128)S(1)} %get-tuple-element.39.refs_3_.refs_2_), channel_id=1, source_target_pairs={{0,1},{1,2},{2,3},{3,4},{4,5},{5,6},{6,7},{7,8},{8,9},{9,10},{10,1... | collective-permute-start | bytes 3145736 | tf_op jit(solution)/shard_map/ppermute | solution.py:29
  134.9 11.2 %collective-permute-start.5 = (f32[256,8,128]{2,1,0:T(8,128)S(1)}, f32[256,8,128]{2,1,0:T(8,128)S(1)}, u32[]{:S(2)}, u32[]{:S(2)}) collective-permute-start(f32[256,8,128]{2,1,0:T(8,128)S(1)} %get-tuple-element.39.refs_3_.refs_2_), channel_id=1, source_target_pairs={{0,2},{1,3},{2,4},{3,5},{4,6},{5,7},{6,8},{7,9},{8,10},{9,11},{10,... | collective-permute-start | bytes 3145736 | tf_op jit(solution)/shard_map/ppermute | solution.py:29
  146.1 2.2 collective-permute-start.9
  150.1 2.1 collective-permute-start.4
  152.9 2.2 collective-permute-done.7.refs_4_
  155.1 11.8 %collective-permute-start.8 = (f32[3,32768]{1,0:T(4,128)S(1)}, f32[3,32768]{1,0:T(4,128)}, u32[]{:S(2)}, u32[]{:S(2)}) collective-permute-start(f32[3,32768]{1,0:T(4,128)S(1)} %slice_add_fusion.1.refs_5_.refs_7_), channel_id=1, source_target_pairs={{0,2},{1,3},{2,4},{3,5},{4,6},{5,7},{6,8},{7,9},{8,10},{9,11},{10,... | collective-permute-start | bytes 1179656 | tf_op jit(solution)/shard_map/ppermute | solution.py:29
  166.9 1.9 collective-permute-start.10
  168.8 9.6 %collective-permute-done.5.refs_0_ = f32[256,8,128]{2,1,0:T(8,128)S(1)} collective-permute-done((f32[256,8,128]{2,1,0:T(8,128)S(1)}, f32[256,8,128]{2,1,0:T(8,128)S(1)}, u32[]{:S(2)}, u32[]{:S(2)}) %collective-permute-start.5) | collective-permute-done | bytes 1048608 | tf_op jit(solution)/shard_map/ppermute | solution.py:29
  178.5 9.9 %collective-permute-start.11 = (f32[3,32768]{1,0:T(4,128)}, f32[3,32768]{1,0:T(4,128)}, u32[]{:S(2)}, u32[]{:S(2)}) collective-permute-start(f32[3,32768]{1,0:T(4,128)} %get-tuple-element.33.refs_5_.refs_12_), channel_id=1, source_target_pairs={{0,2},{1,3},{2,4},{3,5},{4,6},{5,7},{6,8},{7,9},{8,10},{9,11},{10,... | collective-permute-start | bytes 1179656 | tf_op jit(solution)/shard_map/ppermute | solution.py:29
  188.4 1.9 collective-permute-start.12
  190.3 3.4 %collective-permute-start.13 = (f32[3,32768]{1,0:T(4,128)}, f32[3,32768]{1,0:T(4,128)}, u32[]{:S(2)}, u32[]{:S(2)}) collective-permute-start(f32[3,32768]{1,0:T(4,128)} %get-tuple-element.33.refs_5_.refs_12_), channel_id=1, source_target_pairs={{2,0},{3,1},{4,2},{5,3},{6,4},{7,5},{8,6},{9,7},{10,8},{11,9},{12,... | collective-permute-start | bytes 1179656 | tf_op jit(solution)/shard_map/ppermute | solution.py:29
  194.4 39.1 %pair_tiles_2.1 = f32[8,128]{1,0:T(8,128)S(1)} custom-call(s32[1]{0:T(128)S(6)} %select_n.146.refs_0_, s32[256]{0:T(256)S(1)} %fusion.46.refs_1_, s32[768]{0:T(1024)S(1)} %fusion.15.refs_2_, f32[256,8,128]{2,1,0:T(8,128)S(1)} %get-tuple-element.39.refs_3_.refs_2_, f32[256,8,128]{2,1,0:T(8,128)S(1)} %collective-permute-done.refs_4_.refs_3_, ...), custom_call_target="tpu_custom_call" | custom-call | tf_op jit(solution)/shard_map/pair_tiles_2/pallas_call | solution.py:274
  234.6 46.9 %volume_tiles.1 = f32[256,16,128]{2,1,0:T(8,128)} custom-call(s32[1]{0:T(128)S(6)} %select_n.159.groups, s32[512]{0:T(512)} %or_select_fusion.vol_list, f32[256,8,128]{2,1,0:T(8,128)} %get-tuple-element.38.vol_geo, f32[256,8,128]{2,1,0:T(8,128)} %copy-done.13, f32[256,8,128]{2,1,0:T(8,128)} %copy-done.12, f32[256,8,128]{2,1,0:T(8,128)} %copy-done, ...), custom_call_target="tpu_custom_call" | custom-call | tf_op jit(solution)/shard_map/volume_tiles/pallas_call | solution.py:339
  281.6 46.3 %all_to_all.5 = f32[128,1,128]{2,1,0:T(1,128)S(1)} all-to-all(f32[128,1,128]{2,1,0:T(1,128)S(1)} %broadcast_in_dim.43), channel_id=1, replica_groups=mesh['nodes'=128] {'nodes'}, dimensions={0} | all-to-all | bytes 131072 | tf_op jit(solution)/shard_map/all_to_all | solution.py:452
  328.2 2.1 multiply_add_fusion
  (83 shorter events, 11.0 us)
Async XLA Ops:
  4.0 190.4 %copy-start = (f32[256,8,128]{2,1,0:T(8,128)}, f32[256,8,128]{2,1,0:T(8,128)S(1)}, u32[]{:S(2)}) copy-start(f32[256,8,128]{2,1,0:T(8,128)S(1)} %get-tuple-element.39.refs_3_.refs_2_) | copy-start | bytes 3145732
  4.0 20.3 %collective-permute-start = (f32[256,8,128]{2,1,0:T(8,128)S(1)}, f32[256,8,128]{2,1,0:T(8,128)S(1)}, u32[]{:S(2)}, u32[]{:S(2)}) collective-permute-start(f32[256,8,128]{2,1,0:T(8,128)S(1)} %get-tuple-element.39.refs_3_.refs_2_), channel_id=1, source_target_pairs={{1,0},{2,1},{3,2},{4,3},{5,4},{6,5},{7,6},{8,7},{9,8},{10,9},{11,1... | collective-permute-start | bytes 3145736 | tf_op jit(solution)/shard_map/ppermute | solution.py:29
  24.3 170.1 %copy-start.1 = (f32[256,8,128]{2,1,0:T(8,128)}, f32[256,8,128]{2,1,0:T(8,128)S(1)}, u32[]{:S(2)}) copy-start(f32[256,8,128]{2,1,0:T(8,128)S(1)} %collective-permute-done.refs_4_.refs_3_) | copy-start | bytes 3145732
  24.5 169.9 %copy-start.4 = (f32[125,8,128]{2,1,0:T(8,128)}, f32[125,8,128]{2,1,0:T(8,128)S(1)}, u32[]{:S(2)}) copy-start(f32[125,8,128]{2,1,0:T(8,128)S(1)} %broadcast_in_dim.19.refs_5_.refs_7_.refs_15_) | copy-start | bytes 1536004
  61.4 8.0 %collective-permute-start.1 = (f32[4,32768]{1,0:T(4,128)S(1)}, f32[4,32768]{1,0:T(4,128)S(1)}, u32[]{:S(2)}, u32[]{:S(2)}) collective-permute-start(f32[4,32768]{1,0:T(4,128)S(1)} %get-tuple-element.9), channel_id=1, source_target_pairs={{0,1},{1,2},{2,3},{3,4},{4,5},{5,6},{6,7},{7,8},{8,9},{9,10},{10,1... | collective-permute-start | bytes 1572872 | tf_op jit(solution)/shard_map/ppermute | solution.py:29
  70.1 96.8 %copy-start.2 = (f32[3,32768]{1,0:T(4,128)}, f32[3,32768]{1,0:T(4,128)S(1)}, u32[]{:S(2)}) copy-start(f32[3,32768]{1,0:T(4,128)S(1)} %slice_add_fusion.1.refs_5_.refs_7_) | copy-start | bytes 1179652
  70.1 15.5 %collective-permute-start.2 = (f32[3,32768]{1,0:T(4,128)S(1)}, f32[3,32768]{1,0:T(4,128)S(1)}, u32[]{:S(2)}, u32[]{:S(2)}) collective-permute-start(f32[3,32768]{1,0:T(4,128)S(1)} %slice_add_fusion.1.refs_5_.refs_7_), channel_id=1, source_target_pairs={{1,0},{2,1},{3,2},{4,3},{5,4},{6,5},{7,6},{8,7},{9,8},{10,9},{11,1... | collective-permute-start | bytes 1179656 | tf_op jit(solution)/shard_map/ppermute | solution.py:29
  85.5 64.5 %copy-start.6 = (f32[3,32768]{1,0:T(4,128)}, f32[3,32768]{1,0:T(4,128)S(1)}, u32[]{:S(2)}) copy-start(f32[3,32768]{1,0:T(4,128)S(1)} %collective-permute-done.2.refs_6_.refs_8_) | copy-start | bytes 1179652
  122.8 71.0 %copy-start.18 = (s32[512]{0:T(512)S(1)}, s32[512]{0:T(512)}, u32[]{:S(2)}) copy-start(s32[512]{0:T(512)} %param.17) | copy-start | bytes 6148
  122.8 71.0 %copy-start.19 = (s32[512]{0:T(512)S(1)}, s32[512]{0:T(512)}, u32[]{:S(2)}) copy-start(s32[512]{0:T(512)} %param.18) | copy-start | bytes 6148
  122.8 25.5 %collective-permute-start.3 = (f32[4,32768]{1,0:T(4,128)S(1)}, f32[4,32768]{1,0:T(4,128)S(1)}, u32[]{:S(2)}, u32[]{:S(2)}) collective-permute-start(f32[4,32768]{1,0:T(4,128)S(1)} %get-tuple-element.11), channel_id=1, source_target_pairs={{0,1},{1,2},{2,3},{3,4},{4,5},{5,6},{6,7},{7,8},{8,9},{9,10},{10,1... | collective-permute-start | bytes 1572872 | tf_op jit(solution)/shard_map/ppermute | solution.py:29
  124.7 30.3 %collective-permute-start.7 = (f32[256,8,128]{2,1,0:T(8,128)S(1)}, f32[256,8,128]{2,1,0:T(8,128)S(1)}, u32[]{:S(2)}, u32[]{:S(2)}) collective-permute-start(f32[256,8,128]{2,1,0:T(8,128)S(1)} %get-tuple-element.39.refs_3_.refs_2_), channel_id=1, source_target_pairs={{2,0},{3,1},{4,2},{5,3},{6,4},{7,5},{8,6},{9,7},{10,8},{11,9},{12,... | collective-permute-start | bytes 3145736 | tf_op jit(solution)/shard_map/ppermute | solution.py:29
  126.7 40.2 %collective-permute-start.6 = (f32[256,8,128]{2,1,0:T(8,128)S(1)}, f32[256,8,128]{2,1,0:T(8,128)S(1)}, u32[]{:S(2)}, u32[]{:S(2)}) collective-permute-start(f32[256,8,128]{2,1,0:T(8,128)S(1)} %get-tuple-element.39.refs_3_.refs_2_), channel_id=1, source_target_pairs={{0,1},{1,2},{2,3},{3,4},{4,5},{5,6},{6,7},{7,8},{8,9},{9,10},{10,1... | collective-permute-start | bytes 3145736 | tf_op jit(solution)/shard_map/ppermute | solution.py:29
  134.9 43.5 %collective-permute-start.5 = (f32[256,8,128]{2,1,0:T(8,128)S(1)}, f32[256,8,128]{2,1,0:T(8,128)S(1)}, u32[]{:S(2)}, u32[]{:S(2)}) collective-permute-start(f32[256,8,128]{2,1,0:T(8,128)S(1)} %get-tuple-element.39.refs_3_.refs_2_), channel_id=1, source_target_pairs={{0,2},{1,3},{2,4},{3,5},{4,6},{5,7},{6,8},{7,9},{8,10},{9,11},{10,... | collective-permute-start | bytes 3145736 | tf_op jit(solution)/shard_map/ppermute | solution.py:29
  146.1 42.2 %collective-permute-start.9 = (f32[3,32768]{1,0:T(4,128)S(1)}, f32[3,32768]{1,0:T(4,128)S(1)}, u32[]{:S(2)}, u32[]{:S(2)}) collective-permute-start(f32[3,32768]{1,0:T(4,128)S(1)} %slice_add_fusion.1.refs_5_.refs_7_), channel_id=1, source_target_pairs={{0,1},{1,2},{2,3},{3,4},{4,5},{5,6},{6,7},{7,8},{8,9},{9,10},{10,1... | collective-permute-start | bytes 1179656 | tf_op jit(solution)/shard_map/ppermute | solution.py:29
  150.1 40.2 %collective-permute-start.4 = (f32[3,32768]{1,0:T(4,128)}, f32[3,32768]{1,0:T(4,128)S(1)}, u32[]{:S(2)}, u32[]{:S(2)}) collective-permute-start(f32[3,32768]{1,0:T(4,128)} %get-tuple-element.33.refs_5_.refs_12_), channel_id=1, source_target_pairs={{1,0},{2,1},{3,2},{4,3},{5,4},{6,5},{7,6},{8,7},{9,8},{10,9},{11,1... | collective-permute-start | bytes 1179656 | tf_op jit(solution)/shard_map/ppermute | solution.py:29
  155.1 79.5 %collective-permute-start.8 = (f32[3,32768]{1,0:T(4,128)S(1)}, f32[3,32768]{1,0:T(4,128)}, u32[]{:S(2)}, u32[]{:S(2)}) collective-permute-start(f32[3,32768]{1,0:T(4,128)S(1)} %slice_add_fusion.1.refs_5_.refs_7_), channel_id=1, source_target_pairs={{0,2},{1,3},{2,4},{3,5},{4,6},{5,7},{6,8},{7,9},{8,10},{9,11},{10,... | collective-permute-start | bytes 1179656 | tf_op jit(solution)/shard_map/ppermute | solution.py:29
  166.9 67.7 %collective-permute-start.10 = (f32[3,32768]{1,0:T(4,128)S(1)}, f32[3,32768]{1,0:T(4,128)}, u32[]{:S(2)}, u32[]{:S(2)}) collective-permute-start(f32[3,32768]{1,0:T(4,128)S(1)} %slice_add_fusion.1.refs_5_.refs_7_), channel_id=1, source_target_pairs={{2,0},{3,1},{4,2},{5,3},{6,4},{7,5},{8,6},{9,7},{10,8},{11,9},{12,... | collective-permute-start | bytes 1179656 | tf_op jit(solution)/shard_map/ppermute | solution.py:29
  178.5 56.1 %collective-permute-start.11 = (f32[3,32768]{1,0:T(4,128)}, f32[3,32768]{1,0:T(4,128)}, u32[]{:S(2)}, u32[]{:S(2)}) collective-permute-start(f32[3,32768]{1,0:T(4,128)} %get-tuple-element.33.refs_5_.refs_12_), channel_id=1, source_target_pairs={{0,2},{1,3},{2,4},{3,5},{4,6},{5,7},{6,8},{7,9},{8,10},{9,11},{10,... | collective-permute-start | bytes 1179656 | tf_op jit(solution)/shard_map/ppermute | solution.py:29
  188.4 46.2 %collective-permute-start.12 = (f32[3,32768]{1,0:T(4,128)}, f32[3,32768]{1,0:T(4,128)}, u32[]{:S(2)}, u32[]{:S(2)}) collective-permute-start(f32[3,32768]{1,0:T(4,128)} %get-tuple-element.33.refs_5_.refs_12_), channel_id=1, source_target_pairs={{0,1},{1,2},{2,3},{3,4},{4,5},{5,6},{6,7},{7,8},{8,9},{9,10},{10,1... | collective-permute-start | bytes 1179656 | tf_op jit(solution)/shard_map/ppermute | solution.py:29
  190.3 44.3 %collective-permute-start.13 = (f32[3,32768]{1,0:T(4,128)}, f32[3,32768]{1,0:T(4,128)}, u32[]{:S(2)}, u32[]{:S(2)}) collective-permute-start(f32[3,32768]{1,0:T(4,128)} %get-tuple-element.33.refs_5_.refs_12_), channel_id=1, source_target_pairs={{2,0},{3,1},{4,2},{5,3},{6,4},{7,5},{8,6},{9,7},{10,8},{11,9},{12,... | collective-permute-start | bytes 1179656 | tf_op jit(solution)/shard_map/ppermute | solution.py:29
  234.6 93.6 %copy-start.3 = (f32[3,32768]{1,0:T(4,128)S(1)}, f32[3,32768]{1,0:T(4,128)}, u32[]{:S(2)}) copy-start(f32[3,32768]{1,0:T(4,128)} %copy-done.2) | copy-start | bytes 1179652
  234.6 93.6 %copy-start.9 = (f32[3,32768]{1,0:T(4,128)S(1)}, f32[3,32768]{1,0:T(4,128)}, u32[]{:S(2)}) copy-start(f32[3,32768]{1,0:T(4,128)} %param.11) | copy-start | bytes 1179652
  281.6 48.8 %copy-start.10 = (f32[256,16,128]{2,1,0:T(8,128)S(1)}, f32[256,16,128]{2,1,0:T(8,128)}, u32[]{:S(2)}) copy-start(f32[256,16,128]{2,1,0:T(8,128)} %volume_tiles.1) | copy-start | bytes 6291460
  (10 other events, 190.4 us)

commit v3 on v2

v3 whole, which is shorter than its diff:
```python
import functools

import jax
import jax.numpy as jnp
from jax import lax
from jax.experimental import pallas as pl
from jax.experimental.pallas import tpu as pltpu
from jax.sharding import PartitionSpec as P

TILE = 128
SIDE = 16
CB = 256
VB = 256
MAXT = 768
MAXV = 512
GROUP = 16
PART = 32
SHIFT = 0.75
FAR = 64.0

f32 = jnp.float32
bf16 = jnp.bfloat16
i32 = jnp.int32


def from_behind(block, axis, distance):
    devices = range(lax.axis_size(axis))
    route = [(i - distance, i) for i in devices if i - distance in devices]
    return lax.ppermute(block, axis, route)


def local_coords(points, device):
    block = lax.iota(i32, points.shape[1]) // TILE
    centre = jnp.stack(
        [
            jnp.full(block.shape, 0.5, f32) + device.astype(f32),
            2.0 * (block // SIDE).astype(f32) + 1.0,
            2.0 * (block % SIDE).astype(f32) + 1.0,
        ]
    )
    return (points - centre) * 0.25


def offset_table():
    code = lax.iota(i32, 125)
    step_x = (code // 25 - 2).astype(f32) * 0.25
    step_y = (code // 5 % 5 - 2).astype(f32) * 0.5
    step_z = (code % 5 - 2).astype(f32) * 0.5
    zero = jnp.zeros_like(step_x)
    rows = jnp.stack([step_x, step_y, step_z, step_x, step_y, step_z, zero, zero], axis=1)
    return jnp.broadcast_to(rows[:, :, None], (125, 8, TILE))


def offset_code(step_x, row_cell, col_cell):
    step_y = jnp.clip(col_cell // SIDE - row_cell // SIDE, -2, 2)
    step_z = jnp.clip(col_cell % SIDE - row_cell % SIDE, -2, 2)
    return (step_x + 2) * 25 + (step_y + 2) * 5 + step_z + 2


def row_ids():
    return lax.broadcasted_iota(i32, (8, TILE), 0)


def split(value):
    high = value.astype(bf16).astype(f32)
    return high, value - high


def three_rows(ref, first, count):
    value = ref[:, pl.ds(pl.multiple_of(first * TILE, count * TILE), count * TILE)]
    rest = jnp.zeros((5, TILE), f32)
    return [jnp.concatenate([value[:, k * TILE : (k + 1) * TILE], rest], axis=0) for k in range(count)]


def each_chunk(count, todo):
    def step(at, carry):
        todo(8 * at)
        return carry

    lax.fori_loop(0, count // 8, step, 0)


def column_rows(geo_refs, cols_ref):
    unit = jnp.where(row_ids() == 6, 1.0, 0.0)
    for at, ref in enumerate(geo_refs):

        def fill(first):
            rows = [block + pltpu.roll(block, 3, 0) + unit for block in three_rows(ref, first, 8)]
            cols_ref[pl.ds(at * CB + first, 8)] = jnp.stack(rows)

        each_chunk(CB, fill)
    cols_ref[len(geo_refs) * CB] = jnp.full((8, TILE), FAR, f32)


def vector_rows(refs, vec_ref, unit):
    unit = jnp.where(row_ids() == 3, unit, 0.0)
    for at, ref in enumerate(refs):

        def fill(first):
            rows = []
            for block in three_rows(ref, first, 8):
                high, low = split(block)
                rows.append(high + pltpu.roll(low, 4, 0) + unit)
            vec_ref[pl.ds(at * CB + first, 8)] = jnp.stack(rows)

        each_chunk(CB, fill)
    vec_ref[len(refs) * CB] = jnp.zeros((8, TILE), f32)


def row_features(geo_ref, rows_ref, first, count):
    row = row_ids()
    middle = (row >= 3) & (row < 6)

    def features(coords):
        norm = jnp.sum(coords * coords, axis=0, keepdims=True)
        full = jnp.where(middle, 1.0, jnp.where(row == 6, norm, -2.0 * coords))
        high, rest = split(full)
        mid, low = split(rest)
        last = jnp.where(row < 3, mid, jnp.where(middle, 1.0, low))
        return [high, high, mid, last]

    blocks = three_rows(geo_ref, first, count)
    for k in range(0, count, 4):
        parts = []
        for j in range(4):
            parts += features(blocks[k + j])
        turned = jnp.transpose(jnp.concatenate(parts, axis=0).astype(bf16))
        for j in range(4):
            rows_ref[first + k + j] = turned if j == 0 else pltpu.roll(turned, TILE - j * PART, 1)


def tile_loop(groups, listed, rows_ref, cols_ref, table_ref, dist_ref, tile_ref, use, ahead=None):
    row = row_ids()
    squares = (row >= 3) & (row < 6)
    unit = row == 6
    dist_ref[...] = jnp.full_like(dist_ref, FAR)
    tile_ref[...] = jnp.zeros_like(tile_ref)

    def distances(slot):
        packed = listed[slot]
        moved = cols_ref[(packed >> 8) & 2047] + table_ref[packed >> 19]
        full = jnp.where(squares, moved * moved, moved)
        high, rest = split(full)
        mid, low = split(rest)
        last = jnp.where(squares, low, jnp.where(unit, 1.0, mid))
        features = jnp.concatenate([high, mid, high, last], axis=0).astype(bf16)
        return jnp.dot(rows_ref[packed & 255][:, :PART], features, preferred_element_type=f32)

    def phi(dist_sq):
        dist_sq = jnp.maximum(dist_sq, 1e-12)
        gap = jnp.maximum(0.5 - dist_sq * lax.rsqrt(dist_sq), 0.0)
        gap_sq = gap * gap
        return gap_sq * gap_sq * (0.625 - gap)

    def step(at, carry):
        used = jnp.maximum(at - 2, 0) * GROUP
        first = jnp.minimum(at, groups - 1) * GROUP
        found = []
        for k in range(0, GROUP, 2):
            found += use(used, k)
            for j in (k, k + 1):
                tile_ref[j] = phi(dist_ref[j]).astype(tile_ref.dtype)
            for j in (k, k + 1):
                dist_ref[j] = distances(first + j)
        for out, block, value in found:
            out[block] += value
        if ahead is not None:
            ahead(jnp.minimum(at + 1, groups - 1) * GROUP)
        return carry

    lax.fori_loop(0, jnp.where(groups > 0, groups + 2, 0), step, 0)


def pair_body(step, groups, diag_list, pair_list, own_geo, right_geo, own_vec, right_vec, table_ref, *refs):
    outs, refs = refs[: 2 if step < 2 else 1], refs[2 if step < 2 else 1 :]
    rows_ref, cols_ref, vec_ref, row_sum, col_sum, dist_ref, tile_ref = refs
    row = row_ids()

    column_rows((own_geo, right_geo), cols_ref)
    vector_rows((own_vec, right_vec), vec_ref, 1.0)
    row_sum[...] = jnp.zeros_like(row_sum)
    col_sum[...] = jnp.zeros_like(col_sum)

    def two(first, second):
        return jnp.concatenate([first, second], axis=0).astype(bf16)

    def use_diag(first, k):
        a, b = diag_list[first + k] & 255, diag_list[first + k + 1] & 255
        left = two(jnp.where(row == 3, 0.0, vec_ref[a]), jnp.where(row == 3, 0.0, vec_ref[b]))
        image = jnp.dot(
            left, jnp.concatenate([tile_ref[k], tile_ref[k + 1]], axis=1), preferred_element_type=f32
        )
        return [(col_sum, a, image[:8, :TILE]), (col_sum, b, image[8:, TILE:])]

    def use_pair(first, k):
        p, q = pair_list[first + k], pair_list[first + k + 1]
        row_a, col_a = p & 255, (p >> 8) & 2047
        row_b, col_b = q & 255, (q >> 8) & 2047
        one, other = tile_ref[k], tile_ref[k + 1]
        left = two(vec_ref[row_a], vec_ref[row_b])
        if step == 2:
            left = left * 2
        image = jnp.dot(left, jnp.concatenate([one, other], axis=1), preferred_element_type=f32)
        found = [(col_sum, col_a, image[:8, :TILE]), (col_sum, col_b, image[8:, TILE:])]
        if step < 2:
            image = lax.dot_general(
                two(vec_ref[col_a], vec_ref[col_b]),
                jnp.concatenate([one, other], axis=0),
                (((1,), (1,)), ((), ())),
                preferred_element_type=f32,
            )
            found += [(row_sum, row_a, image[:8, :TILE]), (row_sum, row_b, image[8:, TILE:])]
        return found

    loop = functools.partial(
        tile_loop, rows_ref=rows_ref, cols_ref=cols_ref, table_ref=table_ref, dist_ref=dist_ref, tile_ref=tile_ref
    )
    ahead = functools.partial(row_features, own_geo, rows_ref, count=GROUP)
    ahead(0)
    loop(jnp.int32(CB // GROUP), diag_list, use=use_diag, ahead=ahead)
    loop(groups[0], pair_list, use=use_pair)

    def fold(value):
        return value + pltpu.roll(value, 4, 0)

    if step < 2:
        own_out, right_out = outs

        def finish(first):
            place = pl.ds(pl.multiple_of(first * TILE, 8 * TILE), 8 * TILE)
            own, right = row_sum[pl.ds(first, 8)] + col_sum[pl.ds(first, 8)], col_sum[pl.ds(CB + first, 8)]
            own_out[:, place] = jnp.concatenate([fold(own[k])[:4] for k in range(8)], axis=1)
            right_out[:, place] = jnp.concatenate([fold(right[k])[:4] for k in range(8)], axis=1)

        each_chunk(CB, finish)
    else:
        (quad_out,) = outs

        def finish(at, sums):
            return tuple(
                total + fold(col_sum[8 * at + k]) * fold(vec_ref[8 * at + k]) for k, total in enumerate(sums)
            )

        zero = jnp.zeros((8, TILE), f32)
        sums = lax.fori_loop(0, 2 * CB // 8, finish, (zero,) * 8)
        quad_out[...] = sum(sums)


def pair_call(step, groups, diag_list, pair_list, *arrays):
    smem = pl.BlockSpec(memory_space=pltpu.SMEM)
    vmem = pl.BlockSpec(memory_space=pltpu.VMEM)
    if step < 2:
        out = (jax.ShapeDtypeStruct((4, CB * TILE), f32),) * 2
    else:
        out = (jax.ShapeDtypeStruct((8, TILE), f32),)
    return pl.pallas_call(
        functools.partial(pair_body, step),
        out_shape=out,
        in_specs=[smem] * 3 + [vmem] * len(arrays),
        out_specs=(vmem,) * len(out),
        scratch_shapes=[
            pltpu.VMEM((CB, TILE, TILE), bf16),
            pltpu.VMEM((2 * CB + 1, 8, TILE), f32),
            pltpu.VMEM((2 * CB + 1, 8, TILE), f32),
            pltpu.VMEM((CB, 8, TILE), f32),
            pltpu.VMEM((2 * CB + 1, 8, TILE), f32),
            pltpu.VMEM((GROUP, TILE, TILE), f32),
            pltpu.VMEM((GROUP, TILE, TILE), bf16),
        ],
        compiler_params=pltpu.CompilerParams(vmem_limit_bytes=48 * 2**20),
        name=f"pair_tiles_{step}",
    )(groups, diag_list, pair_list, *arrays)


def volume_body(groups, vol_list, vol_geo, *refs):
    geos, coefs = refs[:5], refs[5:10]
    table_ref, out, rows_ref, cols_ref, coef_ref, sums, dist_ref, tile_ref = refs[10:]
    column_rows(geos, cols_ref)
    vector_rows(coefs, coef_ref, 0.0)
    sums[...] = jnp.zeros_like(sums)

    def features(at, carry):
        row_features(vol_geo, rows_ref, at * 16, 16)
        return carry

    lax.fori_loop(0, VB // 16, features, 0)

    def use(first, k):
        dims = (((1,), (1,)), ((), ()))
        p, q = vol_list[first + k], vol_list[first + k + 1]
        left = jnp.concatenate([coef_ref[(p >> 8) & 2047], coef_ref[(q >> 8) & 2047]], axis=0).astype(bf16)
        highs, lows = [], []
        for j in (k, k + 1):
            tile = tile_ref[j]
            high = tile.astype(bf16)
            highs.append(high)
            lows.append((tile - high.astype(f32)).astype(bf16))
        image = lax.dot_general(left, jnp.concatenate(highs, axis=0), dims, preferred_element_type=f32)
        image += lax.dot_general(left, jnp.concatenate(lows, axis=0), dims, preferred_element_type=f32)
        return [(sums, p & 255, image[:8, :TILE]), (sums, q & 255, image[8:, TILE:])]

    tile_loop(groups[0], vol_list, rows_ref, cols_ref, table_ref, dist_ref, tile_ref, use)

    def finish(first):
        value = sums[pl.ds(first, 8)]
        rows = [(value[k] + pltpu.roll(value[k], 4, 0))[:3] for k in range(8)]
        out[:, pl.ds(pl.multiple_of(first * TILE, 8 * TILE), 8 * TILE)] = jnp.concatenate(rows, axis=1) * TILE**0.5

    each_chunk(VB, finish)


def volume_call(groups, vol_list, *arrays):
    smem = pl.BlockSpec(memory_space=pltpu.SMEM)
    vmem = pl.BlockSpec(memory_space=pltpu.VMEM)
    return pl.pallas_call(
        volume_body,
        out_shape=jax.ShapeDtypeStruct((3, VB * TILE), f32),
        in_specs=[smem] * 2 + [vmem] * len(arrays),
        out_specs=vmem,
        scratch_shapes=[
            pltpu.VMEM((VB, TILE, TILE), bf16),
            pltpu.VMEM((5 * CB + 1, 8, TILE), f32),
            pltpu.VMEM((5 * CB + 1, 8, TILE), f32),
            pltpu.VMEM((VB, 8, TILE), f32),
            pltpu.VMEM((GROUP, TILE, TILE), f32),
            pltpu.VMEM((GROUP, TILE, TILE), f32),
        ],
        compiler_params=pltpu.CompilerParams(vmem_limit_bytes=56 * 2**20),
        name="volume_tiles",
    )(groups, vol_list, *arrays)


def cg_weights(moment):
    def gram(first, second):
        return sum(a * b * moment[i + j] for i, a in enumerate(first) for j, b in enumerate(second))

    def image(vector):
        grown = [SHIFT * a for a in vector] + [0.0]
        return [a + (vector[k - 1] if k else 0.0) for k, a in enumerate(grown)]

    def axpy(scale, first, second):
        size = max(len(first), len(second))
        pad = lambda v: list(v) + [0.0] * (size - len(v))
        return [scale * a + b for a, b in zip(pad(first), pad(second))]

    one = jnp.ones_like(moment[0])
    residual, direction, total = [one], [one], [0.0 * one]
    norm = gram(residual, residual)
    for step in range(3):
        grown = image(direction)
        length = norm / gram(direction, grown)
        total = axpy(length, direction, total)
        if step < 2:
            residual = axpy(-length, grown, residual)
            norm_next = gram(residual, residual)
            direction = axpy(norm_next / norm, direction, residual)
            norm = norm_next
    return total


def comp_sum(first, second):
    return jnp.sum(first * second, axis=1)


def body(ctrl_points, ctrl_disp, stiffness, pair_rows, pair_cols, pair_count, vol_points, vol_rows, vol_cols, vol_count):
    me = lax.axis_index("nodes")
    devices = lax.axis_size("nodes")
    order = (2, 1, 0, -1, -2)

    geo = {0: local_coords(ctrl_points, me)}
    geo[-1] = from_behind(geo[0], "nodes", -1)
    beside = from_behind(ctrl_disp, "nodes", -1)
    for offset in (1, 2, -2):
        geo[offset] = from_behind(geo[0], "nodes", offset)
    table = offset_table()

    slots = lax.iota(i32, MAXT)
    right = pair_cols >= CB
    live = (slots < pair_count[0]) & (~right | (me < devices - 1))
    code = offset_code(right.astype(i32), pair_rows, pair_cols % CB)
    pair_list = jnp.where(live, pair_rows | (pair_cols << 8) | (code << 19), (2 * CB) << 8)
    pair_groups = (pair_count + GROUP - 1) // GROUP
    own = lax.iota(i32, CB)
    diag_list = own | (own << 8) | (62 << 19)

    slots = lax.iota(i32, MAXV)
    step_x = vol_cols // CB - 2
    source = me + step_x
    live = (slots < vol_count[0]) & (source >= 0) & (source < devices)
    code = offset_code(step_x, vol_rows, vol_cols % CB)
    vol_list = jnp.where(live, vol_rows | (vol_cols << 8) | (code << 19), (5 * CB) << 8)
    vol_groups = (vol_count + GROUP - 1) // GROUP
    vol_geo = local_coords(vol_points, me)

    def images(step, *vectors):
        return pair_call(step, pair_groups, diag_list, pair_list, geo[0], geo[-1], *vectors, table)

    own_part, right_part = images(0, ctrl_disp, beside)
    total = own_part + from_behind(right_part, "nodes", 1)
    diagonal = stiffness[None, :] + total[3:4] - SHIFT
    first = total[:3] + diagonal * ctrl_disp
    own_part, right_part = images(1, first, from_behind(first, "nodes", -1))
    total = own_part + from_behind(right_part, "nodes", 1)
    second = total[:3] + diagonal * first
    (quad,) = images(2, second, from_behind(second, "nodes", -1))
    moments = jnp.concatenate(
        [
            comp_sum(ctrl_disp, ctrl_disp),
            comp_sum(ctrl_disp, first),
            comp_sum(first, first),
            comp_sum(first, second),
            comp_sum(second, second),
            jnp.sum(quad, axis=1)[:3] + comp_sum(diagonal * second, second),
            jnp.zeros((TILE - 18,), f32),
        ]
    )

    sent = jnp.broadcast_to(moments[None, None, :], (devices, 1, TILE))
    moments = jnp.sum(lax.all_to_all(sent, "nodes", 0, 0, tiled=True), axis=(0, 1))
    weights = cg_weights([moments[3 * k : 3 * k + 3] for k in range(6)])
    coef = sum(w[:, None] * u for w, u in zip(weights, (ctrl_disp, first, second)))
    near = [coef if k == 0 else from_behind(coef, "nodes", k) for k in order]
    moved = volume_call(vol_groups, vol_list, vol_geo, *[geo[k] for k in order], *near, table)
    return (coef, moved)


def solution(mesh):
    across = P(None, "nodes")
    flat = P("nodes")
    return jax.shard_map(
        body,
        mesh=mesh,
        in_specs=(across, across, flat, flat, flat, flat, across, flat, flat, flat),
        out_specs=(across, across),
        check_vma=False,
    )
```

time: 338 us -> 270 us (0.80)
  the two profiles are of different devices: /device:TPU:31 before, /device:TPU:97 now
where the time goes in v3:
time: 270 us
  Pallas kernels  120 us (44%)
  starting transfers between devices  84.2 us (31%)
  waiting for transfers between devices  54.5 us (20%)
  other arithmetic  5.85 us (2%)
  local copies, waits for them, and re-layouts  3.37 us (1%)
    pallas_call x3, Pallas kernels, pair_call(): pl.pallas_call(functools.partial(pair_body, step), out_shape=out, in_spec...  90.8 us
    ppermute x13, starting transfers between devices, from_behind(): return lax.ppermute(block, axis, route)  65.7 us
    ppermute x13, waiting for transfers between devices, from_behind(): return lax.ppermute(block, axis, route)  54.5 us
    pallas_call x1, Pallas kernels, volume_call(): pl.pallas_call(volume_body, out_shape=jax.ShapeDtypeStruct((3, VB * TILE)...  29.1 us
    all_to_all x1, starting transfers between devices, body(): lax.all_to_all(sent, 'nodes', 0, 0, tiled=True)  18.5 us
  transfers between devices with their start and end apart: 14, of which 8 were waited for; matrix products, arithmetic and copies ran while one was open for 2% of the time, Pallas kernels for 0%

profile of v3, /device:TPU:97, one launch (start us, length us, event | category | flops | bytes accessed | tf_op | source)
XLA Modules:
  0.0 270.2 jit_solution(12320936543234221879)
XLA Ops:
  0.6 2.6 collective-permute-start.1
  3.7 2.5 subtract_multiply_fusion
  6.2 6.5 %collective-permute-start = (f32[3,32768]{1,0:T(4,128)S(1)}, f32[3,32768]{1,0:T(4,128)S(1)}, u32[]{:S(2)}, u32[]{:S(2)}) collective-permute-start(f32[3,32768]{1,0:T(4,128)S(1)} %get-tuple-element.26.own_geo.refs_2_), channel_id=1, source_target_pairs={{1,0},{2,1},{3,2},{4,3},{5,4},{6,5},{7,6},{8,7},{9,8},{10,9},{11,1... | collective-permute-start | bytes 1179656 | tf_op jit(solution)/shard_map/ppermute | solution.py:29
  13.6 3.4 %collective-permute-done.right_geo.refs_3_ = f32[3,32768]{1,0:T(4,128)S(1)} collective-permute-done((f32[3,32768]{1,0:T(4,128)S(1)}, f32[3,32768]{1,0:T(4,128)S(1)}, u32[]{:S(2)}, u32[]{:S(2)}) %collective-permute-start) | collective-permute-done | bytes 393248 | tf_op jit(solution)/shard_map/ppermute | solution.py:29
  17.2 29.7 %pair_tiles_0.1 = (f32[4,32768]{1,0:T(4,128)S(1)}, f32[4,32768]{1,0:T(4,128)S(1)}) custom-call(s32[1]{0:T(128)S(6)} %select_n.163.groups, s32[256]{0:T(256)S(1)} %fusion.44.diag_list, s32[768]{0:T(1024)S(1)} %fusion.16.pair_list, f32[3,32768]{1,0:T(4,128)S(1)} %get-tuple-element.26.own_geo.refs_2_, f32[3,32768]{1,0:T(4,128)S(1)} %collective-permute-done.right_geo.refs_3_, ...), custom_call_target="tpu_custom_call" | custom-call | tf_op jit(solution)/shard_map/pair_tiles_0/pallas_call | solution.py:256
  46.9 1.9 collective-permute-start.2
  48.9 12.7 %collective-permute-done.2 = f32[4,32768]{1,0:T(4,128)S(1)} collective-permute-done((f32[4,32768]{1,0:T(4,128)S(1)}, f32[4,32768]{1,0:T(4,128)S(1)}, u32[]{:S(2)}, u32[]{:S(2)}) %collective-permute-start.2) | collective-permute-done | bytes 524320 | tf_op jit(solution)/shard_map/ppermute | solution.py:29
  62.9 13.3 %collective-permute-start.3 = (f32[3,32768]{1,0:T(4,128)S(1)}, f32[3,32768]{1,0:T(4,128)S(1)}, u32[]{:S(2)}, u32[]{:S(2)}) collective-permute-start(f32[3,32768]{1,0:T(4,128)S(1)} %slice_add_fusion.1.own_vec), channel_id=1, source_target_pairs={{1,0},{2,1},{3,2},{4,3},{5,4},{6,5},{7,6},{8,7},{9,8},{10,9},{11,1... | collective-permute-start | bytes 1179656 | tf_op jit(solution)/shard_map/ppermute | solution.py:29
  77.8 29.7 %pair_tiles_1.1 = (f32[4,32768]{1,0:T(4,128)S(1)}, f32[4,32768]{1,0:T(4,128)S(1)}) custom-call(s32[1]{0:T(128)S(6)} %select_n.163.groups, s32[256]{0:T(256)S(1)} %fusion.44.diag_list, s32[768]{0:T(1024)S(1)} %fusion.16.pair_list, f32[3,32768]{1,0:T(4,128)S(1)} %get-tuple-element.26.own_geo.refs_2_, f32[3,32768]{1,0:T(4,128)S(1)} %collective-permute-done.right_geo.refs_3_, ...), custom_call_target="tpu_custom_call" | custom-call | tf_op jit(solution)/shard_map/pair_tiles_1/pallas_call | solution.py:256
  109.4 14.7 %collective-permute-done.4 = f32[4,32768]{1,0:T(4,128)S(1)} collective-permute-done((f32[4,32768]{1,0:T(4,128)S(1)}, f32[4,32768]{1,0:T(4,128)S(1)}, u32[]{:S(2)}, u32[]{:S(2)}) %collective-permute-start.4) | collective-permute-done | bytes 524320 | tf_op jit(solution)/shard_map/ppermute | solution.py:29
  125.2 13.3 %collective-permute-start.5 = (f32[3,32768]{1,0:T(4,128)S(1)}, f32[3,32768]{1,0:T(4,128)S(1)}, u32[]{:S(2)}, u32[]{:S(2)}) collective-permute-start(f32[3,32768]{1,0:T(4,128)S(1)} %get-tuple-element.24.own_vec), channel_id=1, source_target_pairs={{1,0},{2,1},{3,2},{4,3},{5,4},{6,5},{7,6},{8,7},{9,8},{10,9},{11,1... | collective-permute-start | bytes 1179656 | tf_op jit(solution)/shard_map/ppermute | solution.py:29
  140.0 31.4 %pair_tiles_2.1 = f32[8,128]{1,0:T(8,128)S(1)} custom-call(s32[1]{0:T(128)S(6)} %select_n.163.groups, s32[256]{0:T(256)S(1)} %fusion.44.diag_list, s32[768]{0:T(1024)S(1)} %fusion.16.pair_list, f32[3,32768]{1,0:T(4,128)S(1)} %get-tuple-element.26.own_geo.refs_2_, f32[3,32768]{1,0:T(4,128)S(1)} %collective-permute-done.right_geo.refs_3_, ...), custom_call_target="tpu_custom_call" | custom-call | tf_op jit(solution)/shard_map/pair_tiles_2/pallas_call | solution.py:256
  172.3 18.5 %all-to-all-start = ((f32[128,1,128]{2,1,0:T(1,128)}), f32[128,1,128]{2,1,0:T(1,128)S(1)}, u32[]{:S(2)}, u32[]{:S(2)}) async-start(f32[128,1,128]{2,1,0:T(1,128)} %broadcast_in_dim.33), calls=%async_computation | async-start | bytes 131072 | tf_op jit(solution)/shard_map/all_to_all | solution.py:419
  190.8 6.7 %collective-permute-start.8 = (f32[3,32768]{1,0:T(4,128)S(1)}, f32[3,32768]{1,0:T(4,128)}, u32[]{:S(2)}, u32[]{:S(2)}) collective-permute-start(f32[3,32768]{1,0:T(4,128)S(1)} %get-tuple-element.26.own_geo.refs_2_), channel_id=1, source_target_pairs={{2,0},{3,1},{4,2},{5,3},{6,4},{7,5},{8,6},{9,7},{10,8},{11,9},{12,... | collective-permute-start | bytes 1179656 | tf_op jit(solution)/shard_map/ppermute | solution.py:29
  197.5 1.9 collective-permute-start.7
  199.5 1.9 collective-permute-start.6
  202.0 8.1 %collective-permute-start.12 = (f32[3,32768]{1,0:T(4,128)S(1)}, f32[3,32768]{1,0:T(4,128)S(1)}, u32[]{:S(2)}, u32[]{:S(2)}) collective-permute-start(f32[3,32768]{1,0:T(4,128)S(1)} %multiply_add_fusion.refs_7_), channel_id=1, source_target_pairs={{2,0},{3,1},{4,2},{5,3},{6,4},{7,5},{8,6},{9,7},{10,8},{11,9},{12,... | collective-permute-start | bytes 1179656 | tf_op jit(solution)/shard_map/ppermute | solution.py:29
  210.1 2.6 collective-permute-start.11
  212.7 3.0 %collective-permute-start.10 = (f32[3,32768]{1,0:T(4,128)S(1)}, f32[3,32768]{1,0:T(4,128)S(1)}, u32[]{:S(2)}, u32[]{:S(2)}) collective-permute-start(f32[3,32768]{1,0:T(4,128)S(1)} %multiply_add_fusion.refs_7_), channel_id=1, source_target_pairs={{0,1},{1,2},{2,3},{3,4},{4,5},{5,6},{6,7},{7,8},{8,9},{9,10},{10,1... | collective-permute-start | bytes 1179656 | tf_op jit(solution)/shard_map/ppermute | solution.py:29
  215.7 1.9 collective-permute-start.9
  219.6 4.0 %collective-permute-done.6.refs_0_ = f32[3,32768]{1,0:T(4,128)} collective-permute-done((f32[3,32768]{1,0:T(4,128)S(1)}, f32[3,32768]{1,0:T(4,128)}, u32[]{:S(2)}, u32[]{:S(2)}) %collective-permute-start.6) | collective-permute-done | bytes 393248 | tf_op jit(solution)/shard_map/ppermute | solution.py:29
  223.6 2.5 collective-permute-done.10.refs_6_
  226.1 14.2 %collective-permute-done.9.refs_5_ = f32[3,32768]{1,0:T(4,128)S(1)} collective-permute-done((f32[3,32768]{1,0:T(4,128)S(1)}, f32[3,32768]{1,0:T(4,128)S(1)}, u32[]{:S(2)}, u32[]{:S(2)}) %collective-permute-start.9) | collective-permute-done | bytes 393248 | tf_op jit(solution)/shard_map/ppermute | solution.py:29
  241.1 29.1 %volume_tiles.1 = f32[3,32768]{1,0:T(4,128)} custom-call(s32[1]{0:T(128)S(6)} %select_n.177.groups, s32[512]{0:T(512)} %or_select_fusion.vol_list, f32[3,32768]{1,0:T(4,128)} %get-tuple-element.25.vol_geo, f32[3,32768]{1,0:T(4,128)} %collective-permute-done.6.refs_0_, f32[3,32768]{1,0:T(4,128)} %collective-permute-done.7.refs_1_, f32[3,32768]{1,0:T(4,128)} %copy-done, ...), custom_call_target="tpu_custom_call" | custom-call | tf_op jit(solution)/shard_map/volume_tiles/pallas_call | solution.py:315
  (62 shorter events, 11.7 us)
Async XLA Ops:
  0.6 13.0 %collective-permute-start.1 = (f32[3,32768]{1,0:T(4,128)}, f32[3,32768]{1,0:T(4,128)S(1)}, u32[]{:S(2)}, u32[]{:S(2)}) collective-permute-start(f32[3,32768]{1,0:T(4,128)} %own_vec.1), channel_id=1, source_target_pairs={{1,0},{2,1},{3,2},{4,3},{5,4},{6,5},{7,6},{8,7},{9,8},{10,9},{11,1... | collective-permute-start | bytes 1179656 | tf_op jit(solution)/shard_map/ppermute | solution.py:29
  3.6 9.9 %copy-start.10 = (s32[768]{0:T(1024)S(1)}, s32[768]{0:T(1024)}, u32[]{:S(2)}) copy-start(s32[768]{0:T(1024)} %param.13) | copy-start | bytes 9220
  3.6 9.9 %copy-start.11 = (s32[768]{0:T(1024)S(1)}, s32[768]{0:T(1024)}, u32[]{:S(2)}) copy-start(s32[768]{0:T(1024)} %param.14) | copy-start | bytes 9220
  6.2 193.3 %copy-start = (f32[3,32768]{1,0:T(4,128)}, f32[3,32768]{1,0:T(4,128)S(1)}, u32[]{:S(2)}) copy-start(f32[3,32768]{1,0:T(4,128)S(1)} %get-tuple-element.26.own_geo.refs_2_) | copy-start | bytes 1179652
  6.2 11.0 %copy-start.3 = (f32[3,32768]{1,0:T(4,128)S(1)}, f32[3,32768]{1,0:T(4,128)}, u32[]{:S(2)}) copy-start(f32[3,32768]{1,0:T(4,128)} %own_vec.1) | copy-start | bytes 1179652
  6.2 10.8 %collective-permute-start = (f32[3,32768]{1,0:T(4,128)S(1)}, f32[3,32768]{1,0:T(4,128)S(1)}, u32[]{:S(2)}, u32[]{:S(2)}) collective-permute-start(f32[3,32768]{1,0:T(4,128)S(1)} %get-tuple-element.26.own_geo.refs_2_), channel_id=1, source_target_pairs={{1,0},{2,1},{3,2},{4,3},{5,4},{6,5},{7,6},{8,7},{9,8},{10,9},{11,1... | collective-permute-start | bytes 1179656 | tf_op jit(solution)/shard_map/ppermute | solution.py:29
  17.0 123.0 %copy-start.2 = (f32[3,32768]{1,0:T(4,128)}, f32[3,32768]{1,0:T(4,128)S(1)}, u32[]{:S(2)}) copy-start(f32[3,32768]{1,0:T(4,128)S(1)} %collective-permute-done.right_geo.refs_3_) | copy-start | bytes 1179652
  17.2 122.8 %copy-start.1 = (f32[125,8,128]{2,1,0:T(8,128)}, f32[125,8,128]{2,1,0:T(8,128)S(1)}, u32[]{:S(2)}) copy-start(f32[125,8,128]{2,1,0:T(8,128)S(1)} %broadcast_in_dim.30.table_ref.refs_10_) | copy-start | bytes 1536004
  46.9 14.7 %collective-permute-start.2 = (f32[4,32768]{1,0:T(4,128)S(1)}, f32[4,32768]{1,0:T(4,128)S(1)}, u32[]{:S(2)}, u32[]{:S(2)}) collective-permute-start(f32[4,32768]{1,0:T(4,128)S(1)} %get-tuple-element.7), channel_id=1, source_target_pairs={{0,1},{1,2},{2,3},{3,4},{4,5},{5,6},{6,7},{7,8},{8,9},{9,10},{10,1... | collective-permute-start | bytes 1572872 | tf_op jit(solution)/shard_map/ppermute | solution.py:29
  62.9 14.8 %collective-permute-start.3 = (f32[3,32768]{1,0:T(4,128)S(1)}, f32[3,32768]{1,0:T(4,128)S(1)}, u32[]{:S(2)}, u32[]{:S(2)}) collective-permute-start(f32[3,32768]{1,0:T(4,128)S(1)} %slice_add_fusion.1.own_vec), channel_id=1, source_target_pairs={{1,0},{2,1},{3,2},{4,3},{5,4},{6,5},{7,6},{8,7},{9,8},{10,9},{11,1... | collective-permute-start | bytes 1179656 | tf_op jit(solution)/shard_map/ppermute | solution.py:29
  107.5 16.6 %collective-permute-start.4 = (f32[4,32768]{1,0:T(4,128)S(1)}, f32[4,32768]{1,0:T(4,128)S(1)}, u32[]{:S(2)}, u32[]{:S(2)}) collective-permute-start(f32[4,32768]{1,0:T(4,128)S(1)} %get-tuple-element.9), channel_id=1, source_target_pairs={{0,1},{1,2},{2,3},{3,4},{4,5},{5,6},{6,7},{7,8},{8,9},{9,10},{10,1... | collective-permute-start | bytes 1572872 | tf_op jit(solution)/shard_map/ppermute | solution.py:29
  125.2 14.8 %collective-permute-start.5 = (f32[3,32768]{1,0:T(4,128)S(1)}, f32[3,32768]{1,0:T(4,128)S(1)}, u32[]{:S(2)}, u32[]{:S(2)}) collective-permute-start(f32[3,32768]{1,0:T(4,128)S(1)} %get-tuple-element.24.own_vec), channel_id=1, source_target_pairs={{1,0},{2,1},{3,2},{4,3},{5,4},{6,5},{7,6},{8,7},{9,8},{10,9},{11,1... | collective-permute-start | bytes 1179656 | tf_op jit(solution)/shard_map/ppermute | solution.py:29
  172.3 29.1 %all-to-all-start = ((f32[128,1,128]{2,1,0:T(1,128)}), f32[128,1,128]{2,1,0:T(1,128)S(1)}, u32[]{:S(2)}, u32[]{:S(2)}) async-start(f32[128,1,128]{2,1,0:T(1,128)} %broadcast_in_dim.33), calls=%async_computation | async-start | bytes 131072 | tf_op jit(solution)/shard_map/all_to_all | solution.py:419
  190.8 21.8 %collective-permute-start.8 = (f32[3,32768]{1,0:T(4,128)S(1)}, f32[3,32768]{1,0:T(4,128)}, u32[]{:S(2)}, u32[]{:S(2)}) collective-permute-start(f32[3,32768]{1,0:T(4,128)S(1)} %get-tuple-element.26.own_geo.refs_2_), channel_id=1, source_target_pairs={{2,0},{3,1},{4,2},{5,3},{6,4},{7,5},{8,6},{9,7},{10,8},{11,9},{12,... | collective-permute-start | bytes 1179656 | tf_op jit(solution)/shard_map/ppermute | solution.py:29
  197.5 18.1 %collective-permute-start.7 = (f32[3,32768]{1,0:T(4,128)S(1)}, f32[3,32768]{1,0:T(4,128)}, u32[]{:S(2)}, u32[]{:S(2)}) collective-permute-start(f32[3,32768]{1,0:T(4,128)S(1)} %get-tuple-element.26.own_geo.refs_2_), channel_id=1, source_target_pairs={{0,1},{1,2},{2,3},{3,4},{4,5},{5,6},{6,7},{7,8},{8,9},{9,10},{10,1... | collective-permute-start | bytes 1179656 | tf_op jit(solution)/shard_map/ppermute | solution.py:29
  199.5 24.1 %collective-permute-start.6 = (f32[3,32768]{1,0:T(4,128)S(1)}, f32[3,32768]{1,0:T(4,128)}, u32[]{:S(2)}, u32[]{:S(2)}) collective-permute-start(f32[3,32768]{1,0:T(4,128)S(1)} %get-tuple-element.26.own_geo.refs_2_), channel_id=1, source_target_pairs={{0,2},{1,3},{2,4},{3,5},{4,6},{5,7},{6,8},{7,9},{8,10},{9,11},{10,... | collective-permute-start | bytes 1179656 | tf_op jit(solution)/shard_map/ppermute | solution.py:29
  201.9 38.4 %copy-start.4 = (f32[3,32768]{1,0:T(4,128)}, f32[3,32768]{1,0:T(4,128)S(1)}, u32[]{:S(2)}) copy-start(f32[3,32768]{1,0:T(4,128)S(1)} %multiply_add_fusion.refs_7_) | copy-start | bytes 1179652
  202.0 21.6 %collective-permute-start.12 = (f32[3,32768]{1,0:T(4,128)S(1)}, f32[3,32768]{1,0:T(4,128)S(1)}, u32[]{:S(2)}, u32[]{:S(2)}) collective-permute-start(f32[3,32768]{1,0:T(4,128)S(1)} %multiply_add_fusion.refs_7_), channel_id=1, source_target_pairs={{2,0},{3,1},{4,2},{5,3},{6,4},{7,5},{8,6},{9,7},{10,8},{11,9},{12,... | collective-permute-start | bytes 1179656 | tf_op jit(solution)/shard_map/ppermute | solution.py:29
  210.1 13.5 %collective-permute-start.11 = (f32[3,32768]{1,0:T(4,128)S(1)}, f32[3,32768]{1,0:T(4,128)S(1)}, u32[]{:S(2)}, u32[]{:S(2)}) collective-permute-start(f32[3,32768]{1,0:T(4,128)S(1)} %multiply_add_fusion.refs_7_), channel_id=1, source_target_pairs={{1,0},{2,1},{3,2},{4,3},{5,4},{6,5},{7,6},{8,7},{9,8},{10,9},{11,1... | collective-permute-start | bytes 1179656 | tf_op jit(solution)/shard_map/ppermute | solution.py:29
  212.7 13.5 %collective-permute-start.10 = (f32[3,32768]{1,0:T(4,128)S(1)}, f32[3,32768]{1,0:T(4,128)S(1)}, u32[]{:S(2)}, u32[]{:S(2)}) collective-permute-start(f32[3,32768]{1,0:T(4,128)S(1)} %multiply_add_fusion.refs_7_), channel_id=1, source_target_pairs={{0,1},{1,2},{2,3},{3,4},{4,5},{5,6},{6,7},{7,8},{8,9},{9,10},{10,1... | collective-permute-start | bytes 1179656 | tf_op jit(solution)/shard_map/ppermute | solution.py:29
  215.7 24.6 %collective-permute-start.9 = (f32[3,32768]{1,0:T(4,128)S(1)}, f32[3,32768]{1,0:T(4,128)S(1)}, u32[]{:S(2)}, u32[]{:S(2)}) collective-permute-start(f32[3,32768]{1,0:T(4,128)S(1)} %multiply_add_fusion.refs_7_), channel_id=1, source_target_pairs={{0,2},{1,3},{2,4},{3,5},{4,6},{5,7},{6,8},{7,9},{8,10},{9,11},{10,... | collective-permute-start | bytes 1179656 | tf_op jit(solution)/shard_map/ppermute | solution.py:29
  223.6 16.8 %copy-start.5 = (f32[3,32768]{1,0:T(4,128)}, f32[3,32768]{1,0:T(4,128)S(1)}, u32[]{:S(2)}) copy-start(f32[3,32768]{1,0:T(4,128)S(1)} %collective-permute-done.12.refs_9_) | copy-start | bytes 1179652
  223.6 16.7 %copy-start.6 = (f32[3,32768]{1,0:T(4,128)}, f32[3,32768]{1,0:T(4,128)S(1)}, u32[]{:S(2)}) copy-start(f32[3,32768]{1,0:T(4,128)S(1)} %collective-permute-done.11.refs_8_) | copy-start | bytes 1179652
  226.1 14.2 %copy-start.7 = (f32[3,32768]{1,0:T(4,128)}, f32[3,32768]{1,0:T(4,128)S(1)}, u32[]{:S(2)}) copy-start(f32[3,32768]{1,0:T(4,128)S(1)} %collective-permute-done.10.refs_6_) | copy-start | bytes 1179652
  (4 other events, 3.1 us)

commit v4 on v3

--- a/solution.py
+++ b/solution.py
@@ -15,6 +15,9 @@
 MAXV = 512
 GROUP = 16
 PART = 32
+RING = 8
+DIAG_GROUPS = CB // GROUP
+PAIR_GROUPS = MAXT // GROUP
 SHIFT = 0.75
 FAR = 64.0
 
@@ -129,7 +132,7 @@
             rows_ref[first + k + j] = turned if j == 0 else pltpu.roll(turned, TILE - j * PART, 1)
 
 
-def tile_loop(groups, listed, rows_ref, cols_ref, table_ref, dist_ref, tile_ref, use, ahead=None):
+def tile_loop(groups, listed, rows_ref, cols_ref, table_ref, dist_ref, tile_ref, use, ahead=None, keep=None):
     row = row_ids()
     squares = (row >= 3) & (row < 6)
     unit = row == 6
@@ -152,31 +155,96 @@
         gap_sq = gap * gap
         return gap_sq * gap_sq * (0.625 - gap)
 
+    if keep is not None:
+        stage_ref, sems, home = keep
+
+    def copy_out(group):
+        slot = lax.rem(group, RING)
+        return pltpu.make_async_copy(stage_ref.at[pl.ds(slot, 1)], home(group), sems.at[slot])
+
     def step(at, carry):
         used = jnp.maximum(at - 2, 0) * GROUP
         first = jnp.minimum(at, groups - 1) * GROUP
+        if keep is not None:
+            stage = lax.rem(at + RING - 1, RING)
+            before = at - 1 - RING
+
+            @pl.when(before >= 0)
+            def _():
+                copy_out(before).wait()
+
         found = []
         for k in range(0, GROUP, 2):
-            found += use(used, k)
+            found += use(used, k, (tile_ref[k], tile_ref[k + 1]))
             for j in (k, k + 1):
-                tile_ref[j] = phi(dist_ref[j]).astype(tile_ref.dtype)
+                tile = phi(dist_ref[j]).astype(tile_ref.dtype)
+                tile_ref[j] = tile
+                if keep is not None:
+                    stage_ref[stage, j] = tile
             for j in (k, k + 1):
                 dist_ref[j] = distances(first + j)
         for out, block, value in found:
             out[block] += value
         if ahead is not None:
             ahead(jnp.minimum(at + 1, groups - 1) * GROUP)
+        if keep is not None:
+
+            @pl.when((at > 0) & (at <= groups))
+            def _():
+                copy_out(at - 1).start()
+
         return carry
 
     lax.fori_loop(0, jnp.where(groups > 0, groups + 2, 0), step, 0)
-
-
-def pair_body(step, groups, diag_list, pair_list, own_geo, right_geo, own_vec, right_vec, table_ref, *refs):
-    outs, refs = refs[: 2 if step < 2 else 1], refs[2 if step < 2 else 1 :]
-    rows_ref, cols_ref, vec_ref, row_sum, col_sum, dist_ref, tile_ref = refs
+    if keep is not None:
+        for back in range(1, RING):
+            group = groups - back
+
+            @pl.when(group >= 0)
+            def _():
+                copy_out(group).wait()
+
+
+def stream_loop(pairs, home, stage_ref, sems, use):
+    ring = stage_ref.shape[0]
+
+    def copy_in(at):
+        slot = lax.rem(at, ring)
+        return pltpu.make_async_copy(home(2 * at, 2), stage_ref.at[slot], sems.at[slot])
+
+    for at in range(ring - 1):
+
+        @pl.when(at < pairs)
+        def _():
+            copy_in(at).start()
+
+    def step(at, carry):
+        @pl.when(at + ring - 1 < pairs)
+        def _():
+            copy_in(at + ring - 1).start()
+
+        copy_in(at).wait()
+        slot = lax.rem(at, ring)
+        found = []
+        for k in range(0, 2 * GROUP, 2):
+            tile = k % GROUP
+            found += use(2 * at * GROUP, k, (stage_ref[slot, k // GROUP, tile], stage_ref[slot, k // GROUP, tile + 1]))
+        for out, block, value in found:
+            out[block] += value
+        return carry
+
+    lax.fori_loop(0, pairs, step, 0)
+
+
+def pair_body(step, groups, diag_list, pair_list, own_vec, right_vec, *refs):
+    if step == 0:
+        own_geo, right_geo, table_ref, stiff_ref, own_out, right_out, tiles = refs[:7]
+        vec_ref, row_sum, col_sum, stage_ref, sems, rows_ref, cols_ref, dist_ref, tile_ref = refs[7:]
+        column_rows((own_geo, right_geo), cols_ref)
+    else:
+        tiles, *outs, vec_ref, row_sum, col_sum, stage_ref, sems = refs
     row = row_ids()
 
-    column_rows((own_geo, right_geo), cols_ref)
     vector_rows((own_vec, right_vec), vec_ref, 1.0)
     row_sum[...] = jnp.zeros_like(row_sum)
     col_sum[...] = jnp.zeros_like(col_sum)
@@ -184,57 +252,70 @@
     def two(first, second):
         return jnp.concatenate([first, second], axis=0).astype(bf16)
 
-    def use_diag(first, k):
+    def use_diag(first, k, pair):
         a, b = diag_list[first + k] & 255, diag_list[first + k + 1] & 255
         left = two(jnp.where(row == 3, 0.0, vec_ref[a]), jnp.where(row == 3, 0.0, vec_ref[b]))
         image = jnp.dot(
-            left, jnp.concatenate([tile_ref[k], tile_ref[k + 1]], axis=1), preferred_element_type=f32
+            left, jnp.concatenate(pair, axis=1), preferred_element_type=f32
         )
         return [(col_sum, a, image[:8, :TILE]), (col_sum, b, image[8:, TILE:])]
 
-    def use_pair(first, k):
+    def use_pair(first, k, pair):
         p, q = pair_list[first + k], pair_list[first + k + 1]
         row_a, col_a = p & 255, (p >> 8) & 2047
         row_b, col_b = q & 255, (q >> 8) & 2047
-        one, other = tile_ref[k], tile_ref[k + 1]
         left = two(vec_ref[row_a], vec_ref[row_b])
         if step == 2:
             left = left * 2
-        image = jnp.dot(left, jnp.concatenate([one, other], axis=1), preferred_element_type=f32)
+        image = jnp.dot(left, jnp.concatenate(pair, axis=1), preferred_element_type=f32)
         found = [(col_sum, col_a, image[:8, :TILE]), (col_sum, col_b, image[8:, TILE:])]
         if step < 2:
             image = lax.dot_general(
                 two(vec_ref[col_a], vec_ref[col_b]),
-                jnp.concatenate([one, other], axis=0),
+                jnp.concatenate(pair, axis=0),
                 (((1,), (1,)), ((), ())),
                 preferred_element_type=f32,
             )
             found += [(row_sum, row_a, image[:8, :TILE]), (row_sum, row_b, image[8:, TILE:])]
         return found
 
-    loop = functools.partial(
-        tile_loop, rows_ref=rows_ref, cols_ref=cols_ref, table_ref=table_ref, dist_ref=dist_ref, tile_ref=tile_ref
-    )
-    ahead = functools.partial(row_features, own_geo, rows_ref, count=GROUP)
-    ahead(0)
-    loop(jnp.int32(CB // GROUP), diag_list, use=use_diag, ahead=ahead)
-    loop(groups[0], pair_list, use=use_pair)
+    def diag_home(group, count=1):
+        return tiles.at[pl.ds(group, count)]
+
+    def pair_home(group, count=1):
+        return tiles.at[pl.ds(DIAG_GROUPS + group, count)]
+
+    if step == 0:
+        loop = functools.partial(
+            tile_loop, rows_ref=rows_ref, cols_ref=cols_ref, table_ref=table_ref, dist_ref=dist_ref, tile_ref=tile_ref
+        )
+        ahead = functools.partial(row_features, own_geo, rows_ref, count=GROUP)
+        ahead(0)
+        loop(jnp.int32(DIAG_GROUPS), diag_list, use=use_diag, ahead=ahead, keep=(stage_ref, sems, diag_home))
+        loop(groups[0], pair_list, use=use_pair, keep=(stage_ref, sems, pair_home))
+    else:
+        stream_loop(jnp.int32(DIAG_GROUPS // 2), diag_home, stage_ref, sems, use_diag)
+        stream_loop(lax.div(groups[0], 2), pair_home, stage_ref, sems, use_pair)
 
     def fold(value):
         return value + pltpu.roll(value, 4, 0)
 
     if step < 2:
-        own_out, right_out = outs
+        images = (own_out, right_out) if step == 0 else outs
 
         def finish(first):
             place = pl.ds(pl.multiple_of(first * TILE, 8 * TILE), 8 * TILE)
             own, right = row_sum[pl.ds(first, 8)] + col_sum[pl.ds(first, 8)], col_sum[pl.ds(CB + first, 8)]
-            own_out[:, place] = jnp.concatenate([fold(own[k])[:4] for k in range(8)], axis=1)
-            right_out[:, place] = jnp.concatenate([fold(right[k])[:4] for k in range(8)], axis=1)
+            own = jnp.concatenate([fold(own[k])[:4] for k in range(8)], axis=1)
+            if step == 0:
+                fourth = lax.broadcasted_iota(i32, own.shape, 0) == 3
+                own = own + jnp.where(fourth, stiff_ref[:, place] - SHIFT, 0.0)
+            images[0][:, place] = own
+            images[1][:, place] = jnp.concatenate([fold(right[k])[:4] for k in range(8)], axis=1)
 
         each_chunk(CB, finish)
     else:
-        (quad_out,) = outs
+        quad_out = outs[0]
 
         def finish(at, sums):
             return tuple(
@@ -246,28 +327,34 @@
         quad_out[...] = sum(sums)
 
 
-def pair_call(step, groups, diag_list, pair_list, *arrays):
+def pair_call(step, *arrays, groups, diag_list, pair_list):
     smem = pl.BlockSpec(memory_space=pltpu.SMEM)
     vmem = pl.BlockSpec(memory_space=pltpu.VMEM)
-    if step < 2:
-        out = (jax.ShapeDtypeStruct((4, CB * TILE), f32),) * 2
-    else:
-        out = (jax.ShapeDtypeStruct((8, TILE), f32),)
-    return pl.pallas_call(
-        functools.partial(pair_body, step),
-        out_shape=out,
-        in_specs=[smem] * 3 + [vmem] * len(arrays),
-        out_specs=(vmem,) * len(out),
-        scratch_shapes=[
+    some = pl.BlockSpec(memory_space=pl.ANY)
+    image = jax.ShapeDtypeStruct((4, CB * TILE), f32)
+    kept = jax.ShapeDtypeStruct((DIAG_GROUPS + PAIR_GROUPS, GROUP, TILE, TILE), bf16)
+    scratch = [
+        pltpu.VMEM((2 * CB + 1, 8, TILE), f32),
+        pltpu.VMEM((CB, 8, TILE), f32),
+        pltpu.VMEM((2 * CB + 1, 8, TILE), f32),
+        pltpu.VMEM((RING, GROUP, TILE, TILE) if step == 0 else (RING // 2, 2, GROUP, TILE, TILE), bf16),
+        pltpu.SemaphoreType.DMA((RING,)),
+    ]
+    if step == 0:
+        scratch += [
             pltpu.VMEM((CB, TILE, TILE), bf16),
-            pltpu.VMEM((2 * CB + 1, 8, TILE), f32),
-            pltpu.VMEM((2 * CB + 1, 8, TILE), f32),
-            pltpu.VMEM((CB, 8, TILE), f32),
             pltpu.VMEM((2 * CB + 1, 8, TILE), f32),
             pltpu.VMEM((GROUP, TILE, TILE), f32),
             pltpu.VMEM((GROUP, TILE, TILE), bf16),
-        ],
+        ]
+    return pl.pallas_call(
+        functools.partial(pair_body, step),
+        out_shape=((image, image, kept), (image, image), (jax.ShapeDtypeStruct((8, TILE), f32),))[step],
+        in_specs=[smem] * 3 + [vmem] * (len(arrays) - 1) + [vmem if step == 0 else some],
+        out_specs=((vmem, vmem, some), (vmem, vmem), (vmem,))[step],
+        scratch_shapes=scratch,
         compiler_params=pltpu.CompilerParams(vmem_limit_bytes=48 * 2**20),
+        cost_estimate=pl.CostEstimate(flops=2 * 10**9, bytes_accessed=10**8, transcendentals=0),
         name=f"pair_tiles_{step}",
     )(groups, diag_list, pair_list, *arrays)
 
@@ -285,13 +372,12 @@
 
     lax.fori_loop(0, VB // 16, features, 0)
 
-    def use(first, k):
+    def use(first, k, pair):
         dims = (((1,), (1,)), ((), ()))
         p, q = vol_list[first + k], vol_list[first + k + 1]
         left = jnp.concatenate([coef_ref[(p >> 8) & 2047], coef_ref[(q >> 8) & 2047]], axis=0).astype(bf16)
         highs, lows = [], []
-        for j in (k, k + 1):
-            tile = tile_ref[j]
+        for tile in pair:
             high = tile.astype(bf16)
             highs.append(high)
             lows.append((tile - high.astype(f32)).astype(bf16))
@@ -326,6 +412,7 @@
             pltpu.VMEM((GROUP, TILE, TILE), f32),
         ],
         compiler_params=pltpu.CompilerParams(vmem_limit_bytes=56 * 2**20),
+        cost_estimate=pl.CostEstimate(flops=2 * 10**9, bytes_accessed=10**8, transcendentals=0),
         name="volume_tiles",
     )(groups, vol_list, *arrays)
 
@@ -379,7 +466,7 @@
     live = (slots < pair_count[0]) & (~right | (me < devices - 1))
     code = offset_code(right.astype(i32), pair_rows, pair_cols % CB)
     pair_list = jnp.where(live, pair_rows | (pair_cols << 8) | (code << 19), (2 * CB) << 8)
-    pair_groups = (pair_count + GROUP - 1) // GROUP
+    pair_groups = (pair_count + 2 * GROUP - 1) // (2 * GROUP) * 2
     own = lax.iota(i32, CB)
     diag_list = own | (own << 8) | (62 << 19)
 
@@ -392,17 +479,25 @@
     vol_groups = (vol_count + GROUP - 1) // GROUP
     vol_geo = local_coords(vol_points, me)
 
-    def images(step, *vectors):
-        return pair_call(step, pair_groups, diag_list, pair_list, geo[0], geo[-1], *vectors, table)
-
-    own_part, right_part = images(0, ctrl_disp, beside)
-    total = own_part + from_behind(right_part, "nodes", 1)
-    diagonal = stiffness[None, :] + total[3:4] - SHIFT
+    images = functools.partial(pair_call, groups=pair_groups, diag_list=diag_list, pair_list=pair_list)
+
+    def exchanged(own_part, right_part):
+        back = from_behind(right_part, "nodes", 1)
+        ahead = from_behind(own_part, "nodes", -1)
+        return own_part + back, ahead + right_part
+
+    own_part, right_part, tiles = images(0, ctrl_disp, beside, geo[0], geo[-1], table, stiffness[None, :])
+    own_part, right_part, geo[1], geo[2], geo[-2] = lax.optimization_barrier(
+        (own_part, right_part, geo[1], geo[2], geo[-2])
+    )
+    total, total_beside = exchanged(own_part, right_part)
+    diagonal, diagonal_beside = total[3:4], total_beside[3:4]
     first = total[:3] + diagonal * ctrl_disp
-    own_part, right_part = images(1, first, from_behind(first, "nodes", -1))
-    total = own_part + from_behind(right_part, "nodes", 1)
+    first_beside = total_beside[:3] + diagonal_beside * beside
+    total, total_beside = exchanged(*images(1, first, first_beside, tiles))
     second = total[:3] + diagonal * first
-    (quad,) = images(2, second, from_behind(second, "nodes", -1))
+    second_beside = total_beside[:3] + diagonal_beside * first_beside
+    (quad,) = images(2, second, second_beside, tiles)
     moments = jnp.concatenate(
         [
             comp_sum(ctrl_disp, ctrl_disp),

time: 270 us -> 227 us (0.84)
  the two profiles are of different devices: /device:TPU:97 before, /device:TPU:33 now
where the time goes in v4:
time: 227 us; the launch traced here: 229 us
  Pallas kernels  108 us (48%)
  starting transfers between devices  51.5 us (23%)
  waiting for transfers between devices  35.2 us (16%)
  blocking collectives  20.6 us (9%)
  other arithmetic  6.88 us (3%)
  local copies, waits for them, and re-layouts  3.68 us (2%)
  between operations  2.35 us (1%)
    pallas_call x3, Pallas kernels, pair_call(): pl.pallas_call(functools.partial(pair_body, step), out_shape=((image, ima...  77 us
    ppermute x13, starting transfers between devices, from_behind(): return lax.ppermute(block, axis, route)  51.5 us
    ppermute x13, waiting for transfers between devices, from_behind(): return lax.ppermute(block, axis, route)  35.2 us
    pallas_call x1, Pallas kernels, volume_call(): pl.pallas_call(volume_body, out_shape=jax.ShapeDtypeStruct((3, VB * TILE)...  31.4 us
    all_to_all x1, blocking collectives, body(): lax.all_to_all(sent, 'nodes', 0, 0, tiled=True)  20.6 us
  transfers between devices with their start and end apart: 13, of which 7 were waited for; matrix products, arithmetic and copies ran while one was open for 1% of the time, Pallas kernels for 17%

profile of v4, /device:TPU:33, one launch (start us, length us, event | category | flops | bytes accessed | tf_op | source)
XLA Modules:
  0.0 228.6 jit_solution(7517203028311716536)
XLA Ops:
  1.1 2.5 %subtract_multiply_fusion = (f32[3,32768]{1,0:T(4,128)}, f32[3,32768]{1,0:T(4,128)S(1)}) fusion(f32[3,32768]{1,0:T(4,128)} %param.16, f32[1,32768]{1,0:T(1,128)S(1)} %get-tuple-element.41, f32[1,32768]{1,0:T(1,128)S(1)} %get-tuple-element.42, f32[3]{0:T(128)S(1)} %pad.clone, f32[3,32768]{1,0:T(4,128)} %param.10), kind=kLoop, calls=%fused_computation.9 | loop fusion | flops 589824 | bytes 1835020 | tf_op jit(solution)/shard_map/mul | solution.py:44
  3.6 2.6 %collective-permute-start.1 = (f32[3,32768]{1,0:T(4,128)S(1)}, f32[3,32768]{1,0:T(4,128)S(1)}, u32[]{:S(2)}, u32[]{:S(2)}) collective-permute-start(f32[3,32768]{1,0:T(4,128)S(1)} %get-tuple-element.38.refs_0_.refs_2_), channel_id=1, source_target_pairs={{1,0},{2,1},{3,2},{4,3},{5,4},{6,5},{7,6},{8,7},{9,8},{10,9},{11,1... | collective-permute-start | bytes 1179656 | tf_op jit(solution)/shard_map/ppermute | solution.py:32
  6.2 3.0 %collective-permute-start.2 = (f32[3,32768]{1,0:T(4,128)S(1)}, f32[3,32768]{1,0:T(4,128)}, u32[]{:S(2)}, u32[]{:S(2)}) collective-permute-start(f32[3,32768]{1,0:T(4,128)S(1)} %get-tuple-element.38.refs_0_.refs_2_), channel_id=1, source_target_pairs={{0,1},{1,2},{2,3},{3,4},{4,5},{5,6},{6,7},{7,8},{8,9},{9,10},{10,1... | collective-permute-start | bytes 1179656 | tf_op jit(solution)/shard_map/ppermute | solution.py:32
  9.2 3.1 %collective-permute-start.3 = (f32[3,32768]{1,0:T(4,128)S(1)}, f32[3,32768]{1,0:T(4,128)}, u32[]{:S(2)}, u32[]{:S(2)}) collective-permute-start(f32[3,32768]{1,0:T(4,128)S(1)} %get-tuple-element.38.refs_0_.refs_2_), channel_id=1, source_target_pairs={{0,2},{1,3},{2,4},{3,5},{4,6},{5,7},{6,8},{7,9},{8,10},{9,11},{10,... | collective-permute-start | bytes 1179656 | tf_op jit(solution)/shard_map/ppermute | solution.py:32
  12.3 9.4 %collective-permute-start.4 = (f32[3,32768]{1,0:T(4,128)S(1)}, f32[3,32768]{1,0:T(4,128)}, u32[]{:S(2)}, u32[]{:S(2)}) collective-permute-start(f32[3,32768]{1,0:T(4,128)S(1)} %get-tuple-element.38.refs_0_.refs_2_), channel_id=1, source_target_pairs={{2,0},{3,1},{4,2},{5,3},{6,4},{7,5},{8,6},{9,7},{10,8},{11,9},{12,... | collective-permute-start | bytes 1179656 | tf_op jit(solution)/shard_map/ppermute | solution.py:32
  21.7 2.6 %collective-permute-start = (f32[3,32768]{1,0:T(4,128)}, f32[3,32768]{1,0:T(4,128)S(1)}, u32[]{:S(2)}, u32[]{:S(2)}) collective-permute-start(f32[3,32768]{1,0:T(4,128)} %own_vec.1), channel_id=1, source_target_pairs={{1,0},{2,1},{3,2},{4,3},{5,4},{6,5},{7,6},{8,7},{9,8},{10,9},{11,1... | collective-permute-start | bytes 1179656 | tf_op jit(solution)/shard_map/ppermute | solution.py:32
  25.9 7.6 %collective-permute-done.right_vec = f32[3,32768]{1,0:T(4,128)S(1)} collective-permute-done((f32[3,32768]{1,0:T(4,128)}, f32[3,32768]{1,0:T(4,128)S(1)}, u32[]{:S(2)}, u32[]{:S(2)}) %collective-permute-start) | collective-permute-done | bytes 393248 | tf_op jit(solution)/shard_map/ppermute | solution.py:32
  35.8 38.8 %pair_tiles_0.1 = (f32[4,32768]{1,0:T(4,128)S(1)}, f32[4,32768]{1,0:T(4,128)S(1)}, bf16[64,16,128,128]{3,2,1,0:T(8,128)(2,1)}) custom-call(s32[1]{0:T(128)S(6)} %mul.399.groups, s32[256]{0:T(256)S(1)} %fusion.44.diag_list, s32[768]{0:T(1024)S(1)} %fusion.16.pair_list, f32[3,32768]{1,0:T(4,128)S(1)} %copy-done, ...), custom_call_target="tpu_custom_call" | custom-call | flops 2000000000 | bytes 100000000 | tf_op jit(solution)/shard_map/pair_tiles_0/pallas_call | solution.py:350
  74.7 4.1 %collective-permute-start.6 = (f32[4,32768]{1,0:T(4,128)S(1)}, f32[4,32768]{1,0:T(4,128)S(1)}, u32[]{:S(2)}, u32[]{:S(2)}) collective-permute-start(f32[4,32768]{1,0:T(4,128)S(1)} %get-tuple-element.14), channel_id=1, source_target_pairs={{1,0},{2,1},{3,2},{4,3},{5,4},{6,5},{7,6},{8,7},{9,8},{10,9},{11,1... | collective-permute-start | bytes 1572872 | tf_op jit(solution)/shard_map/ppermute | solution.py:32
  78.8 1.9 collective-permute-start.5
  80.7 4.4 %collective-permute-done.6 = f32[4,32768]{1,0:T(4,128)S(1)} collective-permute-done((f32[4,32768]{1,0:T(4,128)S(1)}, f32[4,32768]{1,0:T(4,128)S(1)}, u32[]{:S(2)}, u32[]{:S(2)}) %collective-permute-start.6) | collective-permute-done | bytes 524320 | tf_op jit(solution)/shard_map/ppermute | solution.py:32
  87.6 20.7 %pair_tiles_1.1 = (f32[4,32768]{1,0:T(4,128)S(1)}, f32[4,32768]{1,0:T(4,128)S(1)}) custom-call(s32[1]{0:T(128)S(6)} %mul.399.groups, s32[256]{0:T(256)S(1)} %fusion.44.diag_list, s32[768]{0:T(1024)S(1)} %fusion.16.pair_list, f32[3,32768]{1,0:T(4,128)S(1)} %slice_add_fusion.3.own_vec, f32[3,32768]{1,0:T(4,128)S(1)} %slice_add_fusion.2.right_vec, ...), custom_call_target="tpu_custom_call" | custom-call | flops 2000000000 | bytes 100000000 | tf_op jit(solution)/shard_map/pair_tiles_1/pallas_call | solution.py:350
  108.3 8.6 %collective-permute-start.8 = (f32[4,32768]{1,0:T(4,128)S(1)}, f32[4,32768]{1,0:T(4,128)S(1)}, u32[]{:S(2)}, u32[]{:S(2)}) collective-permute-start(f32[4,32768]{1,0:T(4,128)S(1)} %get-tuple-element.17), channel_id=1, source_target_pairs={{1,0},{2,1},{3,2},{4,3},{5,4},{6,5},{7,6},{8,7},{9,8},{10,9},{11,1... | collective-permute-start | bytes 1572872 | tf_op jit(solution)/shard_map/ppermute | solution.py:32
  116.9 1.9 collective-permute-start.7
  119.1 5.8 %collective-permute-done.7 = f32[4,32768]{1,0:T(4,128)S(1)} collective-permute-done((f32[4,32768]{1,0:T(4,128)S(1)}, f32[4,32768]{1,0:T(4,128)S(1)}, u32[]{:S(2)}, u32[]{:S(2)}) %collective-permute-start.7) | collective-permute-done | bytes 524320 | tf_op jit(solution)/shard_map/ppermute | solution.py:32
  125.9 17.5 %pair_tiles_2.1 = f32[8,128]{1,0:T(8,128)S(1)} custom-call(s32[1]{0:T(128)S(6)} %mul.399.groups, s32[256]{0:T(256)S(1)} %fusion.44.diag_list, s32[768]{0:T(1024)S(1)} %fusion.16.pair_list, f32[3,32768]{1,0:T(4,128)S(1)} %get-tuple-element.36.own_vec, f32[3,32768]{1,0:T(4,128)S(1)} %fusion.1.right_vec, bf16[64,16,128,128]{3,2,1,0:T(8,128)(2,1)} %get-tuple-element.16.refs_0_), custom_call_target="tpu_custom_call" | custom-call | flops 2000000000 | bytes 100000000 | tf_op jit(solution)/shard_map/pair_tiles_2/pallas_call | solution.py:350
  143.7 20.6 %all_to_all.5 = f32[128,1,128]{2,1,0:T(1,128)S(1)} all-to-all(f32[128,1,128]{2,1,0:T(1,128)S(1)} %broadcast_in_dim.33), channel_id=1, replica_groups=mesh['nodes'=128] {'nodes'}, dimensions={0} | all-to-all | bytes 131072 | tf_op jit(solution)/shard_map/all_to_all | solution.py:514
  164.8 2.7 %collective-permute-start.10 = (f32[3,32768]{1,0:T(4,128)S(1)}, f32[3,32768]{1,0:T(4,128)S(1)}, u32[]{:S(2)}, u32[]{:S(2)}) collective-permute-start(f32[3,32768]{1,0:T(4,128)S(1)} %multiply_add_fusion.refs_7_), channel_id=1, source_target_pairs={{0,1},{1,2},{2,3},{3,4},{4,5},{5,6},{6,7},{7,8},{8,9},{9,10},{10,1... | collective-permute-start | bytes 1179656 | tf_op jit(solution)/shard_map/ppermute | solution.py:32
  167.5 2.2 collective-permute-start.11
  169.7 7.5 %collective-permute-start.12 = (f32[3,32768]{1,0:T(4,128)S(1)}, f32[3,32768]{1,0:T(4,128)S(1)}, u32[]{:S(2)}, u32[]{:S(2)}) collective-permute-start(f32[3,32768]{1,0:T(4,128)S(1)} %multiply_add_fusion.refs_7_), channel_id=1, source_target_pairs={{2,0},{3,1},{4,2},{5,3},{6,4},{7,5},{8,6},{9,7},{10,8},{11,9},{12,... | collective-permute-start | bytes 1179656 | tf_op jit(solution)/shard_map/ppermute | solution.py:32
  177.2 1.9 collective-permute-start.9
  182.0 7.0 %collective-permute-done.12.refs_9_ = f32[3,32768]{1,0:T(4,128)S(1)} collective-permute-done((f32[3,32768]{1,0:T(4,128)S(1)}, f32[3,32768]{1,0:T(4,128)S(1)}, u32[]{:S(2)}, u32[]{:S(2)}) %collective-permute-start.12) | collective-permute-done | bytes 393248 | tf_op jit(solution)/shard_map/ppermute | solution.py:32
  189.0 7.5 %collective-permute-done.9.refs_5_ = f32[3,32768]{1,0:T(4,128)S(1)} collective-permute-done((f32[3,32768]{1,0:T(4,128)S(1)}, f32[3,32768]{1,0:T(4,128)S(1)}, u32[]{:S(2)}, u32[]{:S(2)}) %collective-permute-start.9) | collective-permute-done | bytes 393248 | tf_op jit(solution)/shard_map/ppermute | solution.py:32
  197.2 31.4 %volume_tiles.1 = f32[3,32768]{1,0:T(4,128)} custom-call(s32[1]{0:T(128)S(6)} %select_n.177.groups, s32[512]{0:T(512)} %or_select_fusion.vol_list, f32[3,32768]{1,0:T(4,128)} %get-tuple-element.37.vol_geo, f32[3,32768]{1,0:T(4,128)} %collective-permute-done.3.refs_0_, f32[3,32768]{1,0:T(4,128)} %collective-permute-done.2.refs_1_, f32[3,32768]{1,0:T(4,128)} %copy-done.2, ...), custom_call_target="tpu_custom_call" | custom-call | flops 2000000000 | bytes 100000000 | tf_op jit(solution)/shard_map/volume_tiles/pallas_call | solution.py:401
  (63 shorter events, 11.0 us)
Async XLA Ops:
  0.6 124.3 %copy-start.1 = (f32[3,32768]{1,0:T(4,128)S(1)}, f32[3,32768]{1,0:T(4,128)}, u32[]{:S(2)}) copy-start(f32[3,32768]{1,0:T(4,128)} %own_vec.1) | copy-start | bytes 1179652
  3.6 139.8 %copy-start.2 = (f32[3,32768]{1,0:T(4,128)}, f32[3,32768]{1,0:T(4,128)S(1)}, u32[]{:S(2)}) copy-start(f32[3,32768]{1,0:T(4,128)S(1)} %get-tuple-element.38.refs_0_.refs_2_) | copy-start | bytes 1179652
  3.6 22.3 %collective-permute-start.1 = (f32[3,32768]{1,0:T(4,128)S(1)}, f32[3,32768]{1,0:T(4,128)S(1)}, u32[]{:S(2)}, u32[]{:S(2)}) collective-permute-start(f32[3,32768]{1,0:T(4,128)S(1)} %get-tuple-element.38.refs_0_.refs_2_), channel_id=1, source_target_pairs={{1,0},{2,1},{3,2},{4,3},{5,4},{6,5},{7,6},{8,7},{9,8},{10,9},{11,1... | collective-permute-start | bytes 1179656 | tf_op jit(solution)/shard_map/ppermute | solution.py:32
  6.2 68.5 %collective-permute-start.2 = (f32[3,32768]{1,0:T(4,128)S(1)}, f32[3,32768]{1,0:T(4,128)}, u32[]{:S(2)}, u32[]{:S(2)}) collective-permute-start(f32[3,32768]{1,0:T(4,128)S(1)} %get-tuple-element.38.refs_0_.refs_2_), channel_id=1, source_target_pairs={{0,1},{1,2},{2,3},{3,4},{4,5},{5,6},{6,7},{7,8},{8,9},{9,10},{10,1... | collective-permute-start | bytes 1179656 | tf_op jit(solution)/shard_map/ppermute | solution.py:32
  9.2 65.5 %collective-permute-start.3 = (f32[3,32768]{1,0:T(4,128)S(1)}, f32[3,32768]{1,0:T(4,128)}, u32[]{:S(2)}, u32[]{:S(2)}) collective-permute-start(f32[3,32768]{1,0:T(4,128)S(1)} %get-tuple-element.38.refs_0_.refs_2_), channel_id=1, source_target_pairs={{0,2},{1,3},{2,4},{3,5},{4,6},{5,7},{6,8},{7,9},{8,10},{9,11},{10,... | collective-permute-start | bytes 1179656 | tf_op jit(solution)/shard_map/ppermute | solution.py:32
  12.3 62.4 %collective-permute-start.4 = (f32[3,32768]{1,0:T(4,128)S(1)}, f32[3,32768]{1,0:T(4,128)}, u32[]{:S(2)}, u32[]{:S(2)}) collective-permute-start(f32[3,32768]{1,0:T(4,128)S(1)} %get-tuple-element.38.refs_0_.refs_2_), channel_id=1, source_target_pairs={{2,0},{3,1},{4,2},{5,3},{6,4},{7,5},{8,6},{9,7},{10,8},{11,9},{12,... | collective-permute-start | bytes 1179656 | tf_op jit(solution)/shard_map/ppermute | solution.py:32
  21.7 11.8 %collective-permute-start = (f32[3,32768]{1,0:T(4,128)}, f32[3,32768]{1,0:T(4,128)S(1)}, u32[]{:S(2)}, u32[]{:S(2)}) collective-permute-start(f32[3,32768]{1,0:T(4,128)} %own_vec.1), channel_id=1, source_target_pairs={{1,0},{2,1},{3,2},{4,3},{5,4},{6,5},{7,6},{8,7},{9,8},{10,9},{11,1... | collective-permute-start | bytes 1179656 | tf_op jit(solution)/shard_map/ppermute | solution.py:32
  25.9 117.5 %copy-start.4 = (f32[3,32768]{1,0:T(4,128)}, f32[3,32768]{1,0:T(4,128)S(1)}, u32[]{:S(2)}) copy-start(f32[3,32768]{1,0:T(4,128)S(1)} %collective-permute-done.1.refs_1_.refs_3_) | copy-start | bytes 1179652
  33.7 109.8 %copy-start.3 = (f32[125,8,128]{2,1,0:T(8,128)}, f32[125,8,128]{2,1,0:T(8,128)S(1)}, u32[]{:S(2)}) copy-start(f32[125,8,128]{2,1,0:T(8,128)S(1)} %broadcast_in_dim.30.refs_2_.refs_10_) | copy-start | bytes 1536004
  33.7 1.2 copy-start
  74.7 10.5 %collective-permute-start.6 = (f32[4,32768]{1,0:T(4,128)S(1)}, f32[4,32768]{1,0:T(4,128)S(1)}, u32[]{:S(2)}, u32[]{:S(2)}) collective-permute-start(f32[4,32768]{1,0:T(4,128)S(1)} %get-tuple-element.14), channel_id=1, source_target_pairs={{1,0},{2,1},{3,2},{4,3},{5,4},{6,5},{7,6},{8,7},{9,8},{10,9},{11,1... | collective-permute-start | bytes 1572872 | tf_op jit(solution)/shard_map/ppermute | solution.py:32
  78.8 8.0 %collective-permute-start.5 = (f32[4,32768]{1,0:T(4,128)S(1)}, f32[4,32768]{1,0:T(4,128)S(1)}, u32[]{:S(2)}, u32[]{:S(2)}) collective-permute-start(f32[4,32768]{1,0:T(4,128)S(1)} %get-tuple-element.15), channel_id=1, source_target_pairs={{0,1},{1,2},{2,3},{3,4},{4,5},{5,6},{6,7},{7,8},{8,9},{9,10},{10,1... | collective-permute-start | bytes 1572872 | tf_op jit(solution)/shard_map/ppermute | solution.py:32
  87.5 92.2 %copy-start.7 = (s32[512]{0:T(512)S(1)}, s32[512]{0:T(512)}, u32[]{:S(2)}) copy-start(s32[512]{0:T(512)} %param.17) | copy-start | bytes 6148
  87.6 92.2 %copy-start.8 = (s32[512]{0:T(512)S(1)}, s32[512]{0:T(512)}, u32[]{:S(2)}) copy-start(s32[512]{0:T(512)} %param.18) | copy-start | bytes 6148
  108.3 10.5 %collective-permute-start.8 = (f32[4,32768]{1,0:T(4,128)S(1)}, f32[4,32768]{1,0:T(4,128)S(1)}, u32[]{:S(2)}, u32[]{:S(2)}) collective-permute-start(f32[4,32768]{1,0:T(4,128)S(1)} %get-tuple-element.17), channel_id=1, source_target_pairs={{1,0},{2,1},{3,2},{4,3},{5,4},{6,5},{7,6},{8,7},{9,8},{10,9},{11,1... | collective-permute-start | bytes 1572872 | tf_op jit(solution)/shard_map/ppermute | solution.py:32
  116.9 8.0 %collective-permute-start.7 = (f32[4,32768]{1,0:T(4,128)S(1)}, f32[4,32768]{1,0:T(4,128)S(1)}, u32[]{:S(2)}, u32[]{:S(2)}) collective-permute-start(f32[4,32768]{1,0:T(4,128)S(1)} %get-tuple-element.18), channel_id=1, source_target_pairs={{0,1},{1,2},{2,3},{3,4},{4,5},{5,6},{6,7},{7,8},{8,9},{9,10},{10,1... | collective-permute-start | bytes 1572872 | tf_op jit(solution)/shard_map/ppermute | solution.py:32
  164.8 31.6 %copy-start.6 = (f32[3,32768]{1,0:T(4,128)}, f32[3,32768]{1,0:T(4,128)S(1)}, u32[]{:S(2)}) copy-start(f32[3,32768]{1,0:T(4,128)S(1)} %multiply_add_fusion.refs_7_) | copy-start | bytes 1179652
  164.8 15.6 %collective-permute-start.10 = (f32[3,32768]{1,0:T(4,128)S(1)}, f32[3,32768]{1,0:T(4,128)S(1)}, u32[]{:S(2)}, u32[]{:S(2)}) collective-permute-start(f32[3,32768]{1,0:T(4,128)S(1)} %multiply_add_fusion.refs_7_), channel_id=1, source_target_pairs={{0,1},{1,2},{2,3},{3,4},{4,5},{5,6},{6,7},{7,8},{8,9},{9,10},{10,1... | collective-permute-start | bytes 1179656 | tf_op jit(solution)/shard_map/ppermute | solution.py:32
  167.5 14.5 %collective-permute-start.11 = (f32[3,32768]{1,0:T(4,128)S(1)}, f32[3,32768]{1,0:T(4,128)S(1)}, u32[]{:S(2)}, u32[]{:S(2)}) collective-permute-start(f32[3,32768]{1,0:T(4,128)S(1)} %multiply_add_fusion.refs_7_), channel_id=1, source_target_pairs={{1,0},{2,1},{3,2},{4,3},{5,4},{6,5},{7,6},{8,7},{9,8},{10,9},{11,1... | collective-permute-start | bytes 1179656 | tf_op jit(solution)/shard_map/ppermute | solution.py:32
  169.7 19.3 %collective-permute-start.12 = (f32[3,32768]{1,0:T(4,128)S(1)}, f32[3,32768]{1,0:T(4,128)S(1)}, u32[]{:S(2)}, u32[]{:S(2)}) collective-permute-start(f32[3,32768]{1,0:T(4,128)S(1)} %multiply_add_fusion.refs_7_), channel_id=1, source_target_pairs={{2,0},{3,1},{4,2},{5,3},{6,4},{7,5},{8,6},{9,7},{10,8},{11,9},{12,... | collective-permute-start | bytes 1179656 | tf_op jit(solution)/shard_map/ppermute | solution.py:32
  177.2 19.2 %collective-permute-start.9 = (f32[3,32768]{1,0:T(4,128)S(1)}, f32[3,32768]{1,0:T(4,128)S(1)}, u32[]{:S(2)}, u32[]{:S(2)}) collective-permute-start(f32[3,32768]{1,0:T(4,128)S(1)} %multiply_add_fusion.refs_7_), channel_id=1, source_target_pairs={{0,2},{1,3},{2,4},{3,5},{4,6},{5,7},{6,8},{7,9},{8,10},{9,11},{10,... | collective-permute-start | bytes 1179656 | tf_op jit(solution)/shard_map/ppermute | solution.py:32
  180.4 16.0 %copy-start.9 = (f32[3,32768]{1,0:T(4,128)}, f32[3,32768]{1,0:T(4,128)S(1)}, u32[]{:S(2)}) copy-start(f32[3,32768]{1,0:T(4,128)S(1)} %collective-permute-done.10.refs_6_) | copy-start | bytes 1179652
  182.0 14.4 %copy-start.10 = (f32[3,32768]{1,0:T(4,128)}, f32[3,32768]{1,0:T(4,128)S(1)}, u32[]{:S(2)}) copy-start(f32[3,32768]{1,0:T(4,128)S(1)} %collective-permute-done.11.refs_8_) | copy-start | bytes 1179652
  189.0 7.5 %copy-start.11 = (f32[3,32768]{1,0:T(4,128)}, f32[3,32768]{1,0:T(4,128)S(1)}, u32[]{:S(2)}) copy-start(f32[3,32768]{1,0:T(4,128)S(1)} %collective-permute-done.12.refs_9_) | copy-start | bytes 1179652
  (2 other events, 1.7 us)

commit v5 on v4

--- a/solution.py
+++ b/solution.py
@@ -32,16 +32,17 @@
     return lax.ppermute(block, axis, route)
 
 
-def local_coords(points, device):
-    block = lax.iota(i32, points.shape[1]) // TILE
-    centre = jnp.stack(
-        [
-            jnp.full(block.shape, 0.5, f32) + device.astype(f32),
-            2.0 * (block // SIDE).astype(f32) + 1.0,
-            2.0 * (block % SIDE).astype(f32) + 1.0,
-        ]
-    )
-    return (points - centre) * 0.25
+def around(block, axis):
+    devices = range(lax.axis_size(axis))
+
+    def send(value, target):
+        return lax.ppermute(value, axis, [(i, target(i)) for i in devices if target(i) in devices])
+
+    far = send(block, lambda i: i - 2 if i % 2 else i + 2)
+    near = send(block, lambda i: i + 1 if i % 2 else i - 1)
+    partner = send(block, lambda i: i ^ 1)
+    shared = send(near, lambda i: i ^ 1)
+    return [far, near, block, partner, shared]
 
 
 def offset_table():
@@ -75,6 +76,16 @@
     return [jnp.concatenate([value[:, k * TILE : (k + 1) * TILE], rest], axis=0) for k in range(count)]
 
 
+def local_coords(blocks, first, device):
+    row = row_ids()
+    along_x = jnp.where(row == 0, 1.0, 0.0) * (device.astype(f32) + 0.5)
+    along_y = jnp.where(row == 1, 2.0, 0.0) * ((first >> 4).astype(f32) + 0.5)
+    along_z = jnp.where(row == 2, 2.0, 0.0)
+    fixed = along_x + along_y
+    cell = (first & 15).astype(f32) + 0.5
+    return [(block - (fixed + along_z * (cell + k))) * 0.25 for k, block in enumerate(blocks)]
+
+
 def each_chunk(count, todo):
     def step(at, carry):
         todo(8 * at)
@@ -83,19 +94,20 @@
     lax.fori_loop(0, count // 8, step, 0)
 
 
-def column_rows(geo_refs, cols_ref):
+def column_rows(geo_refs, devices, cols_ref):
     unit = jnp.where(row_ids() == 6, 1.0, 0.0)
     for at, ref in enumerate(geo_refs):
 
         def fill(first):
-            rows = [block + pltpu.roll(block, 3, 0) + unit for block in three_rows(ref, first, 8)]
+            local = local_coords(three_rows(ref, first, 8), first, devices[at])
+            rows = [block + pltpu.roll(block, 3, 0) + unit for block in local]
             cols_ref[pl.ds(at * CB + first, 8)] = jnp.stack(rows)
 
         each_chunk(CB, fill)
     cols_ref[len(geo_refs) * CB] = jnp.full((8, TILE), FAR, f32)
 
 
-def vector_rows(refs, vec_ref, unit):
+def vector_rows(refs, vec_ref, unit, places=None):
     unit = jnp.where(row_ids() == 3, unit, 0.0)
     for at, ref in enumerate(refs):
 
@@ -104,13 +116,13 @@
             for block in three_rows(ref, first, 8):
                 high, low = split(block)
                 rows.append(high + pltpu.roll(low, 4, 0) + unit)
-            vec_ref[pl.ds(at * CB + first, 8)] = jnp.stack(rows)
+            vec_ref[pl.ds((at if places is None else places[at]) * CB + first, 8)] = jnp.stack(rows)
 
         each_chunk(CB, fill)
     vec_ref[len(refs) * CB] = jnp.zeros((8, TILE), f32)
 
 
-def row_features(geo_ref, rows_ref, first, count):
+def row_features(geo_ref, device, rows_ref, first, count):
     row = row_ids()
     middle = (row >= 3) & (row < 6)
 
@@ -122,7 +134,7 @@
         last = jnp.where(row < 3, mid, jnp.where(middle, 1.0, low))
         return [high, high, mid, last]
 
-    blocks = three_rows(geo_ref, first, count)
+    blocks = local_coords(three_rows(geo_ref, first, count), first, device)
     for k in range(0, count, 4):
         parts = []
         for j in range(4):
@@ -236,11 +248,11 @@
     lax.fori_loop(0, pairs, step, 0)
 
 
-def pair_body(step, groups, diag_list, pair_list, own_vec, right_vec, *refs):
+def pair_body(step, me, groups, diag_list, pair_list, own_vec, right_vec, *refs):
     if step == 0:
         own_geo, right_geo, table_ref, stiff_ref, own_out, right_out, tiles = refs[:7]
         vec_ref, row_sum, col_sum, stage_ref, sems, rows_ref, cols_ref, dist_ref, tile_ref = refs[7:]
-        column_rows((own_geo, right_geo), cols_ref)
+        column_rows((own_geo, right_geo), (me[0], me[0] + 1), cols_ref)
     else:
         tiles, *outs, vec_ref, row_sum, col_sum, stage_ref, sems = refs
     row = row_ids()
@@ -289,8 +301,8 @@
         loop = functools.partial(
             tile_loop, rows_ref=rows_ref, cols_ref=cols_ref, table_ref=table_ref, dist_ref=dist_ref, tile_ref=tile_ref
         )
-        ahead = functools.partial(row_features, own_geo, rows_ref, count=GROUP)
-        ahead(0)
+        ahead = functools.partial(row_features, own_geo, me[0], rows_ref, count=GROUP)
+        ahead(jnp.int32(0))
         loop(jnp.int32(DIAG_GROUPS), diag_list, use=use_diag, ahead=ahead, keep=(stage_ref, sems, diag_home))
         loop(groups[0], pair_list, use=use_pair, keep=(stage_ref, sems, pair_home))
     else:
@@ -327,7 +339,7 @@
         quad_out[...] = sum(sums)
 
 
-def pair_call(step, *arrays, groups, diag_list, pair_list):
+def pair_call(step, *arrays, me, groups, diag_list, pair_list):
     smem = pl.BlockSpec(memory_space=pltpu.SMEM)
     vmem = pl.BlockSpec(memory_space=pltpu.VMEM)
     some = pl.BlockSpec(memory_space=pl.ANY)
@@ -350,24 +362,25 @@
     return pl.pallas_call(
         functools.partial(pair_body, step),
         out_shape=((image, image, kept), (image, image), (jax.ShapeDtypeStruct((8, TILE), f32),))[step],
-        in_specs=[smem] * 3 + [vmem] * (len(arrays) - 1) + [vmem if step == 0 else some],
+        in_specs=[smem] * 4 + [vmem] * (len(arrays) - 1) + [vmem if step == 0 else some],
         out_specs=((vmem, vmem, some), (vmem, vmem), (vmem,))[step],
         scratch_shapes=scratch,
         compiler_params=pltpu.CompilerParams(vmem_limit_bytes=48 * 2**20),
         cost_estimate=pl.CostEstimate(flops=2 * 10**9, bytes_accessed=10**8, transcendentals=0),
         name=f"pair_tiles_{step}",
-    )(groups, diag_list, pair_list, *arrays)
-
-
-def volume_body(groups, vol_list, vol_geo, *refs):
+    )(me, groups, diag_list, pair_list, *arrays)
+
+
+def volume_body(me, groups, vol_list, vol_geo, *refs):
     geos, coefs = refs[:5], refs[5:10]
     table_ref, out, rows_ref, cols_ref, coef_ref, sums, dist_ref, tile_ref = refs[10:]
-    column_rows(geos, cols_ref)
-    vector_rows(coefs, coef_ref, 0.0)
+    column_rows(geos, [me[0] + k for k in range(-2, 3)], cols_ref)
+    odd = lax.rem(me[0], 2)
+    vector_rows(coefs, coef_ref, 0.0, [jnp.where(odd == 1, 4 - k, k) for k in range(5)])
     sums[...] = jnp.zeros_like(sums)
 
     def features(at, carry):
-        row_features(vol_geo, rows_ref, at * 16, 16)
+        row_features(vol_geo, me[0], rows_ref, at * 16, 16)
         return carry
 
     lax.fori_loop(0, VB // 16, features, 0)
@@ -395,13 +408,13 @@
     each_chunk(VB, finish)
 
 
-def volume_call(groups, vol_list, *arrays):
+def volume_call(me, groups, vol_list, *arrays):
     smem = pl.BlockSpec(memory_space=pltpu.SMEM)
     vmem = pl.BlockSpec(memory_space=pltpu.VMEM)
     return pl.pallas_call(
         volume_body,
         out_shape=jax.ShapeDtypeStruct((3, VB * TILE), f32),
-        in_specs=[smem] * 2 + [vmem] * len(arrays),
+        in_specs=[smem] * 3 + [vmem] * len(arrays),
         out_specs=vmem,
         scratch_shapes=[
             pltpu.VMEM((VB, TILE, TILE), bf16),
@@ -414,7 +427,7 @@
         compiler_params=pltpu.CompilerParams(vmem_limit_bytes=56 * 2**20),
         cost_estimate=pl.CostEstimate(flops=2 * 10**9, bytes_accessed=10**8, transcendentals=0),
         name="volume_tiles",
-    )(groups, vol_list, *arrays)
+    )(me, groups, vol_list, *arrays)
 
 
 def cg_weights(moment):
@@ -454,11 +467,11 @@
     devices = lax.axis_size("nodes")
     order = (2, 1, 0, -1, -2)
 
-    geo = {0: local_coords(ctrl_points, me)}
-    geo[-1] = from_behind(geo[0], "nodes", -1)
+    geo = {0: ctrl_points, -1: from_behind(ctrl_points, "nodes", -1)}
     beside = from_behind(ctrl_disp, "nodes", -1)
+    later, beside = lax.optimization_barrier((ctrl_points, beside))
     for offset in (1, 2, -2):
-        geo[offset] = from_behind(geo[0], "nodes", offset)
+        geo[offset] = from_behind(later, "nodes", offset)
     table = offset_table()
 
     slots = lax.iota(i32, MAXT)
@@ -477,9 +490,9 @@
     code = offset_code(step_x, vol_rows, vol_cols % CB)
     vol_list = jnp.where(live, vol_rows | (vol_cols << 8) | (code << 19), (5 * CB) << 8)
     vol_groups = (vol_count + GROUP - 1) // GROUP
-    vol_geo = local_coords(vol_points, me)
-
-    images = functools.partial(pair_call, groups=pair_groups, diag_list=diag_list, pair_list=pair_list)
+    here = me.astype(i32)[None]
+
+    images = functools.partial(pair_call, me=here, groups=pair_groups, diag_list=diag_list, pair_list=pair_list)
 
     def exchanged(own_part, right_part):
         back = from_behind(right_part, "nodes", 1)
@@ -514,8 +527,8 @@
     moments = jnp.sum(lax.all_to_all(sent, "nodes", 0, 0, tiled=True), axis=(0, 1))
     weights = cg_weights([moments[3 * k : 3 * k + 3] for k in range(6)])
     coef = sum(w[:, None] * u for w, u in zip(weights, (ctrl_disp, first, second)))
-    near = [coef if k == 0 else from_behind(coef, "nodes", k) for k in order]
-    moved = volume_call(vol_groups, vol_list, vol_geo, *[geo[k] for k in order], *near, table)
+    near = around(coef, "nodes")
+    moved = volume_call(here, vol_groups, vol_list, vol_points, *[geo[k] for k in order], *near, table)
     return (coef, moved)
 
 

time: 227 us -> 208 us (0.916)
  the two profiles are of different devices: /device:TPU:33 before, /device:TPU:64 now
where the time goes in v5:
time: 208 us
  Pallas kernels  93.3 us (45%)
  starting transfers between devices  44.2 us (21%)
  waiting for transfers between devices  41.1 us (20%)
  blocking collectives  16.7 us (8%)
  local copies, waits for them, and re-layouts  6.4 us (3%)
  other arithmetic  4.02 us (2%)
  between operations  2.37 us (1%)
    pallas_call x3, Pallas kernels, pair_call(): pl.pallas_call(functools.partial(pair_body, step), out_shape=((image, ima...  62 us
    ppermute x9, starting transfers between devices, from_behind(): return lax.ppermute(block, axis, route)  38.6 us
    pallas_call x1, Pallas kernels, volume_call(): pl.pallas_call(volume_body, out_shape=jax.ShapeDtypeStruct((3, VB * TILE)...  31.2 us
    ppermute x9, waiting for transfers between devices, from_behind(): return lax.ppermute(block, axis, route)  27.7 us
    all_to_all x1, blocking collectives, body(): lax.all_to_all(sent, 'nodes', 0, 0, tiled=True)  16.7 us
    ppermute x4, waiting for transfers between devices, send(): lax.ppermute(value, axis, [(i, target(i)) for i in devices if target(i) i...  13.4 us
    unnamed x32, local copies, waits for them, and re-layouts  5.66 us
    ppermute x4, starting transfers between devices, send(): lax.ppermute(value, axis, [(i, target(i)) for i in devices if target(i) i...  5.64 us
  transfers between devices with their start and end apart: 13, of which 7 were waited for; matrix products, arithmetic and copies ran while one was open for 1% of the time, Pallas kernels for 15%

profile of v5, /device:TPU:64, one launch (start us, length us, event | category | flops | bytes accessed | tf_op | source)
XLA Modules:
  0.0 208.0 jit_solution(1763759923238484350)
XLA Ops:
  0.6 6.1 %collective-permute-start = (f32[3,32768]{1,0:T(4,128)}, f32[3,32768]{1,0:T(4,128)S(1)}, u32[]{:S(2)}, u32[]{:S(2)}) collective-permute-start(f32[3,32768]{1,0:T(4,128)} %own_vec.1), channel_id=1, source_target_pairs={{1,0},{2,1},{3,2},{4,3},{5,4},{6,5},{7,6},{8,7},{9,8},{10,9},{11,1... | collective-permute-start | bytes 1179656 | tf_op jit(solution)/shard_map/ppermute | solution.py:32
  6.7 2.6 %collective-permute-start.1 = (f32[3,32768]{1,0:T(4,128)}, f32[3,32768]{1,0:T(4,128)S(1)}, u32[]{:S(2)}, u32[]{:S(2)}) collective-permute-start(f32[3,32768]{1,0:T(4,128)} %refs_2_.1), channel_id=1, source_target_pairs={{1,0},{2,1},{3,2},{4,3},{5,4},{6,5},{7,6},{8,7},{9,8},{10,9},{11,1... | collective-permute-start | bytes 1179656 | tf_op jit(solution)/shard_map/ppermute | solution.py:32
  10.2 3.5 %collective-permute-done.right_vec = f32[3,32768]{1,0:T(4,128)S(1)} collective-permute-done((f32[3,32768]{1,0:T(4,128)}, f32[3,32768]{1,0:T(4,128)S(1)}, u32[]{:S(2)}, u32[]{:S(2)}) %collective-permute-start) | collective-permute-done | bytes 393248 | tf_op jit(solution)/shard_map/ppermute | solution.py:32
  13.7 1.9 collective-permute-start.2
  15.7 1.9 collective-permute-start.3
  17.6 8.3 %collective-permute-start.4 = (f32[3,32768]{1,0:T(4,128)}, f32[3,32768]{1,0:T(4,128)S(1)}, u32[]{:S(2)}, u32[]{:S(2)}) collective-permute-start(f32[3,32768]{1,0:T(4,128)} %refs_2_.1), channel_id=1, source_target_pairs={{2,0},{3,1},{4,2},{5,3},{6,4},{7,5},{8,6},{9,7},{10,8},{11,9},{12,... | collective-permute-start | bytes 1179656 | tf_op jit(solution)/shard_map/ppermute | solution.py:32
  26.9 1.2 copy-done
  30.0 31.8 %pair_tiles_0.1 = (f32[4,32768]{1,0:T(4,128)S(1)}, f32[4,32768]{1,0:T(4,128)S(1)}, bf16[64,16,128,128]{3,2,1,0:T(8,128)(2,1)}) custom-call(s32[1]{0:T(128)} %bitcast.me, s32[1]{0:T(128)S(6)} %mul.371.groups, s32[256]{0:T(256)S(1)} %fusion.41.diag_list, s32[768]{0:T(1024)S(1)} %fusion.13.pair_list, f32[3,32768]{1,0:T(4,128)S(1)} %copy-done, ...), custom_call_target="tpu_custom_call" | custom-call | flops 2000000000 | bytes 100000000 | tf_op jit(solution)/shard_map/pair_tiles_0/pallas_call | solution.py:362
  62.7 8.7 %collective-permute-start.6 = (f32[4,32768]{1,0:T(4,128)S(1)}, f32[4,32768]{1,0:T(4,128)S(1)}, u32[]{:S(2)}, u32[]{:S(2)}) collective-permute-start(f32[4,32768]{1,0:T(4,128)S(1)} %get-tuple-element.18), channel_id=1, source_target_pairs={{1,0},{2,1},{3,2},{4,3},{5,4},{6,5},{7,6},{8,7},{9,8},{10,9},{11,1... | collective-permute-start | bytes 1572872 | tf_op jit(solution)/shard_map/ppermute | solution.py:32
  71.5 2.6 %collective-permute-start.5 = (f32[4,32768]{1,0:T(4,128)S(1)}, f32[4,32768]{1,0:T(4,128)S(1)}, u32[]{:S(2)}, u32[]{:S(2)}) collective-permute-start(f32[4,32768]{1,0:T(4,128)S(1)} %get-tuple-element.19), channel_id=1, source_target_pairs={{0,1},{1,2},{2,3},{3,4},{4,5},{5,6},{6,7},{7,8},{8,9},{9,10},{10,1... | collective-permute-start | bytes 1572872 | tf_op jit(solution)/shard_map/ppermute | solution.py:32
  74.0 4.1 %collective-permute-done.6 = f32[4,32768]{1,0:T(4,128)S(1)} collective-permute-done((f32[4,32768]{1,0:T(4,128)S(1)}, f32[4,32768]{1,0:T(4,128)S(1)}, u32[]{:S(2)}, u32[]{:S(2)}) %collective-permute-start.6) | collective-permute-done | bytes 524320 | tf_op jit(solution)/shard_map/ppermute | solution.py:32
  78.6 7.6 %collective-permute-done.5 = f32[4,32768]{1,0:T(4,128)S(1)} collective-permute-done((f32[4,32768]{1,0:T(4,128)S(1)}, f32[4,32768]{1,0:T(4,128)S(1)}, u32[]{:S(2)}, u32[]{:S(2)}) %collective-permute-start.5) | collective-permute-done | bytes 524320 | tf_op jit(solution)/shard_map/ppermute | solution.py:32
  86.7 16.2 %pair_tiles_1.1 = (f32[4,32768]{1,0:T(4,128)S(1)}, f32[4,32768]{1,0:T(4,128)S(1)}) custom-call(s32[1]{0:T(128)} %bitcast.me, s32[1]{0:T(128)S(6)} %mul.371.groups, s32[256]{0:T(256)S(1)} %fusion.41.diag_list, s32[768]{0:T(1024)S(1)} %fusion.13.pair_list, f32[3,32768]{1,0:T(4,128)S(1)} %slice_add_fusion.3.own_vec, f32[3,32768]{1,0:T(4,128)S(1)} %slice_add_fusion.2.right_vec, ...), custom_call_target="tpu_custom_call" | custom-call | flops 2000000000 | bytes 100000000 | tf_op jit(solution)/shard_map/pair_tiles_1/pallas_call | solution.py:362
  103.0 4.5 %collective-permute-start.8 = (f32[4,32768]{1,0:T(4,128)S(1)}, f32[4,32768]{1,0:T(4,128)S(1)}, u32[]{:S(2)}, u32[]{:S(2)}) collective-permute-start(f32[4,32768]{1,0:T(4,128)S(1)} %get-tuple-element.21), channel_id=1, source_target_pairs={{1,0},{2,1},{3,2},{4,3},{5,4},{6,5},{7,6},{8,7},{9,8},{10,9},{11,1... | collective-permute-start | bytes 1572872 | tf_op jit(solution)/shard_map/ppermute | solution.py:32
  107.5 1.9 collective-permute-start.7
  109.4 4.7 %collective-permute-done.8 = f32[4,32768]{1,0:T(4,128)S(1)} collective-permute-done((f32[4,32768]{1,0:T(4,128)S(1)}, f32[4,32768]{1,0:T(4,128)S(1)}, u32[]{:S(2)}, u32[]{:S(2)}) %collective-permute-start.8) | collective-permute-done | bytes 524320 | tf_op jit(solution)/shard_map/ppermute | solution.py:32
  114.4 7.8 %collective-permute-done.7 = f32[4,32768]{1,0:T(4,128)S(1)} collective-permute-done((f32[4,32768]{1,0:T(4,128)S(1)}, f32[4,32768]{1,0:T(4,128)S(1)}, u32[]{:S(2)}, u32[]{:S(2)}) %collective-permute-start.7) | collective-permute-done | bytes 524320 | tf_op jit(solution)/shard_map/ppermute | solution.py:32
  123.3 14.0 %pair_tiles_2.1 = f32[8,128]{1,0:T(8,128)S(1)} custom-call(s32[1]{0:T(128)} %bitcast.me, s32[1]{0:T(128)S(6)} %mul.371.groups, s32[256]{0:T(256)S(1)} %fusion.41.diag_list, s32[768]{0:T(1024)S(1)} %fusion.13.pair_list, f32[3,32768]{1,0:T(4,128)S(1)} %get-tuple-element.40.own_vec, f32[3,32768]{1,0:T(4,128)S(1)} %fusion.1.right_vec, ...), custom_call_target="tpu_custom_call" | custom-call | flops 2000000000 | bytes 100000000 | tf_op jit(solution)/shard_map/pair_tiles_2/pallas_call | solution.py:362
  137.6 16.7 %all_to_all.5 = f32[128,1,128]{2,1,0:T(1,128)S(1)} all-to-all(f32[128,1,128]{2,1,0:T(1,128)S(1)} %broadcast_in_dim.37), channel_id=1, replica_groups=mesh['nodes'=128] {'nodes'}, dimensions={0} | all-to-all | bytes 131072 | tf_op jit(solution)/shard_map/all_to_all | solution.py:527
  154.8 3.6 %collective-permute-start.10 = (f32[3,32768]{1,0:T(4,128)S(1)}, f32[3,32768]{1,0:T(4,128)S(1)}, u32[]{:S(2)}, u32[]{:S(2)}) collective-permute-start(f32[3,32768]{1,0:T(4,128)S(1)} %multiply_add_fusion.refs_7_), channel_id=1, source_target_pairs={{1,2},{2,1},{3,4},{4,3},{5,6},{6,5},{7,8},{8,7},{9,10},{10,9},{11,... | collective-permute-start | bytes 1179656 | tf_op jit(solution)/shard_map/ppermute | solution.py:39
  158.5 1.9 collective-permute-start.9
  160.5 10.3 %collective-permute-done.10.refs_6_ = f32[3,32768]{1,0:T(4,128)S(1)} collective-permute-done((f32[3,32768]{1,0:T(4,128)S(1)}, f32[3,32768]{1,0:T(4,128)S(1)}, u32[]{:S(2)}, u32[]{:S(2)}) %collective-permute-start.10) | collective-permute-done | bytes 393248 | tf_op jit(solution)/shard_map/ppermute | solution.py:39
  172.1 3.0 %collective-permute-done.9.refs_5_ = f32[3,32768]{1,0:T(4,128)S(1)} collective-permute-done((f32[3,32768]{1,0:T(4,128)S(1)}, f32[3,32768]{1,0:T(4,128)S(1)}, u32[]{:S(2)}, u32[]{:S(2)}) %collective-permute-start.9) | collective-permute-done | bytes 393248 | tf_op jit(solution)/shard_map/ppermute | solution.py:39
  176.8 31.2 %volume_tiles.1 = f32[3,32768]{1,0:T(4,128)} custom-call(s32[1]{0:T(128)} %bitcast.me, s32[1]{0:T(128)S(6)} %select_n.129.groups, s32[512]{0:T(512)} %or_select_fusion.vol_list, f32[3,32768]{1,0:T(4,128)} %vol_geo.1, f32[3,32768]{1,0:T(4,128)} %copy-done.10, f32[3,32768]{1,0:T(4,128)} %copy-done.9, f32[3,32768]{1,0:T(4,128)} %refs_2_.1, ...), custom_call_target="tpu_custom_call" | custom-call | flops 2000000000 | bytes 100000000 | tf_op jit(solution)/shard_map/volume_tiles/pallas_call | solution.py:414
  (66 shorter events, 9.3 us)
Async XLA Ops:
  0.6 13.1 %collective-permute-start = (f32[3,32768]{1,0:T(4,128)}, f32[3,32768]{1,0:T(4,128)S(1)}, u32[]{:S(2)}, u32[]{:S(2)}) collective-permute-start(f32[3,32768]{1,0:T(4,128)} %own_vec.1), channel_id=1, source_target_pairs={{1,0},{2,1},{3,2},{4,3},{5,4},{6,5},{7,6},{8,7},{9,8},{10,9},{11,1... | collective-permute-start | bytes 1179656 | tf_op jit(solution)/shard_map/ppermute | solution.py:32
  6.7 19.9 %collective-permute-start.1 = (f32[3,32768]{1,0:T(4,128)}, f32[3,32768]{1,0:T(4,128)S(1)}, u32[]{:S(2)}, u32[]{:S(2)}) collective-permute-start(f32[3,32768]{1,0:T(4,128)} %refs_2_.1), channel_id=1, source_target_pairs={{1,0},{2,1},{3,2},{4,3},{5,4},{6,5},{7,6},{8,7},{9,8},{10,9},{11,1... | collective-permute-start | bytes 1179656 | tf_op jit(solution)/shard_map/ppermute | solution.py:32
  13.7 48.1 %collective-permute-start.2 = (f32[3,32768]{1,0:T(4,128)}, f32[3,32768]{1,0:T(4,128)S(1)}, u32[]{:S(2)}, u32[]{:S(2)}) collective-permute-start(f32[3,32768]{1,0:T(4,128)} %refs_2_.1), channel_id=1, source_target_pairs={{0,1},{1,2},{2,3},{3,4},{4,5},{5,6},{6,7},{7,8},{8,9},{9,10},{10,1... | collective-permute-start | bytes 1179656 | tf_op jit(solution)/shard_map/ppermute | solution.py:32
  15.7 46.2 %collective-permute-start.3 = (f32[3,32768]{1,0:T(4,128)}, f32[3,32768]{1,0:T(4,128)S(1)}, u32[]{:S(2)}, u32[]{:S(2)}) collective-permute-start(f32[3,32768]{1,0:T(4,128)} %refs_2_.1), channel_id=1, source_target_pairs={{0,2},{1,3},{2,4},{3,5},{4,6},{5,7},{6,8},{7,9},{8,10},{9,11},{10,... | collective-permute-start | bytes 1179656 | tf_op jit(solution)/shard_map/ppermute | solution.py:32
  17.6 44.3 %collective-permute-start.4 = (f32[3,32768]{1,0:T(4,128)}, f32[3,32768]{1,0:T(4,128)S(1)}, u32[]{:S(2)}, u32[]{:S(2)}) collective-permute-start(f32[3,32768]{1,0:T(4,128)} %refs_2_.1), channel_id=1, source_target_pairs={{2,0},{3,1},{4,2},{5,3},{6,4},{7,5},{8,6},{9,7},{10,8},{11,9},{12,... | collective-permute-start | bytes 1179656 | tf_op jit(solution)/shard_map/ppermute | solution.py:32
  26.6 110.7 %copy-start.4 = (f32[3,32768]{1,0:T(4,128)}, f32[3,32768]{1,0:T(4,128)S(1)}, u32[]{:S(2)}) copy-start(f32[3,32768]{1,0:T(4,128)S(1)} %collective-permute-done.1.refs_1_.refs_3_) | copy-start | bytes 1179652
  26.9 110.5 %copy-start.2 = (f32[125,8,128]{2,1,0:T(8,128)}, f32[125,8,128]{2,1,0:T(8,128)S(1)}, u32[]{:S(2)}) copy-start(f32[125,8,128]{2,1,0:T(8,128)S(1)} %broadcast_in_dim.34.refs_2_.refs_10_) | copy-start | bytes 1536004
  26.9 1.2 copy-start
  61.8 75.5 %copy-start.9 = (f32[3,32768]{1,0:T(4,128)}, f32[3,32768]{1,0:T(4,128)S(1)}, u32[]{:S(2)}) copy-start(f32[3,32768]{1,0:T(4,128)S(1)} %collective-permute-done.2.refs_1_) | copy-start | bytes 1179652
  61.8 24.8 %copy-start.10 = (f32[3,32768]{1,0:T(4,128)}, f32[3,32768]{1,0:T(4,128)S(1)}, u32[]{:S(2)}) copy-start(f32[3,32768]{1,0:T(4,128)S(1)} %collective-permute-done.3.refs_0_) | copy-start | bytes 1179652
  62.7 15.4 %collective-permute-start.6 = (f32[4,32768]{1,0:T(4,128)S(1)}, f32[4,32768]{1,0:T(4,128)S(1)}, u32[]{:S(2)}, u32[]{:S(2)}) collective-permute-start(f32[4,32768]{1,0:T(4,128)S(1)} %get-tuple-element.18), channel_id=1, source_target_pairs={{1,0},{2,1},{3,2},{4,3},{5,4},{6,5},{7,6},{8,7},{9,8},{10,9},{11,1... | collective-permute-start | bytes 1572872 | tf_op jit(solution)/shard_map/ppermute | solution.py:32
  71.5 14.7 %collective-permute-start.5 = (f32[4,32768]{1,0:T(4,128)S(1)}, f32[4,32768]{1,0:T(4,128)S(1)}, u32[]{:S(2)}, u32[]{:S(2)}) collective-permute-start(f32[4,32768]{1,0:T(4,128)S(1)} %get-tuple-element.19), channel_id=1, source_target_pairs={{0,1},{1,2},{2,3},{3,4},{4,5},{5,6},{6,7},{7,8},{8,9},{9,10},{10,1... | collective-permute-start | bytes 1572872 | tf_op jit(solution)/shard_map/ppermute | solution.py:32
  86.7 67.8 %copy-start.1 = (f32[3,32768]{1,0:T(4,128)S(1)}, f32[3,32768]{1,0:T(4,128)}, u32[]{:S(2)}) copy-start(f32[3,32768]{1,0:T(4,128)} %own_vec.1) | copy-start | bytes 1179652
  86.7 84.8 %copy-start.7 = (s32[512]{0:T(512)S(1)}, s32[512]{0:T(512)}, u32[]{:S(2)}) copy-start(s32[512]{0:T(512)} %param.17) | copy-start | bytes 6148
  86.7 84.8 %copy-start.8 = (s32[512]{0:T(512)S(1)}, s32[512]{0:T(512)}, u32[]{:S(2)}) copy-start(s32[512]{0:T(512)} %param.18) | copy-start | bytes 6148
  103.0 11.2 %collective-permute-start.8 = (f32[4,32768]{1,0:T(4,128)S(1)}, f32[4,32768]{1,0:T(4,128)S(1)}, u32[]{:S(2)}, u32[]{:S(2)}) collective-permute-start(f32[4,32768]{1,0:T(4,128)S(1)} %get-tuple-element.21), channel_id=1, source_target_pairs={{1,0},{2,1},{3,2},{4,3},{5,4},{6,5},{7,6},{8,7},{9,8},{10,9},{11,1... | collective-permute-start | bytes 1572872 | tf_op jit(solution)/shard_map/ppermute | solution.py:32
  107.5 14.7 %collective-permute-start.7 = (f32[4,32768]{1,0:T(4,128)S(1)}, f32[4,32768]{1,0:T(4,128)S(1)}, u32[]{:S(2)}, u32[]{:S(2)}) collective-permute-start(f32[4,32768]{1,0:T(4,128)S(1)} %get-tuple-element.22), channel_id=1, source_target_pairs={{0,1},{1,2},{2,3},{3,4},{4,5},{5,6},{6,7},{7,8},{8,9},{9,10},{10,1... | collective-permute-start | bytes 1572872 | tf_op jit(solution)/shard_map/ppermute | solution.py:32
  154.8 20.4 %copy-start.6 = (f32[3,32768]{1,0:T(4,128)}, f32[3,32768]{1,0:T(4,128)S(1)}, u32[]{:S(2)}) copy-start(f32[3,32768]{1,0:T(4,128)S(1)} %multiply_add_fusion.refs_7_) | copy-start | bytes 1179652
  154.8 16.0 %collective-permute-start.10 = (f32[3,32768]{1,0:T(4,128)S(1)}, f32[3,32768]{1,0:T(4,128)S(1)}, u32[]{:S(2)}, u32[]{:S(2)}) collective-permute-start(f32[3,32768]{1,0:T(4,128)S(1)} %multiply_add_fusion.refs_7_), channel_id=1, source_target_pairs={{1,2},{2,1},{3,4},{4,3},{5,6},{6,5},{7,8},{8,7},{9,10},{10,9},{11,... | collective-permute-start | bytes 1179656 | tf_op jit(solution)/shard_map/ppermute | solution.py:39
  158.4 13.6 %collective-permute-start.11 = (f32[3,32768]{1,0:T(4,128)S(1)}, f32[3,32768]{1,0:T(4,128)S(1)}, u32[]{:S(2)}, u32[]{:S(2)}) collective-permute-start(f32[3,32768]{1,0:T(4,128)S(1)} %multiply_add_fusion.refs_7_), channel_id=1, source_target_pairs={{0,1},{1,0},{2,3},{3,2},{4,5},{5,4},{6,7},{7,6},{8,9},{9,8},{10,11... | collective-permute-start | bytes 1179656 | tf_op jit(solution)/shard_map/ppermute | solution.py:39
  158.5 16.6 %collective-permute-start.9 = (f32[3,32768]{1,0:T(4,128)S(1)}, f32[3,32768]{1,0:T(4,128)S(1)}, u32[]{:S(2)}, u32[]{:S(2)}) collective-permute-start(f32[3,32768]{1,0:T(4,128)S(1)} %multiply_add_fusion.refs_7_), channel_id=1, source_target_pairs={{0,2},{2,4},{3,1},{4,6},{5,3},{6,8},{7,5},{8,10},{9,7},{10,12},{11... | collective-permute-start | bytes 1179656 | tf_op jit(solution)/shard_map/ppermute | solution.py:39
  170.8 4.4 %copy-start.12 = (f32[3,32768]{1,0:T(4,128)}, f32[3,32768]{1,0:T(4,128)S(1)}, u32[]{:S(2)}) copy-start(f32[3,32768]{1,0:T(4,128)S(1)} %collective-permute-done.10.refs_6_) | copy-start | bytes 1179652
  170.8 4.4 %collective-permute-start.12 = (f32[3,32768]{1,0:T(4,128)S(1)}, f32[3,32768]{1,0:T(4,128)S(1)}, u32[]{:S(2)}, u32[]{:S(2)}) collective-permute-start(f32[3,32768]{1,0:T(4,128)S(1)} %collective-permute-done.10.refs_6_), channel_id=1, source_target_pairs={{0,1},{1,0},{2,3},{3,2},{4,5},{5,4},{6,7},{7,6},{8,9},{9,8},{10,11... | collective-permute-start | bytes 1179656 | tf_op jit(solution)/shard_map/ppermute | solution.py:39
  172.1 3.1 %copy-start.13 = (f32[3,32768]{1,0:T(4,128)}, f32[3,32768]{1,0:T(4,128)S(1)}, u32[]{:S(2)}) copy-start(f32[3,32768]{1,0:T(4,128)S(1)} %collective-permute-done.11.refs_8_) | copy-start | bytes 1179652
  (5 other events, 4.4 us)

commit v6 on v5

--- a/solution.py
+++ b/solution.py
@@ -248,16 +248,22 @@
     lax.fori_loop(0, pairs, step, 0)
 
 
-def pair_body(step, me, groups, diag_list, pair_list, own_vec, right_vec, *refs):
-    if step == 0:
-        own_geo, right_geo, table_ref, stiff_ref, own_out, right_out, tiles = refs[:7]
-        vec_ref, row_sum, col_sum, stage_ref, sems, rows_ref, cols_ref, dist_ref, tile_ref = refs[7:]
+def pair_body(step, me, groups, diag_list, pair_list, *refs):
+    row = row_ids()
+    own = functools.partial(row_features, device=me[0], count=GROUP)
+    if step == "diag":
+        own_vec, own_geo, table_ref, stiff_ref, own_out, diag_tiles = refs[:6]
+        vec_ref, row_sum, col_sum, stage_ref, sems, rows_ref, cols_ref, dist_ref, tile_ref = refs[6:]
+        column_rows((own_geo,), (me[0],), cols_ref)
+        vector_rows((own_vec,), vec_ref, 1.0)
+    elif step == "pairs":
+        own_vec, right_vec, own_geo, right_geo, table_ref, diag_ref, own_out, right_out, pair_tiles = refs[:9]
+        vec_ref, row_sum, col_sum, stage_ref, sems, rows_ref, cols_ref, dist_ref, tile_ref = refs[9:]
         column_rows((own_geo, right_geo), (me[0], me[0] + 1), cols_ref)
+        vector_rows((own_vec, right_vec), vec_ref, 1.0)
     else:
-        tiles, *outs, vec_ref, row_sum, col_sum, stage_ref, sems = refs
-    row = row_ids()
-
-    vector_rows((own_vec, right_vec), vec_ref, 1.0)
+        own_vec, right_vec, diag_tiles, pair_tiles, *outs, vec_ref, row_sum, col_sum, stage_ref, sems = refs
+        vector_rows((own_vec, right_vec), vec_ref, 1.0)
     row_sum[...] = jnp.zeros_like(row_sum)
     col_sum[...] = jnp.zeros_like(col_sum)
 
@@ -281,7 +287,7 @@
             left = left * 2
         image = jnp.dot(left, jnp.concatenate(pair, axis=1), preferred_element_type=f32)
         found = [(col_sum, col_a, image[:8, :TILE]), (col_sum, col_b, image[8:, TILE:])]
-        if step < 2:
+        if step != 2:
             image = lax.dot_general(
                 two(vec_ref[col_a], vec_ref[col_b]),
                 jnp.concatenate(pair, axis=0),
@@ -292,19 +298,32 @@
         return found
 
     def diag_home(group, count=1):
-        return tiles.at[pl.ds(group, count)]
+        return diag_tiles.at[pl.ds(group, count)]
 
     def pair_home(group, count=1):
-        return tiles.at[pl.ds(DIAG_GROUPS + group, count)]
-
-    if step == 0:
+        return pair_tiles.at[pl.ds(group, count)]
+
+    if step in ("diag", "pairs"):
         loop = functools.partial(
             tile_loop, rows_ref=rows_ref, cols_ref=cols_ref, table_ref=table_ref, dist_ref=dist_ref, tile_ref=tile_ref
         )
-        ahead = functools.partial(row_features, own_geo, me[0], rows_ref, count=GROUP)
-        ahead(jnp.int32(0))
-        loop(jnp.int32(DIAG_GROUPS), diag_list, use=use_diag, ahead=ahead, keep=(stage_ref, sems, diag_home))
-        loop(groups[0], pair_list, use=use_pair, keep=(stage_ref, sems, pair_home))
+
+        def features(at, carry):
+            own(own_geo, rows_ref=rows_ref, first=at * GROUP)
+            return carry
+
+        if step == "diag":
+            features(jnp.int32(0), 0)
+            loop(
+                jnp.int32(DIAG_GROUPS),
+                diag_list,
+                use=use_diag,
+                ahead=lambda first: own(own_geo, rows_ref=rows_ref, first=first),
+                keep=(stage_ref, sems, diag_home),
+            )
+        else:
+            lax.fori_loop(0, DIAG_GROUPS, features, 0)
+            loop(groups[0], pair_list, use=use_pair, keep=(stage_ref, sems, pair_home))
     else:
         stream_loop(jnp.int32(DIAG_GROUPS // 2), diag_home, stage_ref, sems, use_diag)
         stream_loop(lax.div(groups[0], 2), pair_home, stage_ref, sems, use_pair)
@@ -312,18 +331,25 @@
     def fold(value):
         return value + pltpu.roll(value, 4, 0)
 
-    if step < 2:
-        images = (own_out, right_out) if step == 0 else outs
+    if step != 2:
+        if step == "diag":
+            images = (own_out,)
+        else:
+            images = (own_out, right_out) if step == "pairs" else outs
 
         def finish(first):
             place = pl.ds(pl.multiple_of(first * TILE, 8 * TILE), 8 * TILE)
-            own, right = row_sum[pl.ds(first, 8)] + col_sum[pl.ds(first, 8)], col_sum[pl.ds(CB + first, 8)]
-            own = jnp.concatenate([fold(own[k])[:4] for k in range(8)], axis=1)
-            if step == 0:
-                fourth = lax.broadcasted_iota(i32, own.shape, 0) == 3
-                own = own + jnp.where(fourth, stiff_ref[:, place] - SHIFT, 0.0)
-            images[0][:, place] = own
-            images[1][:, place] = jnp.concatenate([fold(right[k])[:4] for k in range(8)], axis=1)
+            sums = row_sum[pl.ds(first, 8)] + col_sum[pl.ds(first, 8)]
+            image = jnp.concatenate([fold(sums[k])[:4] for k in range(8)], axis=1)
+            if step == "diag":
+                fourth = lax.broadcasted_iota(i32, image.shape, 0) == 3
+                image = image + jnp.where(fourth, stiff_ref[:, place] - SHIFT, 0.0)
+            elif step == "pairs":
+                image = image + diag_ref[:, place]
+            images[0][:, place] = image
+            if step != "diag":
+                sums = col_sum[pl.ds(CB + first, 8)]
+                images[1][:, place] = jnp.concatenate([fold(sums[k])[:4] for k in range(8)], axis=1)
 
         each_chunk(CB, finish)
     else:
@@ -343,27 +369,34 @@
     smem = pl.BlockSpec(memory_space=pltpu.SMEM)
     vmem = pl.BlockSpec(memory_space=pltpu.VMEM)
     some = pl.BlockSpec(memory_space=pl.ANY)
-    image = jax.ShapeDtypeStruct((4, CB * TILE), f32)
-    kept = jax.ShapeDtypeStruct((DIAG_GROUPS + PAIR_GROUPS, GROUP, TILE, TILE), bf16)
+    image = (jax.ShapeDtypeStruct((4, CB * TILE), f32), vmem)
+    out = {
+        "diag": (image, (jax.ShapeDtypeStruct((DIAG_GROUPS, GROUP, TILE, TILE), bf16), some)),
+        "pairs": (image, image, (jax.ShapeDtypeStruct((PAIR_GROUPS, GROUP, TILE, TILE), bf16), some)),
+        1: (image, image),
+        2: ((jax.ShapeDtypeStruct((8, TILE), f32), vmem),),
+    }[step]
+    first = step in ("diag", "pairs")
+    blocks = (1 if step == "diag" else 2) * CB + 1
     scratch = [
-        pltpu.VMEM((2 * CB + 1, 8, TILE), f32),
+        pltpu.VMEM((blocks, 8, TILE), f32),
         pltpu.VMEM((CB, 8, TILE), f32),
-        pltpu.VMEM((2 * CB + 1, 8, TILE), f32),
-        pltpu.VMEM((RING, GROUP, TILE, TILE) if step == 0 else (RING // 2, 2, GROUP, TILE, TILE), bf16),
+        pltpu.VMEM((blocks, 8, TILE), f32),
+        pltpu.VMEM((RING, GROUP, TILE, TILE) if first else (RING // 2, 2, GROUP, TILE, TILE), bf16),
         pltpu.SemaphoreType.DMA((RING,)),
     ]
-    if step == 0:
+    if first:
         scratch += [
             pltpu.VMEM((CB, TILE, TILE), bf16),
-            pltpu.VMEM((2 * CB + 1, 8, TILE), f32),
+            pltpu.VMEM((blocks, 8, TILE), f32),
             pltpu.VMEM((GROUP, TILE, TILE), f32),
             pltpu.VMEM((GROUP, TILE, TILE), bf16),
         ]
     return pl.pallas_call(
         functools.partial(pair_body, step),
-        out_shape=((image, image, kept), (image, image), (jax.ShapeDtypeStruct((8, TILE), f32),))[step],
-        in_specs=[smem] * 4 + [vmem] * (len(arrays) - 1) + [vmem if step == 0 else some],
-        out_specs=((vmem, vmem, some), (vmem, vmem), (vmem,))[step],
+        out_shape=tuple(shape for shape, _ in out),
+        in_specs=[smem] * 4 + ([vmem] * len(arrays) if first else [vmem, vmem, some, some]),
+        out_specs=tuple(spec for _, spec in out),
         scratch_shapes=scratch,
         compiler_params=pltpu.CompilerParams(vmem_limit_bytes=48 * 2**20),
         cost_estimate=pl.CostEstimate(flops=2 * 10**9, bytes_accessed=10**8, transcendentals=0),
@@ -469,9 +502,6 @@
 
     geo = {0: ctrl_points, -1: from_behind(ctrl_points, "nodes", -1)}
     beside = from_behind(ctrl_disp, "nodes", -1)
-    later, beside = lax.optimization_barrier((ctrl_points, beside))
-    for offset in (1, 2, -2):
-        geo[offset] = from_behind(later, "nodes", offset)
     table = offset_table()
 
     slots = lax.iota(i32, MAXT)
@@ -499,18 +529,26 @@
         ahead = from_behind(own_part, "nodes", -1)
         return own_part + back, ahead + right_part
 
-    own_part, right_part, tiles = images(0, ctrl_disp, beside, geo[0], geo[-1], table, stiffness[None, :])
+    own_part, diag_tiles = images("diag", ctrl_disp, ctrl_points, table, stiffness[None, :])
+    own_part, right_part, pair_tiles = images(
+        "pairs", ctrl_disp, beside, ctrl_points, geo[-1], table, own_part
+    )
+    tiles = (diag_tiles, pair_tiles)
+    total, total_beside = exchanged(own_part, right_part)
+    diagonal, diagonal_beside = total[3:4], total_beside[3:4]
+    first = total[:3] + diagonal * ctrl_disp
+    first_beside = total_beside[:3] + diagonal_beside * beside
+    later, first = lax.optimization_barrier((ctrl_points, first))
+    for offset in (1, 2, -2):
+        geo[offset] = from_behind(later, "nodes", offset)
+    own_part, right_part = images(1, first, first_beside, *tiles)
     own_part, right_part, geo[1], geo[2], geo[-2] = lax.optimization_barrier(
         (own_part, right_part, geo[1], geo[2], geo[-2])
     )
     total, total_beside = exchanged(own_part, right_part)
-    diagonal, diagonal_beside = total[3:4], total_beside[3:4]
-    first = total[:3] + diagonal * ctrl_disp
-    first_beside = total_beside[:3] + diagonal_beside * beside
-    total, total_beside = exchanged(*images(1, first, first_beside, tiles))
     second = total[:3] + diagonal * first
     second_beside = total_beside[:3] + diagonal_beside * first_beside
-    (quad,) = images(2, second, second_beside, tiles)
+    (quad,) = images(2, second, second_beside, *tiles)
     moments = jnp.concatenate(
         [
             comp_sum(ctrl_disp, ctrl_disp),

time: 208 us -> 210 us (level)
  the two profiles are of different devices: /device:TPU:64 before, /device:TPU:31 now
where the time goes in v6:
time: 210 us; the launch traced here: 211 us
  Pallas kernels  91.9 us (44%)
  starting transfers between devices  48.9 us (23%)
  blocking collectives  35.6 us (17%)
  waiting for transfers between devices  22.8 us (11%)
  local copies, waits for them, and re-layouts  5.52 us (3%)
  other arithmetic  3.99 us (2%)
  between operations  2.38 us (1%)
    pallas_call x4, Pallas kernels, pair_call(): pl.pallas_call(functools.partial(pair_body, step), out_shape=tuple((shape...  58.9 us
    ppermute x9, starting transfers between devices, from_behind(): return lax.ppermute(block, axis, route)  40.8 us
    all_to_all x1, blocking collectives, body(): lax.all_to_all(sent, 'nodes', 0, 0, tiled=True)  35.6 us
    pallas_call x1, Pallas kernels, volume_call(): pl.pallas_call(volume_body, out_shape=jax.ShapeDtypeStruct((3, VB * TILE)...  33 us
    ppermute x9, waiting for transfers between devices, from_behind(): return lax.ppermute(block, axis, route)  11.8 us
    ppermute x4, waiting for transfers between devices, send(): lax.ppermute(value, axis, [(i, target(i)) for i in devices if target(i) i...  11 us
    ppermute x4, starting transfers between devices, send(): lax.ppermute(value, axis, [(i, target(i)) for i in devices if target(i) i...  8.02 us
    unnamed x32, local copies, waits for them, and re-layouts  4.79 us
  transfers between devices with their start and end apart: 13, of which 6 were waited for; matrix products, arithmetic and copies ran while one was open for 1% of the time, Pallas kernels for 13%

profile of v6, /device:TPU:31, one launch (start us, length us, event | category | flops | bytes accessed | tf_op | source)
XLA Modules:
  0.0 211.0 jit_solution(13737681001815061437)
XLA Ops:
  0.6 2.6 %collective-permute-start = (f32[3,32768]{1,0:T(4,128)}, f32[3,32768]{1,0:T(4,128)S(1)}, u32[]{:S(2)}, u32[]{:S(2)}) collective-permute-start(f32[3,32768]{1,0:T(4,128)} %refs_0_.3), channel_id=1, source_target_pairs={{1,0},{2,1},{3,2},{4,3},{5,4},{6,5},{7,6},{8,7},{9,8},{10,9},{11,1... | collective-permute-start | bytes 1179656 | tf_op jit(solution)/shard_map/ppermute | solution.py:32
  3.2 2.2 %collective-permute-start.1 = (f32[3,32768]{1,0:T(4,128)}, f32[3,32768]{1,0:T(4,128)S(1)}, u32[]{:S(2)}, u32[]{:S(2)}) collective-permute-start(f32[3,32768]{1,0:T(4,128)} %refs_2_.3), channel_id=1, source_target_pairs={{1,0},{2,1},{3,2},{4,3},{5,4},{6,5},{7,6},{8,7},{9,8},{10,9},{11,1... | collective-permute-start | bytes 1179656 | tf_op jit(solution)/shard_map/ppermute | solution.py:32
  7.2 1.2 copy-done
  8.5 1.0 copy-done.3
  10.4 13.6 %pair_tiles_diag.1 = (f32[4,32768]{1,0:T(4,128)S(1)}, bf16[16,16,128,128]{3,2,1,0:T(8,128)(2,1)}) custom-call(s32[1]{0:T(128)} %bitcast.me, s32[1]{0:T(128)S(6)} %mul.371.groups, s32[256]{0:T(256)S(1)} %fusion.41.diag_list, s32[768]{0:T(1024)S(1)} %fusion.13.pair_list, f32[3,32768]{1,0:T(4,128)S(1)} %copy-done, f32[3,32768]{1,0:T(4,128)S(1)} %copy-done.3, ...), custom_call_target="tpu_custom_call" | custom-call | flops 2000000000 | bytes 100000000 | tf_op jit(solution)/shard_map/pair_tiles_diag/pallas_call | solution.py:395
  24.1 19.9 %pair_tiles_pairs.1 = (f32[4,32768]{1,0:T(4,128)S(1)}, f32[4,32768]{1,0:T(4,128)S(1)}, bf16[48,16,128,128]{3,2,1,0:T(8,128)(2,1)}) custom-call(s32[1]{0:T(128)} %bitcast.me, s32[1]{0:T(128)S(6)} %mul.371.groups, s32[256]{0:T(256)S(1)} %fusion.41.diag_list, s32[768]{0:T(1024)S(1)} %fusion.13.pair_list, f32[3,32768]{1,0:T(4,128)S(1)} %copy-done, ...), custom_call_target="tpu_custom_call" | custom-call | flops 2000000000 | bytes 100000000 | tf_op jit(solution)/shard_map/pair_tiles_pairs/pallas_call | solution.py:395
  43.9 10.5 %collective-permute-start.2 = (f32[4,32768]{1,0:T(4,128)S(1)}, f32[4,32768]{1,0:T(4,128)S(1)}, u32[]{:S(2)}, u32[]{:S(2)}) collective-permute-start(f32[4,32768]{1,0:T(4,128)S(1)} %get-tuple-element.18), channel_id=1, source_target_pairs={{0,1},{1,2},{2,3},{3,4},{4,5},{5,6},{6,7},{7,8},{8,9},{9,10},{10,1... | collective-permute-start | bytes 1572872 | tf_op jit(solution)/shard_map/ppermute | solution.py:32
  54.4 1.9 collective-permute-start.3
  56.4 4.2 %collective-permute-done.2 = f32[4,32768]{1,0:T(4,128)S(1)} collective-permute-done((f32[4,32768]{1,0:T(4,128)S(1)}, f32[4,32768]{1,0:T(4,128)S(1)}, u32[]{:S(2)}, u32[]{:S(2)}) %collective-permute-start.2) | collective-permute-done | bytes 524320 | tf_op jit(solution)/shard_map/ppermute | solution.py:32
  61.0 8.6 %collective-permute-start.4 = (f32[3,32768]{1,0:T(4,128)S(1)}, f32[3,32768]{1,0:T(4,128)S(1)}, u32[]{:S(2)}, u32[]{:S(2)}) collective-permute-start(f32[3,32768]{1,0:T(4,128)S(1)} %copy-done.3), channel_id=1, source_target_pairs={{0,1},{1,2},{2,3},{3,4},{4,5},{5,6},{6,7},{7,8},{8,9},{9,10},{10,1... | collective-permute-start | bytes 1179656 | tf_op jit(solution)/shard_map/ppermute | solution.py:32
  69.6 1.9 collective-permute-start.5
  71.6 3.4 %collective-permute-start.6 = (f32[3,32768]{1,0:T(4,128)S(1)}, f32[3,32768]{1,0:T(4,128)S(1)}, u32[]{:S(2)}, u32[]{:S(2)}) collective-permute-start(f32[3,32768]{1,0:T(4,128)S(1)} %copy-done.3), channel_id=1, source_target_pairs={{2,0},{3,1},{4,2},{5,3},{6,4},{7,5},{8,6},{9,7},{10,8},{11,9},{12,... | collective-permute-start | bytes 1179656 | tf_op jit(solution)/shard_map/ppermute | solution.py:32
  75.4 13.5 %pair_tiles_1.1 = (f32[4,32768]{1,0:T(4,128)S(1)}, f32[4,32768]{1,0:T(4,128)S(1)}) custom-call(s32[1]{0:T(128)} %bitcast.me, s32[1]{0:T(128)S(6)} %mul.371.groups, s32[256]{0:T(256)S(1)} %fusion.41.diag_list, s32[768]{0:T(1024)S(1)} %fusion.13.pair_list, f32[3,32768]{1,0:T(4,128)S(1)} %slice_add_fusion.3.refs_0_, f32[3,32768]{1,0:T(4,128)S(1)} %slice_add_fusion.2.refs_1_, ...), custom_call_target="tpu_custom_call" | custom-call | flops 2000000000 | bytes 100000000 | tf_op jit(solution)/shard_map/pair_tiles_1/pallas_call | solution.py:395
  89.0 1.8 collective-permute-done.6.refs_4_
  90.8 3.1 %collective-permute-start.8 = (f32[4,32768]{1,0:T(4,128)S(1)}, f32[4,32768]{1,0:T(4,128)S(1)}, u32[]{:S(2)}, u32[]{:S(2)}) collective-permute-start(f32[4,32768]{1,0:T(4,128)S(1)} %get-tuple-element.25), channel_id=1, source_target_pairs={{1,0},{2,1},{3,2},{4,3},{5,4},{6,5},{7,6},{8,7},{9,8},{10,9},{11,1... | collective-permute-start | bytes 1572872 | tf_op jit(solution)/shard_map/ppermute | solution.py:32
  93.9 6.6 %collective-permute-start.7 = (f32[4,32768]{1,0:T(4,128)S(1)}, f32[4,32768]{1,0:T(4,128)S(1)}, u32[]{:S(2)}, u32[]{:S(2)}) collective-permute-start(f32[4,32768]{1,0:T(4,128)S(1)} %get-tuple-element.26), channel_id=1, source_target_pairs={{0,1},{1,2},{2,3},{3,4},{4,5},{5,6},{6,7},{7,8},{8,9},{9,10},{10,1... | collective-permute-start | bytes 1572872 | tf_op jit(solution)/shard_map/ppermute | solution.py:32
  100.6 4.9 %collective-permute-done.8 = f32[4,32768]{1,0:T(4,128)S(1)} collective-permute-done((f32[4,32768]{1,0:T(4,128)S(1)}, f32[4,32768]{1,0:T(4,128)S(1)}, u32[]{:S(2)}, u32[]{:S(2)}) %collective-permute-start.8) | collective-permute-done | bytes 524320 | tf_op jit(solution)/shard_map/ppermute | solution.py:32
  107.7 11.9 %pair_tiles_2.1 = f32[8,128]{1,0:T(8,128)S(1)} custom-call(s32[1]{0:T(128)} %bitcast.me, s32[1]{0:T(128)S(6)} %mul.371.groups, s32[256]{0:T(256)S(1)} %fusion.41.diag_list, s32[768]{0:T(1024)S(1)} %fusion.13.pair_list, f32[3,32768]{1,0:T(4,128)S(1)} %get-tuple-element.44.refs_0_, f32[3,32768]{1,0:T(4,128)S(1)} %fusion.1.refs_1_, ...), custom_call_target="tpu_custom_call" | custom-call | flops 2000000000 | bytes 100000000 | tf_op jit(solution)/shard_map/pair_tiles_2/pallas_call | solution.py:395
  119.9 35.6 %all_to_all.5 = f32[128,1,128]{2,1,0:T(1,128)S(1)} all-to-all(f32[128,1,128]{2,1,0:T(1,128)S(1)} %broadcast_in_dim.37), channel_id=1, replica_groups=mesh['nodes'=128] {'nodes'}, dimensions={0} | all-to-all | bytes 131072 | tf_op jit(solution)/shard_map/all_to_all | solution.py:565
  156.1 6.0 %collective-permute-start.10 = (f32[3,32768]{1,0:T(4,128)S(1)}, f32[3,32768]{1,0:T(4,128)S(1)}, u32[]{:S(2)}, u32[]{:S(2)}) collective-permute-start(f32[3,32768]{1,0:T(4,128)S(1)} %multiply_add_fusion.refs_7_), channel_id=1, source_target_pairs={{1,2},{2,1},{3,4},{4,3},{5,6},{6,5},{7,8},{8,7},{9,10},{10,9},{11,... | collective-permute-start | bytes 1179656 | tf_op jit(solution)/shard_map/ppermute | solution.py:39
  162.2 1.9 collective-permute-start.9
  164.1 6.7 %collective-permute-done.10.refs_6_ = f32[3,32768]{1,0:T(4,128)S(1)} collective-permute-done((f32[3,32768]{1,0:T(4,128)S(1)}, f32[3,32768]{1,0:T(4,128)S(1)}, u32[]{:S(2)}, u32[]{:S(2)}) %collective-permute-start.10) | collective-permute-done | bytes 393248 | tf_op jit(solution)/shard_map/ppermute | solution.py:39
  172.1 4.3 %collective-permute-done.9.refs_5_ = f32[3,32768]{1,0:T(4,128)S(1)} collective-permute-done((f32[3,32768]{1,0:T(4,128)S(1)}, f32[3,32768]{1,0:T(4,128)S(1)}, u32[]{:S(2)}, u32[]{:S(2)}) %collective-permute-start.9) | collective-permute-done | bytes 393248 | tf_op jit(solution)/shard_map/ppermute | solution.py:39
  178.0 33.0 %volume_tiles.1 = f32[3,32768]{1,0:T(4,128)} custom-call(s32[1]{0:T(128)} %bitcast.me, s32[1]{0:T(128)S(6)} %select_n.129.groups, s32[512]{0:T(512)} %or_select_fusion.vol_list, f32[3,32768]{1,0:T(4,128)} %vol_geo.1, f32[3,32768]{1,0:T(4,128)} %copy-done.10, f32[3,32768]{1,0:T(4,128)} %copy-done.9, f32[3,32768]{1,0:T(4,128)} %refs_2_.3, ...), custom_call_target="tpu_custom_call" | custom-call | flops 2000000000 | bytes 100000000 | tf_op jit(solution)/shard_map/volume_tiles/pallas_call | solution.py:447
  (67 shorter events, 8.3 us)
Async XLA Ops:
  0.6 23.4 %collective-permute-start = (f32[3,32768]{1,0:T(4,128)}, f32[3,32768]{1,0:T(4,128)S(1)}, u32[]{:S(2)}, u32[]{:S(2)}) collective-permute-start(f32[3,32768]{1,0:T(4,128)} %refs_0_.3), channel_id=1, source_target_pairs={{1,0},{2,1},{3,2},{4,3},{5,4},{6,5},{7,6},{8,7},{9,8},{10,9},{11,1... | collective-permute-start | bytes 1179656 | tf_op jit(solution)/shard_map/ppermute | solution.py:32
  3.2 20.8 %collective-permute-start.1 = (f32[3,32768]{1,0:T(4,128)}, f32[3,32768]{1,0:T(4,128)S(1)}, u32[]{:S(2)}, u32[]{:S(2)}) collective-permute-start(f32[3,32768]{1,0:T(4,128)} %refs_2_.3), channel_id=1, source_target_pairs={{1,0},{2,1},{3,2},{4,3},{5,4},{6,5},{7,6},{8,7},{9,8},{10,9},{11,1... | collective-permute-start | bytes 1179656 | tf_op jit(solution)/shard_map/ppermute | solution.py:32
  7.2 81.7 %copy-start.2 = (f32[125,8,128]{2,1,0:T(8,128)}, f32[125,8,128]{2,1,0:T(8,128)S(1)}, u32[]{:S(2)}) copy-start(f32[125,8,128]{2,1,0:T(8,128)S(1)} %broadcast_in_dim.34.refs_2_.refs_4_.refs_10_) | copy-start | bytes 1536004
  24.0 81.7 %copy-start.4 = (f32[3,32768]{1,0:T(4,128)}, f32[3,32768]{1,0:T(4,128)S(1)}, u32[]{:S(2)}) copy-start(f32[3,32768]{1,0:T(4,128)S(1)} %collective-permute-done.1.refs_3_) | copy-start | bytes 1179652
  24.0 82.6 %copy-start.1 = (f32[3,32768]{1,0:T(4,128)S(1)}, f32[3,32768]{1,0:T(4,128)}, u32[]{:S(2)}) copy-start(f32[3,32768]{1,0:T(4,128)} %refs_0_.3) | copy-start | bytes 1179652
  43.9 16.6 %collective-permute-start.2 = (f32[4,32768]{1,0:T(4,128)S(1)}, f32[4,32768]{1,0:T(4,128)S(1)}, u32[]{:S(2)}, u32[]{:S(2)}) collective-permute-start(f32[4,32768]{1,0:T(4,128)S(1)} %get-tuple-element.18), channel_id=1, source_target_pairs={{0,1},{1,2},{2,3},{3,4},{4,5},{5,6},{6,7},{7,8},{8,9},{9,10},{10,1... | collective-permute-start | bytes 1572872 | tf_op jit(solution)/shard_map/ppermute | solution.py:32
  54.4 20.5 %collective-permute-start.3 = (f32[4,32768]{1,0:T(4,128)S(1)}, f32[4,32768]{1,0:T(4,128)S(1)}, u32[]{:S(2)}, u32[]{:S(2)}) collective-permute-start(f32[4,32768]{1,0:T(4,128)S(1)} %get-tuple-element.17), channel_id=1, source_target_pairs={{1,0},{2,1},{3,2},{4,3},{5,4},{6,5},{7,6},{8,7},{9,8},{10,9},{11,1... | collective-permute-start | bytes 1572872 | tf_op jit(solution)/shard_map/ppermute | solution.py:32
  61.0 28.0 %collective-permute-start.4 = (f32[3,32768]{1,0:T(4,128)S(1)}, f32[3,32768]{1,0:T(4,128)S(1)}, u32[]{:S(2)}, u32[]{:S(2)}) collective-permute-start(f32[3,32768]{1,0:T(4,128)S(1)} %copy-done.3), channel_id=1, source_target_pairs={{0,1},{1,2},{2,3},{3,4},{4,5},{5,6},{6,7},{7,8},{8,9},{9,10},{10,1... | collective-permute-start | bytes 1179656 | tf_op jit(solution)/shard_map/ppermute | solution.py:32
  69.6 19.4 %collective-permute-start.5 = (f32[3,32768]{1,0:T(4,128)S(1)}, f32[3,32768]{1,0:T(4,128)S(1)}, u32[]{:S(2)}, u32[]{:S(2)}) collective-permute-start(f32[3,32768]{1,0:T(4,128)S(1)} %copy-done.3), channel_id=1, source_target_pairs={{0,2},{1,3},{2,4},{3,5},{4,6},{5,7},{6,8},{7,9},{8,10},{9,11},{10,... | collective-permute-start | bytes 1179656 | tf_op jit(solution)/shard_map/ppermute | solution.py:32
  71.6 19.2 %collective-permute-start.6 = (f32[3,32768]{1,0:T(4,128)S(1)}, f32[3,32768]{1,0:T(4,128)S(1)}, u32[]{:S(2)}, u32[]{:S(2)}) collective-permute-start(f32[3,32768]{1,0:T(4,128)S(1)} %copy-done.3), channel_id=1, source_target_pairs={{2,0},{3,1},{4,2},{5,3},{6,4},{7,5},{8,6},{9,7},{10,8},{11,9},{12,... | collective-permute-start | bytes 1179656 | tf_op jit(solution)/shard_map/ppermute | solution.py:32
  89.0 82.5 %copy-start.7 = (s32[512]{0:T(512)S(1)}, s32[512]{0:T(512)}, u32[]{:S(2)}) copy-start(s32[512]{0:T(512)} %param.17) | copy-start | bytes 6148
  89.0 82.5 %copy-start.8 = (s32[512]{0:T(512)S(1)}, s32[512]{0:T(512)}, u32[]{:S(2)}) copy-start(s32[512]{0:T(512)} %param.18) | copy-start | bytes 6148
  89.0 18.7 %copy-start.9 = (f32[3,32768]{1,0:T(4,128)}, f32[3,32768]{1,0:T(4,128)S(1)}, u32[]{:S(2)}) copy-start(f32[3,32768]{1,0:T(4,128)S(1)} %collective-permute-done.4.refs_1_) | copy-start | bytes 1179652
  89.0 18.7 %copy-start.10 = (f32[3,32768]{1,0:T(4,128)}, f32[3,32768]{1,0:T(4,128)S(1)}, u32[]{:S(2)}) copy-start(f32[3,32768]{1,0:T(4,128)S(1)} %collective-permute-done.5.refs_0_) | copy-start | bytes 1179652
  90.8 16.9 %copy-start.11 = (f32[3,32768]{1,0:T(4,128)}, f32[3,32768]{1,0:T(4,128)S(1)}, u32[]{:S(2)}) copy-start(f32[3,32768]{1,0:T(4,128)S(1)} %collective-permute-done.6.refs_4_) | copy-start | bytes 1179652
  90.8 14.7 %collective-permute-start.8 = (f32[4,32768]{1,0:T(4,128)S(1)}, f32[4,32768]{1,0:T(4,128)S(1)}, u32[]{:S(2)}, u32[]{:S(2)}) collective-permute-start(f32[4,32768]{1,0:T(4,128)S(1)} %get-tuple-element.25), channel_id=1, source_target_pairs={{1,0},{2,1},{3,2},{4,3},{5,4},{6,5},{7,6},{8,7},{9,8},{10,9},{11,1... | collective-permute-start | bytes 1572872 | tf_op jit(solution)/shard_map/ppermute | solution.py:32
  93.9 12.8 %collective-permute-start.7 = (f32[4,32768]{1,0:T(4,128)S(1)}, f32[4,32768]{1,0:T(4,128)S(1)}, u32[]{:S(2)}, u32[]{:S(2)}) collective-permute-start(f32[4,32768]{1,0:T(4,128)S(1)} %get-tuple-element.26), channel_id=1, source_target_pairs={{0,1},{1,2},{2,3},{3,4},{4,5},{5,6},{6,7},{7,8},{8,9},{9,10},{10,1... | collective-permute-start | bytes 1572872 | tf_op jit(solution)/shard_map/ppermute | solution.py:32
  156.1 20.4 %copy-start.6 = (f32[3,32768]{1,0:T(4,128)}, f32[3,32768]{1,0:T(4,128)S(1)}, u32[]{:S(2)}) copy-start(f32[3,32768]{1,0:T(4,128)S(1)} %multiply_add_fusion.refs_7_) | copy-start | bytes 1179652
  156.1 14.7 %collective-permute-start.10 = (f32[3,32768]{1,0:T(4,128)S(1)}, f32[3,32768]{1,0:T(4,128)S(1)}, u32[]{:S(2)}, u32[]{:S(2)}) collective-permute-start(f32[3,32768]{1,0:T(4,128)S(1)} %multiply_add_fusion.refs_7_), channel_id=1, source_target_pairs={{1,2},{2,1},{3,4},{4,3},{5,6},{6,5},{7,8},{8,7},{9,10},{10,9},{11,... | collective-permute-start | bytes 1179656 | tf_op jit(solution)/shard_map/ppermute | solution.py:39
  162.1 10.0 %collective-permute-start.11 = (f32[3,32768]{1,0:T(4,128)S(1)}, f32[3,32768]{1,0:T(4,128)S(1)}, u32[]{:S(2)}, u32[]{:S(2)}) collective-permute-start(f32[3,32768]{1,0:T(4,128)S(1)} %multiply_add_fusion.refs_7_), channel_id=1, source_target_pairs={{0,1},{1,0},{2,3},{3,2},{4,5},{5,4},{6,7},{7,6},{8,9},{9,8},{10,11... | collective-permute-start | bytes 1179656 | tf_op jit(solution)/shard_map/ppermute | solution.py:39
  162.2 14.2 %collective-permute-start.9 = (f32[3,32768]{1,0:T(4,128)S(1)}, f32[3,32768]{1,0:T(4,128)S(1)}, u32[]{:S(2)}, u32[]{:S(2)}) collective-permute-start(f32[3,32768]{1,0:T(4,128)S(1)} %multiply_add_fusion.refs_7_), channel_id=1, source_target_pairs={{0,2},{2,4},{3,1},{4,6},{5,3},{6,8},{7,5},{8,10},{9,7},{10,12},{11... | collective-permute-start | bytes 1179656 | tf_op jit(solution)/shard_map/ppermute | solution.py:39
  170.8 5.6 %copy-start.12 = (f32[3,32768]{1,0:T(4,128)}, f32[3,32768]{1,0:T(4,128)S(1)}, u32[]{:S(2)}) copy-start(f32[3,32768]{1,0:T(4,128)S(1)} %collective-permute-done.10.refs_6_) | copy-start | bytes 1179652
  170.8 5.6 %collective-permute-start.12 = (f32[3,32768]{1,0:T(4,128)S(1)}, f32[3,32768]{1,0:T(4,128)S(1)}, u32[]{:S(2)}, u32[]{:S(2)}) collective-permute-start(f32[3,32768]{1,0:T(4,128)S(1)} %collective-permute-done.10.refs_6_), channel_id=1, source_target_pairs={{0,1},{1,0},{2,3},{3,2},{4,5},{5,4},{6,7},{7,6},{8,9},{9,8},{10,11... | collective-permute-start | bytes 1179656 | tf_op jit(solution)/shard_map/ppermute | solution.py:39
  172.1 4.3 %copy-start.13 = (f32[3,32768]{1,0:T(4,128)}, f32[3,32768]{1,0:T(4,128)S(1)}, u32[]{:S(2)}) copy-start(f32[3,32768]{1,0:T(4,128)S(1)} %collective-permute-done.11.refs_8_) | copy-start | bytes 1179652
  (5 other events, 4.8 us)

commit v7 on v6

--- a/solution.py
+++ b/solution.py
@@ -16,6 +16,7 @@
 GROUP = 16
 PART = 32
 RING = 8
+EIGHT = 8
 DIAG_GROUPS = CB // GROUP
 PAIR_GROUPS = MAXT // GROUP
 SHIFT = 0.75
@@ -43,6 +44,12 @@
     partner = send(block, lambda i: i ^ 1)
     shared = send(near, lambda i: i ^ 1)
     return [far, near, block, partner, shared]
+
+
+def gathered_eights(block, axis, shift):
+    size = lax.axis_size(axis)
+    groups = [[(EIGHT * g + shift + k) % size for k in range(EIGHT)] for g in range(size // EIGHT)]
+    return lax.all_gather(block, axis, axis_index_groups=groups)
 
 
 def offset_table():
@@ -404,10 +411,25 @@
     )(me, groups, diag_list, pair_list, *arrays)
 
 
-def volume_body(me, groups, vol_list, vol_geo, *refs):
-    geos, coefs = refs[:5], refs[5:10]
-    table_ref, out, rows_ref, cols_ref, coef_ref, sums, dist_ref, tile_ref = refs[10:]
-    column_rows(geos, [me[0] + k for k in range(-2, 3)], cols_ref)
+def volume_body(me, groups, vol_list, vol_geo, own_geo, ahead_geo, *refs):
+    coefs, refs = refs[:5], refs[5:]
+    table_ref, plain, shifted, out, rows_ref, cols_ref, coef_ref, sums, dist_ref, tile_ref, far_geo, sems = refs
+    at = lax.rem(me[0], EIGHT)
+    inner = (at >= 2) & (at < EIGHT - 2)
+
+    def fetch(source, index, k):
+        return pltpu.make_async_copy(source.at[index], far_geo.at[k], sems.at[k])
+
+    for k, step in enumerate((-2, -1, 2)):
+
+        @pl.when(inner)
+        def _():
+            fetch(plain, at + step, k).start()
+
+        @pl.when(jnp.logical_not(inner))
+        def _():
+            fetch(shifted, lax.rem(at + EIGHT // 2, EIGHT) + step, k).start()
+
     odd = lax.rem(me[0], 2)
     vector_rows(coefs, coef_ref, 0.0, [jnp.where(odd == 1, 4 - k, k) for k in range(5)])
     sums[...] = jnp.zeros_like(sums)
@@ -417,6 +439,10 @@
         return carry
 
     lax.fori_loop(0, VB // 16, features, 0)
+    for k in range(3):
+        fetch(plain, 0, k).wait()
+    geos = (far_geo.at[0], far_geo.at[1], own_geo, ahead_geo, far_geo.at[2])
+    column_rows(geos, [me[0] + k for k in range(-2, 3)], cols_ref)
 
     def use(first, k, pair):
         dims = (((1,), (1,)), ((), ()))
@@ -447,7 +473,7 @@
     return pl.pallas_call(
         volume_body,
         out_shape=jax.ShapeDtypeStruct((3, VB * TILE), f32),
-        in_specs=[smem] * 3 + [vmem] * len(arrays),
+        in_specs=[smem] * 3 + [vmem] * (len(arrays) - 2) + [pl.BlockSpec(memory_space=pl.ANY)] * 2,
         out_specs=vmem,
         scratch_shapes=[
             pltpu.VMEM((VB, TILE, TILE), bf16),
@@ -456,6 +482,8 @@
             pltpu.VMEM((VB, 8, TILE), f32),
             pltpu.VMEM((GROUP, TILE, TILE), f32),
             pltpu.VMEM((GROUP, TILE, TILE), f32),
+            pltpu.VMEM((3, 3, CB * TILE), f32),
+            pltpu.SemaphoreType.DMA((3,)),
         ],
         compiler_params=pltpu.CompilerParams(vmem_limit_bytes=56 * 2**20),
         cost_estimate=pl.CostEstimate(flops=2 * 10**9, bytes_accessed=10**8, transcendentals=0),
@@ -498,10 +526,10 @@
 def body(ctrl_points, ctrl_disp, stiffness, pair_rows, pair_cols, pair_count, vol_points, vol_rows, vol_cols, vol_count):
     me = lax.axis_index("nodes")
     devices = lax.axis_size("nodes")
-    order = (2, 1, 0, -1, -2)
-
-    geo = {0: ctrl_points, -1: from_behind(ctrl_points, "nodes", -1)}
+
+    ahead = from_behind(ctrl_points, "nodes", -1)
     beside = from_behind(ctrl_disp, "nodes", -1)
+    gathered = [gathered_eights(ctrl_points, "nodes", shift) for shift in (0, EIGHT // 2)]
     table = offset_table()
 
     slots = lax.iota(i32, MAXT)
@@ -531,20 +559,16 @@
 
     own_part, diag_tiles = images("diag", ctrl_disp, ctrl_points, table, stiffness[None, :])
     own_part, right_part, pair_tiles = images(
-        "pairs", ctrl_disp, beside, ctrl_points, geo[-1], table, own_part
+        "pairs", ctrl_disp, beside, ctrl_points, ahead, table, own_part
     )
+    own_part, right_part, gathered[0] = lax.optimization_barrier((own_part, right_part, gathered[0]))
     tiles = (diag_tiles, pair_tiles)
     total, total_beside = exchanged(own_part, right_part)
     diagonal, diagonal_beside = total[3:4], total_beside[3:4]
     first = total[:3] + diagonal * ctrl_disp
     first_beside = total_beside[:3] + diagonal_beside * beside
-    later, first = lax.optimization_barrier((ctrl_points, first))
-    for offset in (1, 2, -2):
-        geo[offset] = from_behind(later, "nodes", offset)
     own_part, right_part = images(1, first, first_beside, *tiles)
-    own_part, right_part, geo[1], geo[2], geo[-2] = lax.optimization_barrier(
-        (own_part, right_part, geo[1], geo[2], geo[-2])
-    )
+    own_part, right_part, gathered[1] = lax.optimization_barrier((own_part, right_part, gathered[1]))
     total, total_beside = exchanged(own_part, right_part)
     second = total[:3] + diagonal * first
     second_beside = total_beside[:3] + diagonal_beside * first_beside
@@ -566,7 +590,7 @@
     weights = cg_weights([moments[3 * k : 3 * k + 3] for k in range(6)])
     coef = sum(w[:, None] * u for w, u in zip(weights, (ctrl_disp, first, second)))
     near = around(coef, "nodes")
-    moved = volume_call(here, vol_groups, vol_list, vol_points, *[geo[k] for k in order], *near, table)
+    moved = volume_call(here, vol_groups, vol_list, vol_points, ctrl_points, ahead, *near, table, *gathered)
     return (coef, moved)
 
 

time: 210 us -> 238 us (1.13)
  waiting for transfers between devices: 22.8 us -> 51.9 us
  blocking collectives: 35.6 us -> 19.5 us
  between operations: 2.38 us -> 17.1 us
  starting transfers between devices: 48.9 us -> 34.7 us
  Pallas kernels: 91.9 us -> 102 us
    all_gather x0 -> x2, waiting for transfers between devices: none -> 26.4 us  [gathered_eights(): return lax.all_gather(block, axis, axis_index_groups=groups)]
    ppermute x9 -> x6, starting transfers between devices: 40.8 us -> 24.3 us  [from_behind(): return lax.ppermute(block, axis, route)]
    all_to_all x1, blocking collectives: 35.6 us -> 19.5 us  [body(): lax.all_to_all(sent, 'nodes', 0, 0, tiled=True)]
    pallas_call x4, Pallas kernels: 58.9 us -> 68.6 us  [pair_call(): pl.pallas_call(functools.partial(pair_body, step), out_shape=tuple((shape...]
    ppermute x9 -> x6, waiting for transfers between devices: 11.8 us -> 16.1 us  [from_behind(): return lax.ppermute(block, axis, route)]
    unnamed x32 -> x26, local copies, waits for them, and re-layouts: 4.79 us -> 4.97 us
  transfers between devices with their start and end apart: 13 -> 12, of which waited for: 6 -> 7; matrix products, arithmetic and copies ran while one was open for 1% -> 2% of each run, Pallas kernels for 13% -> 23%
where the time goes in v7:
time: 238 us; the launch traced here: 237 us
  Pallas kernels  102 us (43%)
  waiting for transfers between devices  51.9 us (22%)
  starting transfers between devices  34.7 us (15%)
  blocking collectives  19.5 us (8%)
  between operations  17.1 us (7%)
  other arithmetic  6.1 us (3%)
  local copies, waits for them, and re-layouts  5.7 us (2%)
    pallas_call x4, Pallas kernels, pair_call(): pl.pallas_call(functools.partial(pair_body, step), out_shape=tuple((shape...  68.6 us
    pallas_call x1, Pallas kernels, volume_call(): pl.pallas_call(volume_body, out_shape=jax.ShapeDtypeStruct((3, VB * TILE)...  33.3 us
    all_gather x2, waiting for transfers between devices, gathered_eights(): return lax.all_gather(block, axis, axis_index_groups=groups)  26.4 us
    ppermute x6, starting transfers between devices, from_behind(): return lax.ppermute(block, axis, route)  24.3 us
    all_to_all x1, blocking collectives, body(): lax.all_to_all(sent, 'nodes', 0, 0, tiled=True)  19.5 us
    ppermute x6, waiting for transfers between devices, from_behind(): return lax.ppermute(block, axis, route)  16.1 us
    ppermute x4, starting transfers between devices, send(): lax.ppermute(value, axis, [(i, target(i)) for i in devices if target(i) i...  10.3 us
    ppermute x4, waiting for transfers between devices, send(): lax.ppermute(value, axis, [(i, target(i)) for i in devices if target(i) i...  8.75 us
  transfers between devices with their start and end apart: 12, of which 7 were waited for; matrix products, arithmetic and copies ran while one was open for 2% of the time, Pallas kernels for 23%

profile of v7, /device:TPU:31, one launch (start us, length us, event | category | flops | bytes accessed | tf_op | source)
XLA Modules:
  0.0 236.9 jit_solution(11678031974978682362)
XLA Ops:
  8.8 2.6 %collective-permute-start.1 = (f32[3,32768]{1,0:T(4,128)}, f32[3,32768]{1,0:T(4,128)S(1)}, u32[]{:S(2)}, u32[]{:S(2)}) collective-permute-start(f32[3,32768]{1,0:T(4,128)} %own_geo.1), channel_id=1, source_target_pairs={{1,0},{2,1},{3,2},{4,3},{5,4},{6,5},{7,6},{8,7},{9,8},{10,9},{11,1... | collective-permute-start | bytes 1179656 | tf_op jit(solution)/shard_map/ppermute | solution.py:33
  11.4 2.2 collective-permute-start
  15.4 1.2 copy-done
  18.6 13.6 %pair_tiles_diag.1 = (f32[4,32768]{1,0:T(4,128)S(1)}, bf16[16,16,128,128]{3,2,1,0:T(8,128)(2,1)}) custom-call(s32[1]{0:T(128)} %bitcast.me, s32[1]{0:T(128)S(6)} %mul.371.groups, s32[256]{0:T(256)S(1)} %fusion.41.diag_list, s32[768]{0:T(1024)S(1)} %fusion.13.pair_list, f32[3,32768]{1,0:T(4,128)S(1)} %copy-done.1, f32[3,32768]{1,0:T(4,128)S(1)} %copy-done, ...), custom_call_target="tpu_custom_call" | custom-call | flops 2000000000 | bytes 100000000 | tf_op jit(solution)/shard_map/pair_tiles_diag/pallas_call | solution.py:402
  32.1 5.2 %collective-permute-done.refs_1_ = f32[3,32768]{1,0:T(4,128)S(1)} collective-permute-done((f32[3,32768]{1,0:T(4,128)}, f32[3,32768]{1,0:T(4,128)S(1)}, u32[]{:S(2)}, u32[]{:S(2)}) %collective-permute-start) | collective-permute-done | bytes 393248 | tf_op jit(solution)/shard_map/ppermute | solution.py:33
  37.4 24.7 %pair_tiles_pairs.1 = (f32[4,32768]{1,0:T(4,128)S(1)}, f32[4,32768]{1,0:T(4,128)S(1)}, bf16[48,16,128,128]{3,2,1,0:T(8,128)(2,1)}) custom-call(s32[1]{0:T(128)} %bitcast.me, s32[1]{0:T(128)S(6)} %mul.371.groups, s32[256]{0:T(256)S(1)} %fusion.41.diag_list, s32[768]{0:T(1024)S(1)} %fusion.13.pair_list, f32[3,32768]{1,0:T(4,128)S(1)} %copy-done.1, ...), custom_call_target="tpu_custom_call" | custom-call | flops 2000000000 | bytes 100000000 | tf_op jit(solution)/shard_map/pair_tiles_pairs/pallas_call | solution.py:402
  62.1 1.9 collective-permute-start.3
  64.0 7.9 %collective-permute-start.2 = (f32[4,32768]{1,0:T(4,128)S(1)}, f32[4,32768]{1,0:T(4,128)}, u32[]{:S(2)}, u32[]{:S(2)}) collective-permute-start(f32[4,32768]{1,0:T(4,128)S(1)} %get-tuple-element.19), channel_id=1, source_target_pairs={{0,1},{1,2},{2,3},{3,4},{4,5},{5,6},{6,7},{7,8},{8,9},{9,10},{10,1... | collective-permute-start | bytes 1572872 | tf_op jit(solution)/shard_map/ppermute | solution.py:33
  71.9 5.0 %collective-permute-done.3 = f32[4,32768]{1,0:T(4,128)} collective-permute-done((f32[4,32768]{1,0:T(4,128)S(1)}, f32[4,32768]{1,0:T(4,128)}, u32[]{:S(2)}, u32[]{:S(2)}) %collective-permute-start.3) | collective-permute-done | bytes 524320 | tf_op jit(solution)/shard_map/ppermute | solution.py:33
  76.9 1.2 add.319
  78.3 1.2 add.317
  80.0 16.3 %pair_tiles_1.1 = (f32[4,32768]{1,0:T(4,128)S(1)}, f32[4,32768]{1,0:T(4,128)S(1)}) custom-call(s32[1]{0:T(128)} %bitcast.me, s32[1]{0:T(128)S(6)} %mul.371.groups, s32[256]{0:T(256)S(1)} %fusion.41.diag_list, s32[768]{0:T(1024)S(1)} %fusion.13.pair_list, f32[3,32768]{1,0:T(4,128)S(1)} %slice_add_fusion.3.refs_0_, f32[3,32768]{1,0:T(4,128)S(1)} %slice_add_fusion.2.refs_1_, ...), custom_call_target="tpu_custom_call" | custom-call | flops 2000000000 | bytes 100000000 | tf_op jit(solution)/shard_map/pair_tiles_1/pallas_call | solution.py:402
  96.3 26.3 %all-gather.9.cloned.1.call-done.refs_7_ = f32[8,3,32768]{2,1,0:T(4,128)} async-done(((f32[1,3,32768]{2,1,0:T(4,128)}), f32[8,3,32768]{2,1,0:T(4,128)}) %all-gather.9.cloned.1.call-update) | async-done | bytes 3145744 | tf_op jit(solution)/shard_map/all_gather | solution.py:52
  122.7 1.9 collective-permute-start.5
  124.6 7.9 %collective-permute-start.4 = (f32[4,32768]{1,0:T(4,128)S(1)}, f32[4,32768]{1,0:T(4,128)S(1)}, u32[]{:S(2)}, u32[]{:S(2)}) collective-permute-start(f32[4,32768]{1,0:T(4,128)S(1)} %get-tuple-element.25), channel_id=1, source_target_pairs={{0,1},{1,2},{2,3},{3,4},{4,5},{5,6},{6,7},{7,8},{8,9},{9,10},{10,1... | collective-permute-start | bytes 1572872 | tf_op jit(solution)/shard_map/ppermute | solution.py:33
  132.5 4.9 %collective-permute-done.5 = f32[4,32768]{1,0:T(4,128)S(1)} collective-permute-done((f32[4,32768]{1,0:T(4,128)S(1)}, f32[4,32768]{1,0:T(4,128)S(1)}, u32[]{:S(2)}, u32[]{:S(2)}) %collective-permute-start.5) | collective-permute-done | bytes 524320 | tf_op jit(solution)/shard_map/ppermute | solution.py:33
  139.6 14.1 %pair_tiles_2.1 = f32[8,128]{1,0:T(8,128)S(1)} custom-call(s32[1]{0:T(128)} %bitcast.me, s32[1]{0:T(128)S(6)} %mul.371.groups, s32[256]{0:T(256)S(1)} %fusion.41.diag_list, s32[768]{0:T(1024)S(1)} %fusion.13.pair_list, f32[3,32768]{1,0:T(4,128)S(1)} %get-tuple-element.42.refs_0_, f32[3,32768]{1,0:T(4,128)S(1)} %fusion.1.refs_1_, ...), custom_call_target="tpu_custom_call" | custom-call | flops 2000000000 | bytes 100000000 | tf_op jit(solution)/shard_map/pair_tiles_2/pallas_call | solution.py:402
  153.9 19.5 %all_to_all.5 = f32[128,1,128]{2,1,0:T(1,128)S(1)} all-to-all(f32[128,1,128]{2,1,0:T(1,128)S(1)} %broadcast_in_dim.37), channel_id=1, replica_groups=mesh['nodes'=128] {'nodes'}, dimensions={0} | all-to-all | bytes 131072 | tf_op jit(solution)/shard_map/all_to_all | solution.py:589
  173.9 6.0 %collective-permute-start.7 = (f32[3,32768]{1,0:T(4,128)S(1)}, f32[3,32768]{1,0:T(4,128)S(1)}, u32[]{:S(2)}, u32[]{:S(2)}) collective-permute-start(f32[3,32768]{1,0:T(4,128)S(1)} %multiply_add_fusion.refs_2_), channel_id=1, source_target_pairs={{1,2},{2,1},{3,4},{4,3},{5,6},{6,5},{7,8},{8,7},{9,10},{10,9},{11,... | collective-permute-start | bytes 1179656 | tf_op jit(solution)/shard_map/ppermute | solution.py:40
  180.0 1.9 collective-permute-start.6
  181.9 2.3 collective-permute-start.8
  184.2 4.6 %collective-permute-done.7.refs_1_ = f32[3,32768]{1,0:T(4,128)S(1)} collective-permute-done((f32[3,32768]{1,0:T(4,128)S(1)}, f32[3,32768]{1,0:T(4,128)S(1)}, u32[]{:S(2)}, u32[]{:S(2)}) %collective-permute-start.7) | collective-permute-done | bytes 393248 | tf_op jit(solution)/shard_map/ppermute | solution.py:40
  190.1 4.2 %collective-permute-done.6.refs_0_ = f32[3,32768]{1,0:T(4,128)S(1)} collective-permute-done((f32[3,32768]{1,0:T(4,128)S(1)}, f32[3,32768]{1,0:T(4,128)S(1)}, u32[]{:S(2)}, u32[]{:S(2)}) %collective-permute-start.6) | collective-permute-done | bytes 393248 | tf_op jit(solution)/shard_map/ppermute | solution.py:40
  196.1 33.3 %volume_tiles.1 = f32[3,32768]{1,0:T(4,128)} custom-call(s32[1]{0:T(128)} %bitcast.me, s32[1]{0:T(128)S(6)} %select_n.129.groups, s32[512]{0:T(512)} %or_select_fusion.vol_list, f32[3,32768]{1,0:T(4,128)} %vol_geo.1, f32[3,32768]{1,0:T(4,128)} %own_geo.1, f32[3,32768]{1,0:T(4,128)} %copy-done.4, f32[3,32768]{1,0:T(4,128)} %copy-done.8, ...), custom_call_target="tpu_custom_call" | custom-call | flops 2000000000 | bytes 100000000 | tf_op jit(solution)/shard_map/volume_tiles/pallas_call | solution.py:473
  (61 shorter events, 9.9 us)
Async XLA Ops:
  8.0 54.1 %all-gather.7.cloned.1.call-start = ((), (), s32[]{:S(2)}) async-start(), calls=%async_computation.1 | async-start | bytes 4718592 | tf_op jit(solution)/shard_map/all_gather | solution.py:52
  8.7 113.9 %all-gather.9.cloned.1.call-start = ((), (), s32[]{:S(2)}) async-start(), calls=%async_computation.2 | async-start | bytes 4718592 | tf_op jit(solution)/shard_map/all_gather | solution.py:52
  8.8 28.6 %collective-permute-start.1 = (f32[3,32768]{1,0:T(4,128)}, f32[3,32768]{1,0:T(4,128)S(1)}, u32[]{:S(2)}, u32[]{:S(2)}) collective-permute-start(f32[3,32768]{1,0:T(4,128)} %own_geo.1), channel_id=1, source_target_pairs={{1,0},{2,1},{3,2},{4,3},{5,4},{6,5},{7,6},{8,7},{9,8},{10,9},{11,1... | collective-permute-start | bytes 1179656 | tf_op jit(solution)/shard_map/ppermute | solution.py:33
  11.4 26.0 %collective-permute-start = (f32[3,32768]{1,0:T(4,128)}, f32[3,32768]{1,0:T(4,128)S(1)}, u32[]{:S(2)}, u32[]{:S(2)}) collective-permute-start(f32[3,32768]{1,0:T(4,128)} %refs_0_.3), channel_id=1, source_target_pairs={{1,0},{2,1},{3,2},{4,3},{5,4},{6,5},{7,6},{8,7},{9,8},{10,9},{11,1... | collective-permute-start | bytes 1179656 | tf_op jit(solution)/shard_map/ppermute | solution.py:33
  15.4 62.8 %copy-start.3 = (f32[125,8,128]{2,1,0:T(8,128)}, f32[125,8,128]{2,1,0:T(8,128)S(1)}, u32[]{:S(2)}) copy-start(f32[125,8,128]{2,1,0:T(8,128)S(1)} %broadcast_in_dim.34.refs_2_.refs_4_.refs_5_) | copy-start | bytes 1536004
  15.4 1.2 copy-start
  16.6 1.0 copy-start.1
  17.6 0.9 copy-start.5
  18.6 61.1 %copy-start.2 = (f32[3,32768]{1,0:T(4,128)S(1)}, f32[3,32768]{1,0:T(4,128)}, u32[]{:S(2)}) copy-start(f32[3,32768]{1,0:T(4,128)} %refs_0_.3) | copy-start | bytes 1179652
  37.4 59.0 %copy-start.4 = (f32[3,32768]{1,0:T(4,128)}, f32[3,32768]{1,0:T(4,128)S(1)}, u32[]{:S(2)}) copy-start(f32[3,32768]{1,0:T(4,128)S(1)} %collective-permute-done.1.refs_3_.ahead_geo) | copy-start | bytes 1179652
  62.1 14.8 %collective-permute-start.3 = (f32[4,32768]{1,0:T(4,128)S(1)}, f32[4,32768]{1,0:T(4,128)}, u32[]{:S(2)}, u32[]{:S(2)}) collective-permute-start(f32[4,32768]{1,0:T(4,128)S(1)} %get-tuple-element.18), channel_id=1, source_target_pairs={{1,0},{2,1},{3,2},{4,3},{5,4},{6,5},{7,6},{8,7},{9,8},{10,9},{11,1... | collective-permute-start | bytes 1572872 | tf_op jit(solution)/shard_map/ppermute | solution.py:33
  64.0 14.2 %collective-permute-start.2 = (f32[4,32768]{1,0:T(4,128)S(1)}, f32[4,32768]{1,0:T(4,128)}, u32[]{:S(2)}, u32[]{:S(2)}) collective-permute-start(f32[4,32768]{1,0:T(4,128)S(1)} %get-tuple-element.19), channel_id=1, source_target_pairs={{0,1},{1,2},{2,3},{3,4},{4,5},{5,6},{6,7},{7,8},{8,9},{9,10},{10,1... | collective-permute-start | bytes 1572872 | tf_op jit(solution)/shard_map/ppermute | solution.py:33
  122.7 14.7 %collective-permute-start.5 = (f32[4,32768]{1,0:T(4,128)S(1)}, f32[4,32768]{1,0:T(4,128)S(1)}, u32[]{:S(2)}, u32[]{:S(2)}) collective-permute-start(f32[4,32768]{1,0:T(4,128)S(1)} %get-tuple-element.24), channel_id=1, source_target_pairs={{1,0},{2,1},{3,2},{4,3},{5,4},{6,5},{7,6},{8,7},{9,8},{10,9},{11,1... | collective-permute-start | bytes 1572872 | tf_op jit(solution)/shard_map/ppermute | solution.py:33
  124.6 14.0 %collective-permute-start.4 = (f32[4,32768]{1,0:T(4,128)S(1)}, f32[4,32768]{1,0:T(4,128)S(1)}, u32[]{:S(2)}, u32[]{:S(2)}) collective-permute-start(f32[4,32768]{1,0:T(4,128)S(1)} %get-tuple-element.25), channel_id=1, source_target_pairs={{0,1},{1,2},{2,3},{3,4},{4,5},{5,6},{6,7},{7,8},{8,9},{9,10},{10,1... | collective-permute-start | bytes 1572872 | tf_op jit(solution)/shard_map/ppermute | solution.py:33
  139.6 49.8 %copy-start.11 = (s32[512]{0:T(512)S(1)}, s32[512]{0:T(512)}, u32[]{:S(2)}) copy-start(s32[512]{0:T(512)} %param.17) | copy-start | bytes 6148
  139.6 49.9 %copy-start.12 = (s32[512]{0:T(512)S(1)}, s32[512]{0:T(512)}, u32[]{:S(2)}) copy-start(s32[512]{0:T(512)} %param.18) | copy-start | bytes 6148
  173.9 20.4 %copy-start.6 = (f32[3,32768]{1,0:T(4,128)}, f32[3,32768]{1,0:T(4,128)S(1)}, u32[]{:S(2)}) copy-start(f32[3,32768]{1,0:T(4,128)S(1)} %multiply_add_fusion.refs_2_) | copy-start | bytes 1179652
  173.9 14.8 %collective-permute-start.7 = (f32[3,32768]{1,0:T(4,128)S(1)}, f32[3,32768]{1,0:T(4,128)S(1)}, u32[]{:S(2)}, u32[]{:S(2)}) collective-permute-start(f32[3,32768]{1,0:T(4,128)S(1)} %multiply_add_fusion.refs_2_), channel_id=1, source_target_pairs={{1,2},{2,1},{3,4},{4,3},{5,6},{6,5},{7,8},{8,7},{9,10},{10,9},{11,... | collective-permute-start | bytes 1179656 | tf_op jit(solution)/shard_map/ppermute | solution.py:40
  180.0 14.3 %collective-permute-start.6 = (f32[3,32768]{1,0:T(4,128)S(1)}, f32[3,32768]{1,0:T(4,128)S(1)}, u32[]{:S(2)}, u32[]{:S(2)}) collective-permute-start(f32[3,32768]{1,0:T(4,128)S(1)} %multiply_add_fusion.refs_2_), channel_id=1, source_target_pairs={{0,2},{2,4},{3,1},{4,6},{5,3},{6,8},{7,5},{8,10},{9,7},{10,12},{11... | collective-permute-start | bytes 1179656 | tf_op jit(solution)/shard_map/ppermute | solution.py:40
  181.9 12.4 %collective-permute-start.8 = (f32[3,32768]{1,0:T(4,128)S(1)}, f32[3,32768]{1,0:T(4,128)S(1)}, u32[]{:S(2)}, u32[]{:S(2)}) collective-permute-start(f32[3,32768]{1,0:T(4,128)S(1)} %multiply_add_fusion.refs_2_), channel_id=1, source_target_pairs={{0,1},{1,0},{2,3},{3,2},{4,5},{5,4},{6,7},{7,6},{8,9},{9,8},{10,11... | collective-permute-start | bytes 1179656 | tf_op jit(solution)/shard_map/ppermute | solution.py:40
  188.8 5.5 %copy-start.7 = (f32[3,32768]{1,0:T(4,128)}, f32[3,32768]{1,0:T(4,128)S(1)}, u32[]{:S(2)}) copy-start(f32[3,32768]{1,0:T(4,128)S(1)} %collective-permute-done.7.refs_1_) | copy-start | bytes 1179652
  188.8 5.5 %collective-permute-start.9 = (f32[3,32768]{1,0:T(4,128)S(1)}, f32[3,32768]{1,0:T(4,128)S(1)}, u32[]{:S(2)}, u32[]{:S(2)}) collective-permute-start(f32[3,32768]{1,0:T(4,128)S(1)} %collective-permute-done.7.refs_1_), channel_id=1, source_target_pairs={{0,1},{1,0},{2,3},{3,2},{4,5},{5,4},{6,7},{7,6},{8,9},{9,8},{10,11... | collective-permute-start | bytes 1179656 | tf_op jit(solution)/shard_map/ppermute | solution.py:40
  194.3 1.0 copy-start.9
  195.3 0.8 copy-start.10
  (1 other events, 0.8 us)
Sparse Core Ops, SparseCore 0:
  10.5 34.7 all-gather.6
Sparse Core Ops, SparseCore 1:
  72.0 50.6 all-gather.8

commit v8 on v6

--- a/solution.py
+++ b/solution.py
@@ -217,52 +217,65 @@
                 copy_out(group).wait()
 
 
-def stream_loop(pairs, home, stage_ref, sems, use):
+def stream(diag_tiles, pair_tiles, pairs, stage_ref, sems):
     ring = stage_ref.shape[0]
-
-    def copy_in(at):
+    diag_pairs = DIAG_GROUPS // 2
+    total = diag_pairs + pairs
+
+    def copy_in(tiles, at, slot):
+        return pltpu.make_async_copy(tiles.at[pl.ds(2 * at, 2)], stage_ref.at[slot], sems.at[slot])
+
+    def start(at):
         slot = lax.rem(at, ring)
-        return pltpu.make_async_copy(home(2 * at, 2), stage_ref.at[slot], sems.at[slot])
+
+        @pl.when(at < diag_pairs)
+        def _():
+            copy_in(diag_tiles, at, slot).start()
+
+        @pl.when((at >= diag_pairs) & (at < total))
+        def _():
+            copy_in(pair_tiles, at - diag_pairs, slot).start()
 
     for at in range(ring - 1):
-
-        @pl.when(at < pairs)
-        def _():
-            copy_in(at).start()
-
-    def step(at, carry):
-        @pl.when(at + ring - 1 < pairs)
-        def _():
-            copy_in(at + ring - 1).start()
-
-        copy_in(at).wait()
-        slot = lax.rem(at, ring)
-        found = []
-        for k in range(0, 2 * GROUP, 2):
-            tile = k % GROUP
-            found += use(2 * at * GROUP, k, (stage_ref[slot, k // GROUP, tile], stage_ref[slot, k // GROUP, tile + 1]))
-        for out, block, value in found:
-            out[block] += value
-        return carry
-
-    lax.fori_loop(0, pairs, step, 0)
+        start(jnp.int32(at))
+
+    def loop(first, count, use):
+        def step(at, carry):
+            here = first + at
+            start(here + ring - 1)
+            slot = lax.rem(here, ring)
+            copy_in(diag_tiles, 0, slot).wait()
+            found = []
+            for k in range(0, 2 * GROUP, 2):
+                part, tile = k // GROUP, k % GROUP
+                found += use(2 * at * GROUP, k, (stage_ref[slot, part, tile], stage_ref[slot, part, tile + 1]))
+            for out, block, value in found:
+                out[block] += value
+            return carry
+
+        lax.fori_loop(0, count, step, 0)
+
+    return loop
 
 
 def pair_body(step, me, groups, diag_list, pair_list, *refs):
     row = row_ids()
     own = functools.partial(row_features, device=me[0], count=GROUP)
     if step == "diag":
-        own_vec, own_geo, table_ref, stiff_ref, own_out, diag_tiles = refs[:6]
-        vec_ref, row_sum, col_sum, stage_ref, sems, rows_ref, cols_ref, dist_ref, tile_ref = refs[6:]
+        own_vec, own_geo, table_ref, own_out, diag_tiles = refs[:5]
+        vec_ref, row_sum, col_sum, stage_ref, sems, rows_ref, cols_ref, dist_ref, tile_ref = refs[5:]
         column_rows((own_geo,), (me[0],), cols_ref)
         vector_rows((own_vec,), vec_ref, 1.0)
     elif step == "pairs":
-        own_vec, right_vec, own_geo, right_geo, table_ref, diag_ref, own_out, right_out, pair_tiles = refs[:9]
-        vec_ref, row_sum, col_sum, stage_ref, sems, rows_ref, cols_ref, dist_ref, tile_ref = refs[9:]
+        own_vec, right_vec, own_geo, right_geo, table_ref, stiff_ref, diag_ref = refs[:7]
+        own_out, right_out, pair_tiles = refs[7:10]
+        vec_ref, row_sum, col_sum, stage_ref, sems, rows_ref, cols_ref, dist_ref, tile_ref = refs[10:]
         column_rows((own_geo, right_geo), (me[0], me[0] + 1), cols_ref)
         vector_rows((own_vec, right_vec), vec_ref, 1.0)
     else:
         own_vec, right_vec, diag_tiles, pair_tiles, *outs, vec_ref, row_sum, col_sum, stage_ref, sems = refs
+        pairs = lax.div(groups[0], 2)
+        loop = stream(diag_tiles, pair_tiles, pairs, stage_ref, sems)
         vector_rows((own_vec, right_vec), vec_ref, 1.0)
     row_sum[...] = jnp.zeros_like(row_sum)
     col_sum[...] = jnp.zeros_like(col_sum)
@@ -325,8 +338,8 @@
             lax.fori_loop(0, DIAG_GROUPS, features, 0)
             loop(groups[0], pair_list, use=use_pair, keep=(stage_ref, sems, pair_home))
     else:
-        stream_loop(jnp.int32(DIAG_GROUPS // 2), diag_home, stage_ref, sems, use_diag)
-        stream_loop(lax.div(groups[0], 2), pair_home, stage_ref, sems, use_pair)
+        loop(0, DIAG_GROUPS // 2, use_diag)
+        loop(DIAG_GROUPS // 2, pairs, use_pair)
 
     def fold(value):
         return value + pltpu.roll(value, 4, 0)
@@ -341,11 +354,9 @@
             place = pl.ds(pl.multiple_of(first * TILE, 8 * TILE), 8 * TILE)
             sums = row_sum[pl.ds(first, 8)] + col_sum[pl.ds(first, 8)]
             image = jnp.concatenate([fold(sums[k])[:4] for k in range(8)], axis=1)
-            if step == "diag":
+            if step == "pairs":
                 fourth = lax.broadcasted_iota(i32, image.shape, 0) == 3
-                image = image + jnp.where(fourth, stiff_ref[:, place] - SHIFT, 0.0)
-            elif step == "pairs":
-                image = image + diag_ref[:, place]
+                image = image + diag_ref[:, place] + jnp.where(fourth, stiff_ref[:, place] - SHIFT, 0.0)
             images[0][:, place] = image
             if step != "diag":
                 sums = col_sum[pl.ds(CB + first, 8)]
@@ -529,9 +540,9 @@
         ahead = from_behind(own_part, "nodes", -1)
         return own_part + back, ahead + right_part
 
-    own_part, diag_tiles = images("diag", ctrl_disp, ctrl_points, table, stiffness[None, :])
+    own_part, diag_tiles = images("diag", ctrl_disp, ctrl_points, table)
     own_part, right_part, pair_tiles = images(
-        "pairs", ctrl_disp, beside, ctrl_points, geo[-1], table, own_part
+        "pairs", ctrl_disp, beside, ctrl_points, geo[-1], table, stiffness[None, :], own_part
     )
     tiles = (diag_tiles, pair_tiles)
     total, total_beside = exchanged(own_part, right_part)

time: 210 us -> 204 us (0.971)
  Pallas kernels: 91.9 us -> 105 us
  blocking collectives: 35.6 us -> 25.3 us
  starting transfers between devices: 48.9 us -> 40.8 us
  waiting for transfers between devices: 22.8 us -> 20.5 us
    pallas_call x4, Pallas kernels: 58.9 us -> 73 us  [pair_call(): pl.pallas_call(functools.partial(pair_body, step), out_shape=tuple((shape...]
    all_to_all x1, blocking collectives: 35.6 us -> 25.3 us  [body(): lax.all_to_all(sent, 'nodes', 0, 0, tiled=True)]
    ppermute x9, starting transfers between devices: 40.8 us -> 32.8 us  [from_behind(): return lax.ppermute(block, axis, route)]
    ppermute x9, waiting for transfers between devices: 11.8 us -> 9.57 us  [from_behind(): return lax.ppermute(block, axis, route)]
  transfers between devices with their start and end apart: 13 -> 13, of which waited for: 6 -> 5; matrix products, arithmetic and copies ran while one was open for 1% -> 1% of each run, Pallas kernels for 13% -> 15%
where the time goes in v8:
time: 204 us
  Pallas kernels  105 us (51%)
  starting transfers between devices  40.8 us (20%)
  blocking collectives  25.3 us (12%)
  waiting for transfers between devices  20.5 us (10%)
  local copies, waits for them, and re-layouts  5.48 us (3%)
  other arithmetic  3.9 us (2%)
  between operations  2.4 us (1%)
    pallas_call x4, Pallas kernels, pair_call(): pl.pallas_call(functools.partial(pair_body, step), out_shape=tuple((shape...  73 us
    ppermute x9, starting transfers between devices, from_behind(): return lax.ppermute(block, axis, route)  32.8 us
    pallas_call x1, Pallas kernels, volume_call(): pl.pallas_call(volume_body, out_shape=jax.ShapeDtypeStruct((3, VB * TILE)...  32.4 us
    all_to_all x1, blocking collectives, body(): lax.all_to_all(sent, 'nodes', 0, 0, tiled=True)  25.3 us
    ppermute x4, waiting for transfers between devices, send(): lax.ppermute(value, axis, [(i, target(i)) for i in devices if target(i) i...  11 us
    ppermute x9, waiting for transfers between devices, from_behind(): return lax.ppermute(block, axis, route)  9.57 us
    ppermute x4, starting transfers between devices, send(): lax.ppermute(value, axis, [(i, target(i)) for i in devices if target(i) i...  8.02 us
    unnamed x32, local copies, waits for them, and re-layouts  4.74 us
  transfers between devices with their start and end apart: 13, of which 5 were waited for; matrix products, arithmetic and copies ran while one was open for 1% of the time, Pallas kernels for 15%

profile of v8, /device:TPU:31, one launch (start us, length us, event | category | flops | bytes accessed | tf_op | source)
XLA Modules:
  0.0 203.8 jit_solution(9175100949544179523)
XLA Ops:
  0.6 2.6 %collective-permute-start = (f32[3,32768]{1,0:T(4,128)}, f32[3,32768]{1,0:T(4,128)S(1)}, u32[]{:S(2)}, u32[]{:S(2)}) collective-permute-start(f32[3,32768]{1,0:T(4,128)} %refs_0_.3), channel_id=1, source_target_pairs={{1,0},{2,1},{3,2},{4,3},{5,4},{6,5},{7,6},{8,7},{9,8},{10,9},{11,1... | collective-permute-start | bytes 1179656 | tf_op jit(solution)/shard_map/ppermute | solution.py:32
  3.2 2.2 %collective-permute-start.1 = (f32[3,32768]{1,0:T(4,128)}, f32[3,32768]{1,0:T(4,128)S(1)}, u32[]{:S(2)}, u32[]{:S(2)}) collective-permute-start(f32[3,32768]{1,0:T(4,128)} %refs_2_.3), channel_id=1, source_target_pairs={{1,0},{2,1},{3,2},{4,3},{5,4},{6,5},{7,6},{8,7},{9,8},{10,9},{11,1... | collective-permute-start | bytes 1179656 | tf_op jit(solution)/shard_map/ppermute | solution.py:32
  7.2 1.0 copy-done
  8.3 1.0 copy-done.3
  9.3 13.5 %pair_tiles_diag.1 = (f32[4,32768]{1,0:T(4,128)S(1)}, bf16[16,16,128,128]{3,2,1,0:T(8,128)(2,1)}) custom-call(s32[1]{0:T(128)} %bitcast.me, s32[1]{0:T(128)S(6)} %mul.371.groups, s32[256]{0:T(256)S(1)} %fusion.41.diag_list, s32[768]{0:T(1024)S(1)} %fusion.13.pair_list, f32[3,32768]{1,0:T(4,128)S(1)} %copy-done, f32[3,32768]{1,0:T(4,128)S(1)} %copy-done.3, ...), custom_call_target="tpu_custom_call" | custom-call | flops 2000000000 | bytes 100000000 | tf_op jit(solution)/shard_map/pair_tiles_diag/pallas_call | solution.py:406
  22.8 1.0 copy-done.5
  23.9 28.7 %pair_tiles_pairs.1 = (f32[4,32768]{1,0:T(4,128)S(1)}, f32[4,32768]{1,0:T(4,128)S(1)}, bf16[48,16,128,128]{3,2,1,0:T(8,128)(2,1)}) custom-call(s32[1]{0:T(128)} %bitcast.me, s32[1]{0:T(128)S(6)} %mul.371.groups, s32[256]{0:T(256)S(1)} %fusion.41.diag_list, s32[768]{0:T(1024)S(1)} %fusion.13.pair_list, f32[3,32768]{1,0:T(4,128)S(1)} %copy-done, ...), custom_call_target="tpu_custom_call" | custom-call | flops 2000000000 | bytes 100000000 | tf_op jit(solution)/shard_map/pair_tiles_pairs/pallas_call | solution.py:406
  52.6 1.9 collective-permute-start.2
  54.5 2.4 %collective-permute-start.3 = (f32[4,32768]{1,0:T(4,128)S(1)}, f32[4,32768]{1,0:T(4,128)S(1)}, u32[]{:S(2)}, u32[]{:S(2)}) collective-permute-start(f32[4,32768]{1,0:T(4,128)S(1)} %get-tuple-element.17), channel_id=1, source_target_pairs={{1,0},{2,1},{3,2},{4,3},{5,4},{6,5},{7,6},{8,7},{9,8},{10,9},{11,1... | collective-permute-start | bytes 1572872 | tf_op jit(solution)/shard_map/ppermute | solution.py:32
  56.9 3.7 %collective-permute-done.2 = f32[4,32768]{1,0:T(4,128)S(1)} collective-permute-done((f32[4,32768]{1,0:T(4,128)S(1)}, f32[4,32768]{1,0:T(4,128)S(1)}, u32[]{:S(2)}, u32[]{:S(2)}) %collective-permute-start.2) | collective-permute-done | bytes 524320 | tf_op jit(solution)/shard_map/ppermute | solution.py:32
  61.1 8.6 %collective-permute-start.4 = (f32[3,32768]{1,0:T(4,128)S(1)}, f32[3,32768]{1,0:T(4,128)S(1)}, u32[]{:S(2)}, u32[]{:S(2)}) collective-permute-start(f32[3,32768]{1,0:T(4,128)S(1)} %copy-done.3), channel_id=1, source_target_pairs={{0,1},{1,2},{2,3},{3,4},{4,5},{5,6},{6,7},{7,8},{8,9},{9,10},{10,1... | collective-permute-start | bytes 1179656 | tf_op jit(solution)/shard_map/ppermute | solution.py:32
  69.7 1.9 collective-permute-start.5
  71.6 3.4 %collective-permute-start.6 = (f32[3,32768]{1,0:T(4,128)S(1)}, f32[3,32768]{1,0:T(4,128)S(1)}, u32[]{:S(2)}, u32[]{:S(2)}) collective-permute-start(f32[3,32768]{1,0:T(4,128)S(1)} %copy-done.3), channel_id=1, source_target_pairs={{2,0},{3,1},{4,2},{5,3},{6,4},{7,5},{8,6},{9,7},{10,8},{11,9},{12,... | collective-permute-start | bytes 1179656 | tf_op jit(solution)/shard_map/ppermute | solution.py:32
  75.5 16.7 %pair_tiles_1.1 = (f32[4,32768]{1,0:T(4,128)S(1)}, f32[4,32768]{1,0:T(4,128)S(1)}) custom-call(s32[1]{0:T(128)} %bitcast.me, s32[1]{0:T(128)S(6)} %mul.371.groups, s32[256]{0:T(256)S(1)} %fusion.41.diag_list, s32[768]{0:T(1024)S(1)} %fusion.13.pair_list, f32[3,32768]{1,0:T(4,128)S(1)} %slice_add_fusion.3.refs_0_, f32[3,32768]{1,0:T(4,128)S(1)} %slice_add_fusion.2.refs_1_, ...), custom_call_target="tpu_custom_call" | custom-call | flops 2000000000 | bytes 100000000 | tf_op jit(solution)/shard_map/pair_tiles_1/pallas_call | solution.py:406
  92.3 1.9 collective-permute-start.8
  94.2 7.9 %collective-permute-start.7 = (f32[4,32768]{1,0:T(4,128)S(1)}, f32[4,32768]{1,0:T(4,128)S(1)}, u32[]{:S(2)}, u32[]{:S(2)}) collective-permute-start(f32[4,32768]{1,0:T(4,128)S(1)} %get-tuple-element.26), channel_id=1, source_target_pairs={{0,1},{1,2},{2,3},{3,4},{4,5},{5,6},{6,7},{7,8},{8,9},{9,10},{10,1... | collective-permute-start | bytes 1572872 | tf_op jit(solution)/shard_map/ppermute | solution.py:32
  102.1 4.9 %collective-permute-done.8 = f32[4,32768]{1,0:T(4,128)S(1)} collective-permute-done((f32[4,32768]{1,0:T(4,128)S(1)}, f32[4,32768]{1,0:T(4,128)S(1)}, u32[]{:S(2)}, u32[]{:S(2)}) %collective-permute-start.8) | collective-permute-done | bytes 524320 | tf_op jit(solution)/shard_map/ppermute | solution.py:32
  109.2 14.1 %pair_tiles_2.1 = f32[8,128]{1,0:T(8,128)S(1)} custom-call(s32[1]{0:T(128)} %bitcast.me, s32[1]{0:T(128)S(6)} %mul.371.groups, s32[256]{0:T(256)S(1)} %fusion.41.diag_list, s32[768]{0:T(1024)S(1)} %fusion.13.pair_list, f32[3,32768]{1,0:T(4,128)S(1)} %get-tuple-element.44.refs_0_, f32[3,32768]{1,0:T(4,128)S(1)} %fusion.1.refs_1_, ...), custom_call_target="tpu_custom_call" | custom-call | flops 2000000000 | bytes 100000000 | tf_op jit(solution)/shard_map/pair_tiles_2/pallas_call | solution.py:406
  123.6 25.3 %all_to_all.5 = f32[128,1,128]{2,1,0:T(1,128)S(1)} all-to-all(f32[128,1,128]{2,1,0:T(1,128)S(1)} %broadcast_in_dim.37), channel_id=1, replica_groups=mesh['nodes'=128] {'nodes'}, dimensions={0} | all-to-all | bytes 131072 | tf_op jit(solution)/shard_map/all_to_all | solution.py:576
  149.5 6.0 %collective-permute-start.10 = (f32[3,32768]{1,0:T(4,128)S(1)}, f32[3,32768]{1,0:T(4,128)S(1)}, u32[]{:S(2)}, u32[]{:S(2)}) collective-permute-start(f32[3,32768]{1,0:T(4,128)S(1)} %multiply_add_fusion.refs_7_), channel_id=1, source_target_pairs={{1,2},{2,1},{3,4},{4,3},{5,6},{6,5},{7,8},{8,7},{9,10},{10,9},{11,... | collective-permute-start | bytes 1179656 | tf_op jit(solution)/shard_map/ppermute | solution.py:39
  155.6 1.9 collective-permute-start.9
  157.5 6.7 %collective-permute-done.10.refs_6_ = f32[3,32768]{1,0:T(4,128)S(1)} collective-permute-done((f32[3,32768]{1,0:T(4,128)S(1)}, f32[3,32768]{1,0:T(4,128)S(1)}, u32[]{:S(2)}, u32[]{:S(2)}) %collective-permute-start.10) | collective-permute-done | bytes 393248 | tf_op jit(solution)/shard_map/ppermute | solution.py:39
  165.5 4.3 %collective-permute-done.9.refs_5_ = f32[3,32768]{1,0:T(4,128)S(1)} collective-permute-done((f32[3,32768]{1,0:T(4,128)S(1)}, f32[3,32768]{1,0:T(4,128)S(1)}, u32[]{:S(2)}, u32[]{:S(2)}) %collective-permute-start.9) | collective-permute-done | bytes 393248 | tf_op jit(solution)/shard_map/ppermute | solution.py:39
  171.4 32.4 %volume_tiles.1 = f32[3,32768]{1,0:T(4,128)} custom-call(s32[1]{0:T(128)} %bitcast.me, s32[1]{0:T(128)S(6)} %select_n.129.groups, s32[512]{0:T(512)} %or_select_fusion.vol_list, f32[3,32768]{1,0:T(4,128)} %vol_geo.1, f32[3,32768]{1,0:T(4,128)} %copy-done.10, f32[3,32768]{1,0:T(4,128)} %copy-done.9, f32[3,32768]{1,0:T(4,128)} %refs_2_.3, ...), custom_call_target="tpu_custom_call" | custom-call | flops 2000000000 | bytes 100000000 | tf_op jit(solution)/shard_map/volume_tiles/pallas_call | solution.py:458
  (67 shorter events, 7.3 us)
Async XLA Ops:
  0.6 22.2 %collective-permute-start = (f32[3,32768]{1,0:T(4,128)}, f32[3,32768]{1,0:T(4,128)S(1)}, u32[]{:S(2)}, u32[]{:S(2)}) collective-permute-start(f32[3,32768]{1,0:T(4,128)} %refs_0_.3), channel_id=1, source_target_pairs={{1,0},{2,1},{3,2},{4,3},{5,4},{6,5},{7,6},{8,7},{9,8},{10,9},{11,1... | collective-permute-start | bytes 1179656 | tf_op jit(solution)/shard_map/ppermute | solution.py:32
  3.2 19.6 %collective-permute-start.1 = (f32[3,32768]{1,0:T(4,128)}, f32[3,32768]{1,0:T(4,128)S(1)}, u32[]{:S(2)}, u32[]{:S(2)}) collective-permute-start(f32[3,32768]{1,0:T(4,128)} %refs_2_.3), channel_id=1, source_target_pairs={{1,0},{2,1},{3,2},{4,3},{5,4},{6,5},{7,6},{8,7},{9,8},{10,9},{11,1... | collective-permute-start | bytes 1179656 | tf_op jit(solution)/shard_map/ppermute | solution.py:32
  9.3 82.9 %copy-start.2 = (f32[125,8,128]{2,1,0:T(8,128)}, f32[125,8,128]{2,1,0:T(8,128)S(1)}, u32[]{:S(2)}) copy-start(f32[125,8,128]{2,1,0:T(8,128)S(1)} %broadcast_in_dim.34.refs_2_.refs_4_.refs_10_) | copy-start | bytes 1536004
  22.8 84.4 %copy-start.4 = (f32[3,32768]{1,0:T(4,128)}, f32[3,32768]{1,0:T(4,128)S(1)}, u32[]{:S(2)}) copy-start(f32[3,32768]{1,0:T(4,128)S(1)} %collective-permute-done.1.refs_3_) | copy-start | bytes 1179652
  23.9 84.3 %copy-start.1 = (f32[3,32768]{1,0:T(4,128)S(1)}, f32[3,32768]{1,0:T(4,128)}, u32[]{:S(2)}) copy-start(f32[3,32768]{1,0:T(4,128)} %refs_0_.3) | copy-start | bytes 1179652
  52.6 8.0 %collective-permute-start.2 = (f32[4,32768]{1,0:T(4,128)S(1)}, f32[4,32768]{1,0:T(4,128)S(1)}, u32[]{:S(2)}, u32[]{:S(2)}) collective-permute-start(f32[4,32768]{1,0:T(4,128)S(1)} %get-tuple-element.18), channel_id=1, source_target_pairs={{0,1},{1,2},{2,3},{3,4},{4,5},{5,6},{6,7},{7,8},{8,9},{9,10},{10,1... | collective-permute-start | bytes 1572872 | tf_op jit(solution)/shard_map/ppermute | solution.py:32
  54.5 20.5 %collective-permute-start.3 = (f32[4,32768]{1,0:T(4,128)S(1)}, f32[4,32768]{1,0:T(4,128)S(1)}, u32[]{:S(2)}, u32[]{:S(2)}) collective-permute-start(f32[4,32768]{1,0:T(4,128)S(1)} %get-tuple-element.17), channel_id=1, source_target_pairs={{1,0},{2,1},{3,2},{4,3},{5,4},{6,5},{7,6},{8,7},{9,8},{10,9},{11,1... | collective-permute-start | bytes 1572872 | tf_op jit(solution)/shard_map/ppermute | solution.py:32
  61.1 31.1 %collective-permute-start.4 = (f32[3,32768]{1,0:T(4,128)S(1)}, f32[3,32768]{1,0:T(4,128)S(1)}, u32[]{:S(2)}, u32[]{:S(2)}) collective-permute-start(f32[3,32768]{1,0:T(4,128)S(1)} %copy-done.3), channel_id=1, source_target_pairs={{0,1},{1,2},{2,3},{3,4},{4,5},{5,6},{6,7},{7,8},{8,9},{9,10},{10,1... | collective-permute-start | bytes 1179656 | tf_op jit(solution)/shard_map/ppermute | solution.py:32
  69.7 22.5 %collective-permute-start.5 = (f32[3,32768]{1,0:T(4,128)S(1)}, f32[3,32768]{1,0:T(4,128)S(1)}, u32[]{:S(2)}, u32[]{:S(2)}) collective-permute-start(f32[3,32768]{1,0:T(4,128)S(1)} %copy-done.3), channel_id=1, source_target_pairs={{0,2},{1,3},{2,4},{3,5},{4,6},{5,7},{6,8},{7,9},{8,10},{9,11},{10,... | collective-permute-start | bytes 1179656 | tf_op jit(solution)/shard_map/ppermute | solution.py:32
  71.6 20.6 %collective-permute-start.6 = (f32[3,32768]{1,0:T(4,128)S(1)}, f32[3,32768]{1,0:T(4,128)S(1)}, u32[]{:S(2)}, u32[]{:S(2)}) collective-permute-start(f32[3,32768]{1,0:T(4,128)S(1)} %copy-done.3), channel_id=1, source_target_pairs={{2,0},{3,1},{4,2},{5,3},{6,4},{7,5},{8,6},{9,7},{10,8},{11,9},{12,... | collective-permute-start | bytes 1179656 | tf_op jit(solution)/shard_map/ppermute | solution.py:32
  92.2 72.7 %copy-start.7 = (s32[512]{0:T(512)S(1)}, s32[512]{0:T(512)}, u32[]{:S(2)}) copy-start(s32[512]{0:T(512)} %param.17) | copy-start | bytes 6148
  92.2 72.7 %copy-start.8 = (s32[512]{0:T(512)S(1)}, s32[512]{0:T(512)}, u32[]{:S(2)}) copy-start(s32[512]{0:T(512)} %param.18) | copy-start | bytes 6148
  92.2 17.0 %copy-start.9 = (f32[3,32768]{1,0:T(4,128)}, f32[3,32768]{1,0:T(4,128)S(1)}, u32[]{:S(2)}) copy-start(f32[3,32768]{1,0:T(4,128)S(1)} %collective-permute-done.4.refs_1_) | copy-start | bytes 1179652
  92.2 16.9 %copy-start.10 = (f32[3,32768]{1,0:T(4,128)}, f32[3,32768]{1,0:T(4,128)S(1)}, u32[]{:S(2)}) copy-start(f32[3,32768]{1,0:T(4,128)S(1)} %collective-permute-done.5.refs_0_) | copy-start | bytes 1179652
  92.3 16.9 %copy-start.11 = (f32[3,32768]{1,0:T(4,128)}, f32[3,32768]{1,0:T(4,128)S(1)}, u32[]{:S(2)}) copy-start(f32[3,32768]{1,0:T(4,128)S(1)} %collective-permute-done.6.refs_4_) | copy-start | bytes 1179652
  92.3 14.7 %collective-permute-start.8 = (f32[4,32768]{1,0:T(4,128)S(1)}, f32[4,32768]{1,0:T(4,128)S(1)}, u32[]{:S(2)}, u32[]{:S(2)}) collective-permute-start(f32[4,32768]{1,0:T(4,128)S(1)} %get-tuple-element.25), channel_id=1, source_target_pairs={{1,0},{2,1},{3,2},{4,3},{5,4},{6,5},{7,6},{8,7},{9,8},{10,9},{11,1... | collective-permute-start | bytes 1572872 | tf_op jit(solution)/shard_map/ppermute | solution.py:32
  94.2 14.0 %collective-permute-start.7 = (f32[4,32768]{1,0:T(4,128)S(1)}, f32[4,32768]{1,0:T(4,128)S(1)}, u32[]{:S(2)}, u32[]{:S(2)}) collective-permute-start(f32[4,32768]{1,0:T(4,128)S(1)} %get-tuple-element.26), channel_id=1, source_target_pairs={{0,1},{1,2},{2,3},{3,4},{4,5},{5,6},{6,7},{7,8},{8,9},{9,10},{10,1... | collective-permute-start | bytes 1572872 | tf_op jit(solution)/shard_map/ppermute | solution.py:32
  149.5 20.4 %copy-start.6 = (f32[3,32768]{1,0:T(4,128)}, f32[3,32768]{1,0:T(4,128)S(1)}, u32[]{:S(2)}) copy-start(f32[3,32768]{1,0:T(4,128)S(1)} %multiply_add_fusion.refs_7_) | copy-start | bytes 1179652
  149.5 14.7 %collective-permute-start.10 = (f32[3,32768]{1,0:T(4,128)S(1)}, f32[3,32768]{1,0:T(4,128)S(1)}, u32[]{:S(2)}, u32[]{:S(2)}) collective-permute-start(f32[3,32768]{1,0:T(4,128)S(1)} %multiply_add_fusion.refs_7_), channel_id=1, source_target_pairs={{1,2},{2,1},{3,4},{4,3},{5,6},{6,5},{7,8},{8,7},{9,10},{10,9},{11,... | collective-permute-start | bytes 1179656 | tf_op jit(solution)/shard_map/ppermute | solution.py:39
  155.5 10.0 %collective-permute-start.11 = (f32[3,32768]{1,0:T(4,128)S(1)}, f32[3,32768]{1,0:T(4,128)S(1)}, u32[]{:S(2)}, u32[]{:S(2)}) collective-permute-start(f32[3,32768]{1,0:T(4,128)S(1)} %multiply_add_fusion.refs_7_), channel_id=1, source_target_pairs={{0,1},{1,0},{2,3},{3,2},{4,5},{5,4},{6,7},{7,6},{8,9},{9,8},{10,11... | collective-permute-start | bytes 1179656 | tf_op jit(solution)/shard_map/ppermute | solution.py:39
  155.6 14.2 %collective-permute-start.9 = (f32[3,32768]{1,0:T(4,128)S(1)}, f32[3,32768]{1,0:T(4,128)S(1)}, u32[]{:S(2)}, u32[]{:S(2)}) collective-permute-start(f32[3,32768]{1,0:T(4,128)S(1)} %multiply_add_fusion.refs_7_), channel_id=1, source_target_pairs={{0,2},{2,4},{3,1},{4,6},{5,3},{6,8},{7,5},{8,10},{9,7},{10,12},{11... | collective-permute-start | bytes 1179656 | tf_op jit(solution)/shard_map/ppermute | solution.py:39
  164.2 5.6 %copy-start.12 = (f32[3,32768]{1,0:T(4,128)}, f32[3,32768]{1,0:T(4,128)S(1)}, u32[]{:S(2)}) copy-start(f32[3,32768]{1,0:T(4,128)S(1)} %collective-permute-done.10.refs_6_) | copy-start | bytes 1179652
  164.2 5.6 %collective-permute-start.12 = (f32[3,32768]{1,0:T(4,128)S(1)}, f32[3,32768]{1,0:T(4,128)S(1)}, u32[]{:S(2)}, u32[]{:S(2)}) collective-permute-start(f32[3,32768]{1,0:T(4,128)S(1)} %collective-permute-done.10.refs_6_), channel_id=1, source_target_pairs={{0,1},{1,0},{2,3},{3,2},{4,5},{5,4},{6,7},{7,6},{8,9},{9,8},{10,11... | collective-permute-start | bytes 1179656 | tf_op jit(solution)/shard_map/ppermute | solution.py:39
  165.5 4.3 %copy-start.13 = (f32[3,32768]{1,0:T(4,128)}, f32[3,32768]{1,0:T(4,128)S(1)}, u32[]{:S(2)}) copy-start(f32[3,32768]{1,0:T(4,128)S(1)} %collective-permute-done.11.refs_8_) | copy-start | bytes 1179652
  (5 other events, 4.7 us)

commit v9 on v8

--- a/solution.py
+++ b/solution.py
@@ -16,6 +16,7 @@
 GROUP = 16
 PART = 32
 RING = 8
+CHUNK = 16
 DIAG_GROUPS = CB // GROUP
 PAIR_GROUPS = MAXT // GROUP
 SHIFT = 0.75
@@ -86,12 +87,12 @@
     return [(block - (fixed + along_z * (cell + k))) * 0.25 for k, block in enumerate(blocks)]
 
 
-def each_chunk(count, todo):
+def each_chunk(count, todo, chunk=8):
     def step(at, carry):
-        todo(8 * at)
+        todo(chunk * at)
         return carry
 
-    lax.fori_loop(0, count // 8, step, 0)
+    lax.fori_loop(0, count // chunk, step, 0)
 
 
 def column_rows(geo_refs, devices, cols_ref):
@@ -99,11 +100,11 @@
     for at, ref in enumerate(geo_refs):
 
         def fill(first):
-            local = local_coords(three_rows(ref, first, 8), first, devices[at])
+            local = local_coords(three_rows(ref, first, CHUNK), first, devices[at])
             rows = [block + pltpu.roll(block, 3, 0) + unit for block in local]
-            cols_ref[pl.ds(at * CB + first, 8)] = jnp.stack(rows)
-
-        each_chunk(CB, fill)
+            cols_ref[pl.ds(at * CB + first, CHUNK)] = jnp.stack(rows)
+
+        each_chunk(CB, fill, CHUNK)
     cols_ref[len(geo_refs) * CB] = jnp.full((8, TILE), FAR, f32)
 
 
@@ -113,16 +114,16 @@
 
         def fill(first):
             rows = []
-            for block in three_rows(ref, first, 8):
+            for block in three_rows(ref, first, CHUNK):
                 high, low = split(block)
                 rows.append(high + pltpu.roll(low, 4, 0) + unit)
-            vec_ref[pl.ds((at if places is None else places[at]) * CB + first, 8)] = jnp.stack(rows)
-
-        each_chunk(CB, fill)
+            vec_ref[pl.ds((at if places is None else places[at]) * CB + first, CHUNK)] = jnp.stack(rows)
+
+        each_chunk(CB, fill, CHUNK)
     vec_ref[len(refs) * CB] = jnp.zeros((8, TILE), f32)
 
 
-def row_features(geo_ref, device, rows_ref, first, count):
+def row_features(geo_ref, device, first, count):
     row = row_ids()
     middle = (row >= 3) & (row < 6)
 
@@ -135,13 +136,15 @@
         return [high, high, mid, last]
 
     blocks = local_coords(three_rows(geo_ref, first, count), first, device)
-    for k in range(0, count, 4):
-        parts = []
-        for j in range(4):
-            parts += features(blocks[k + j])
-        turned = jnp.transpose(jnp.concatenate(parts, axis=0).astype(bf16))
-        for j in range(4):
-            rows_ref[first + k + j] = turned if j == 0 else pltpu.roll(turned, TILE - j * PART, 1)
+    parts = [features(block) for block in blocks]
+    return [
+        jnp.transpose(jnp.concatenate(sum(parts[k : k + 4], []), axis=0).astype(bf16)) for k in range(0, count, 4)
+    ]
+
+
+def spread(turned, rows_ref, first):
+    for j in range(4):
+        rows_ref[first + j] = turned if j == 0 else pltpu.roll(turned, TILE - j * PART, 1)
 
 
 def tile_loop(groups, listed, rows_ref, cols_ref, table_ref, dist_ref, tile_ref, use, ahead=None, keep=None):
@@ -260,7 +263,11 @@
 
 def pair_body(step, me, groups, diag_list, pair_list, *refs):
     row = row_ids()
-    own = functools.partial(row_features, device=me[0], count=GROUP)
+
+    def own(geo_ref, rows_ref, first):
+        for k, turned in enumerate(row_features(geo_ref, me[0], first, GROUP)):
+            spread(turned, rows_ref, first + 4 * k)
+
     if step == "diag":
         own_vec, own_geo, table_ref, own_out, diag_tiles = refs[:5]
         vec_ref, row_sum, col_sum, stage_ref, sems, rows_ref, cols_ref, dist_ref, tile_ref = refs[5:]
@@ -424,7 +431,8 @@
     sums[...] = jnp.zeros_like(sums)
 
     def features(at, carry):
-        row_features(vol_geo, me[0], rows_ref, at * 16, 16)
+        for k, turned in enumerate(row_features(vol_geo, me[0], 16 * at, 16)):
+            spread(turned, rows_ref, 16 * at + 4 * k)
         return carry
 
     lax.fori_loop(0, VB // 16, features, 0)

time: 204 us -> 208 us (1.020)
  the two profiles are of different devices: /device:TPU:31 before, /device:TPU:32 now
where the time goes in v9:
time: 208 us; the launch traced here: 207 us
  Pallas kernels  95.5 us (46%)
  starting transfers between devices  43.4 us (21%)
  waiting for transfers between devices  30.7 us (15%)
  blocking collectives  26 us (12%)
  local copies, waits for them, and re-layouts  5.48 us (3%)
  other arithmetic  3.9 us (2%)
  between operations  2.4 us (1%)
    pallas_call x4, Pallas kernels, pair_call(): pl.pallas_call(functools.partial(pair_body, step), out_shape=tuple((shape...  64.2 us
    ppermute x9, starting transfers between devices, from_behind(): return lax.ppermute(block, axis, route)  37.7 us
    pallas_call x1, Pallas kernels, volume_call(): pl.pallas_call(volume_body, out_shape=jax.ShapeDtypeStruct((3, VB * TILE)...  31.3 us
    all_to_all x1, blocking collectives, body(): lax.all_to_all(sent, 'nodes', 0, 0, tiled=True)  26 us
    ppermute x9, waiting for transfers between devices, from_behind(): return lax.ppermute(block, axis, route)  17.5 us
    ppermute x4, waiting for transfers between devices, send(): lax.ppermute(value, axis, [(i, target(i)) for i in devices if target(i) i...  13.2 us
    ppermute x4, starting transfers between devices, send(): lax.ppermute(value, axis, [(i, target(i)) for i in devices if target(i) i...  5.78 us
    unnamed x32, local copies, waits for them, and re-layouts  4.74 us
  transfers between devices with their start and end apart: 13, of which 5 were waited for; matrix products, arithmetic and copies ran while one was open for 1% of the time, Pallas kernels for 13%

profile of v9, /device:TPU:32, one launch (start us, length us, event | category | flops | bytes accessed | tf_op | source)
XLA Modules:
  0.0 207.4 jit_solution(12091323742637690098)
XLA Ops:
  0.6 6.1 %collective-permute-start = (f32[3,32768]{1,0:T(4,128)}, f32[3,32768]{1,0:T(4,128)S(1)}, u32[]{:S(2)}, u32[]{:S(2)}) collective-permute-start(f32[3,32768]{1,0:T(4,128)} %refs_0_.3), channel_id=1, source_target_pairs={{1,0},{2,1},{3,2},{4,3},{5,4},{6,5},{7,6},{8,7},{9,8},{10,9},{11,1... | collective-permute-start | bytes 1179656 | tf_op jit(solution)/shard_map/ppermute | solution.py:33
  6.7 2.6 %collective-permute-start.1 = (f32[3,32768]{1,0:T(4,128)}, f32[3,32768]{1,0:T(4,128)S(1)}, u32[]{:S(2)}, u32[]{:S(2)}) collective-permute-start(f32[3,32768]{1,0:T(4,128)} %refs_2_.3), channel_id=1, source_target_pairs={{1,0},{2,1},{3,2},{4,3},{5,4},{6,5},{7,6},{8,7},{9,8},{10,9},{11,1... | collective-permute-start | bytes 1179656 | tf_op jit(solution)/shard_map/ppermute | solution.py:33
  12.2 1.0 copy-done.3
  13.2 13.3 %pair_tiles_diag.1 = (f32[4,32768]{1,0:T(4,128)S(1)}, bf16[16,16,128,128]{3,2,1,0:T(8,128)(2,1)}) custom-call(s32[1]{0:T(128)} %bitcast.me, s32[1]{0:T(128)S(6)} %mul.371.groups, s32[256]{0:T(256)S(1)} %fusion.41.diag_list, s32[768]{0:T(1024)S(1)} %fusion.13.pair_list, f32[3,32768]{1,0:T(4,128)S(1)} %copy-done, f32[3,32768]{1,0:T(4,128)S(1)} %copy-done.3, ...), custom_call_target="tpu_custom_call" | custom-call | flops 2000000000 | bytes 100000000 | tf_op jit(solution)/shard_map/pair_tiles_diag/pallas_call | solution.py:413
  26.6 1.0 copy-done.5
  27.6 23.9 %pair_tiles_pairs.1 = (f32[4,32768]{1,0:T(4,128)S(1)}, f32[4,32768]{1,0:T(4,128)S(1)}, bf16[48,16,128,128]{3,2,1,0:T(8,128)(2,1)}) custom-call(s32[1]{0:T(128)} %bitcast.me, s32[1]{0:T(128)S(6)} %mul.371.groups, s32[256]{0:T(256)S(1)} %fusion.41.diag_list, s32[768]{0:T(1024)S(1)} %fusion.13.pair_list, f32[3,32768]{1,0:T(4,128)S(1)} %copy-done, ...), custom_call_target="tpu_custom_call" | custom-call | flops 2000000000 | bytes 100000000 | tf_op jit(solution)/shard_map/pair_tiles_pairs/pallas_call | solution.py:413
  51.5 1.9 collective-permute-start.2
  53.4 7.9 %collective-permute-start.3 = (f32[4,32768]{1,0:T(4,128)S(1)}, f32[4,32768]{1,0:T(4,128)S(1)}, u32[]{:S(2)}, u32[]{:S(2)}) collective-permute-start(f32[4,32768]{1,0:T(4,128)S(1)} %get-tuple-element.17), channel_id=1, source_target_pairs={{1,0},{2,1},{3,2},{4,3},{5,4},{6,5},{7,6},{8,7},{9,8},{10,9},{11,1... | collective-permute-start | bytes 1572872 | tf_op jit(solution)/shard_map/ppermute | solution.py:33
  61.3 4.9 %collective-permute-done.2 = f32[4,32768]{1,0:T(4,128)S(1)} collective-permute-done((f32[4,32768]{1,0:T(4,128)S(1)}, f32[4,32768]{1,0:T(4,128)S(1)}, u32[]{:S(2)}, u32[]{:S(2)}) %collective-permute-start.2) | collective-permute-done | bytes 524320 | tf_op jit(solution)/shard_map/ppermute | solution.py:33
  66.7 1.9 collective-permute-start.4
  68.6 1.9 collective-permute-start.5
  70.5 8.1 %collective-permute-start.6 = (f32[3,32768]{1,0:T(4,128)S(1)}, f32[3,32768]{1,0:T(4,128)S(1)}, u32[]{:S(2)}, u32[]{:S(2)}) collective-permute-start(f32[3,32768]{1,0:T(4,128)S(1)} %copy-done.3), channel_id=1, source_target_pairs={{2,0},{3,1},{4,2},{5,3},{6,4},{7,5},{8,6},{9,7},{10,8},{11,9},{12,... | collective-permute-start | bytes 1179656 | tf_op jit(solution)/shard_map/ppermute | solution.py:33
  79.2 14.5 %pair_tiles_1.1 = (f32[4,32768]{1,0:T(4,128)S(1)}, f32[4,32768]{1,0:T(4,128)S(1)}) custom-call(s32[1]{0:T(128)} %bitcast.me, s32[1]{0:T(128)S(6)} %mul.371.groups, s32[256]{0:T(256)S(1)} %fusion.41.diag_list, s32[768]{0:T(1024)S(1)} %fusion.13.pair_list, f32[3,32768]{1,0:T(4,128)S(1)} %slice_add_fusion.3.refs_0_, f32[3,32768]{1,0:T(4,128)S(1)} %slice_add_fusion.2.refs_1_, ...), custom_call_target="tpu_custom_call" | custom-call | flops 2000000000 | bytes 100000000 | tf_op jit(solution)/shard_map/pair_tiles_1/pallas_call | solution.py:413
  93.8 5.3 %collective-permute-start.8 = (f32[4,32768]{1,0:T(4,128)S(1)}, f32[4,32768]{1,0:T(4,128)S(1)}, u32[]{:S(2)}, u32[]{:S(2)}) collective-permute-start(f32[4,32768]{1,0:T(4,128)S(1)} %get-tuple-element.25), channel_id=1, source_target_pairs={{1,0},{2,1},{3,2},{4,3},{5,4},{6,5},{7,6},{8,7},{9,8},{10,9},{11,1... | collective-permute-start | bytes 1572872 | tf_op jit(solution)/shard_map/ppermute | solution.py:33
  99.1 1.9 collective-permute-start.7
  101.0 4.7 %collective-permute-done.8 = f32[4,32768]{1,0:T(4,128)S(1)} collective-permute-done((f32[4,32768]{1,0:T(4,128)S(1)}, f32[4,32768]{1,0:T(4,128)S(1)}, u32[]{:S(2)}, u32[]{:S(2)}) %collective-permute-start.8) | collective-permute-done | bytes 524320 | tf_op jit(solution)/shard_map/ppermute | solution.py:33
  106.0 7.8 %collective-permute-done.7 = f32[4,32768]{1,0:T(4,128)S(1)} collective-permute-done((f32[4,32768]{1,0:T(4,128)S(1)}, f32[4,32768]{1,0:T(4,128)S(1)}, u32[]{:S(2)}, u32[]{:S(2)}) %collective-permute-start.7) | collective-permute-done | bytes 524320 | tf_op jit(solution)/shard_map/ppermute | solution.py:33
  114.9 12.5 %pair_tiles_2.1 = f32[8,128]{1,0:T(8,128)S(1)} custom-call(s32[1]{0:T(128)} %bitcast.me, s32[1]{0:T(128)S(6)} %mul.371.groups, s32[256]{0:T(256)S(1)} %fusion.41.diag_list, s32[768]{0:T(1024)S(1)} %fusion.13.pair_list, f32[3,32768]{1,0:T(4,128)S(1)} %get-tuple-element.44.refs_0_, f32[3,32768]{1,0:T(4,128)S(1)} %fusion.1.refs_1_, ...), custom_call_target="tpu_custom_call" | custom-call | flops 2000000000 | bytes 100000000 | tf_op jit(solution)/shard_map/pair_tiles_2/pallas_call | solution.py:413
  127.7 26.0 %all_to_all.5 = f32[128,1,128]{2,1,0:T(1,128)S(1)} all-to-all(f32[128,1,128]{2,1,0:T(1,128)S(1)} %broadcast_in_dim.37), channel_id=1, replica_groups=mesh['nodes'=128] {'nodes'}, dimensions={0} | all-to-all | bytes 131072 | tf_op jit(solution)/shard_map/all_to_all | solution.py:584
  154.2 3.8 %collective-permute-start.10 = (f32[3,32768]{1,0:T(4,128)S(1)}, f32[3,32768]{1,0:T(4,128)S(1)}, u32[]{:S(2)}, u32[]{:S(2)}) collective-permute-start(f32[3,32768]{1,0:T(4,128)S(1)} %multiply_add_fusion.refs_7_), channel_id=1, source_target_pairs={{1,2},{2,1},{3,4},{4,3},{5,6},{6,5},{7,8},{8,7},{9,10},{10,9},{11,... | collective-permute-start | bytes 1179656 | tf_op jit(solution)/shard_map/ppermute | solution.py:40
  158.1 1.9 collective-permute-start.9
  160.0 10.0 %collective-permute-done.10.refs_6_ = f32[3,32768]{1,0:T(4,128)S(1)} collective-permute-done((f32[3,32768]{1,0:T(4,128)S(1)}, f32[3,32768]{1,0:T(4,128)S(1)}, u32[]{:S(2)}, u32[]{:S(2)}) %collective-permute-start.10) | collective-permute-done | bytes 393248 | tf_op jit(solution)/shard_map/ppermute | solution.py:40
  171.4 3.2 %collective-permute-done.9.refs_5_ = f32[3,32768]{1,0:T(4,128)S(1)} collective-permute-done((f32[3,32768]{1,0:T(4,128)S(1)}, f32[3,32768]{1,0:T(4,128)S(1)}, u32[]{:S(2)}, u32[]{:S(2)}) %collective-permute-start.9) | collective-permute-done | bytes 393248 | tf_op jit(solution)/shard_map/ppermute | solution.py:40
  176.2 31.3 %volume_tiles.1 = f32[3,32768]{1,0:T(4,128)} custom-call(s32[1]{0:T(128)} %bitcast.me, s32[1]{0:T(128)S(6)} %select_n.129.groups, s32[512]{0:T(512)} %or_select_fusion.vol_list, f32[3,32768]{1,0:T(4,128)} %vol_geo.1, f32[3,32768]{1,0:T(4,128)} %copy-done.10, f32[3,32768]{1,0:T(4,128)} %copy-done.9, f32[3,32768]{1,0:T(4,128)} %refs_2_.3, ...), custom_call_target="tpu_custom_call" | custom-call | flops 2000000000 | bytes 100000000 | tf_op jit(solution)/shard_map/volume_tiles/pallas_call | solution.py:466
  (67 shorter events, 7.4 us)
Async XLA Ops:
  0.6 25.9 %collective-permute-start = (f32[3,32768]{1,0:T(4,128)}, f32[3,32768]{1,0:T(4,128)S(1)}, u32[]{:S(2)}, u32[]{:S(2)}) collective-permute-start(f32[3,32768]{1,0:T(4,128)} %refs_0_.3), channel_id=1, source_target_pairs={{1,0},{2,1},{3,2},{4,3},{5,4},{6,5},{7,6},{8,7},{9,8},{10,9},{11,1... | collective-permute-start | bytes 1179656 | tf_op jit(solution)/shard_map/ppermute | solution.py:33
  6.7 19.8 %collective-permute-start.1 = (f32[3,32768]{1,0:T(4,128)}, f32[3,32768]{1,0:T(4,128)S(1)}, u32[]{:S(2)}, u32[]{:S(2)}) collective-permute-start(f32[3,32768]{1,0:T(4,128)} %refs_2_.3), channel_id=1, source_target_pairs={{1,0},{2,1},{3,2},{4,3},{5,4},{6,5},{7,6},{8,7},{9,8},{10,9},{11,1... | collective-permute-start | bytes 1179656 | tf_op jit(solution)/shard_map/ppermute | solution.py:33
  13.2 80.5 %copy-start.2 = (f32[125,8,128]{2,1,0:T(8,128)}, f32[125,8,128]{2,1,0:T(8,128)S(1)}, u32[]{:S(2)}) copy-start(f32[125,8,128]{2,1,0:T(8,128)S(1)} %broadcast_in_dim.34.refs_2_.refs_4_.refs_10_) | copy-start | bytes 1536004
  26.5 79.5 %copy-start.4 = (f32[3,32768]{1,0:T(4,128)}, f32[3,32768]{1,0:T(4,128)S(1)}, u32[]{:S(2)}) copy-start(f32[3,32768]{1,0:T(4,128)S(1)} %collective-permute-done.1.refs_3_) | copy-start | bytes 1179652
  27.6 86.2 %copy-start.1 = (f32[3,32768]{1,0:T(4,128)S(1)}, f32[3,32768]{1,0:T(4,128)}, u32[]{:S(2)}) copy-start(f32[3,32768]{1,0:T(4,128)} %refs_0_.3) | copy-start | bytes 1179652
  51.5 14.7 %collective-permute-start.2 = (f32[4,32768]{1,0:T(4,128)S(1)}, f32[4,32768]{1,0:T(4,128)S(1)}, u32[]{:S(2)}, u32[]{:S(2)}) collective-permute-start(f32[4,32768]{1,0:T(4,128)S(1)} %get-tuple-element.18), channel_id=1, source_target_pairs={{0,1},{1,2},{2,3},{3,4},{4,5},{5,6},{6,7},{7,8},{8,9},{9,10},{10,1... | collective-permute-start | bytes 1572872 | tf_op jit(solution)/shard_map/ppermute | solution.py:33
  53.4 25.3 %collective-permute-start.3 = (f32[4,32768]{1,0:T(4,128)S(1)}, f32[4,32768]{1,0:T(4,128)S(1)}, u32[]{:S(2)}, u32[]{:S(2)}) collective-permute-start(f32[4,32768]{1,0:T(4,128)S(1)} %get-tuple-element.17), channel_id=1, source_target_pairs={{1,0},{2,1},{3,2},{4,3},{5,4},{6,5},{7,6},{8,7},{9,8},{10,9},{11,1... | collective-permute-start | bytes 1572872 | tf_op jit(solution)/shard_map/ppermute | solution.py:33
  66.7 27.1 %collective-permute-start.4 = (f32[3,32768]{1,0:T(4,128)S(1)}, f32[3,32768]{1,0:T(4,128)S(1)}, u32[]{:S(2)}, u32[]{:S(2)}) collective-permute-start(f32[3,32768]{1,0:T(4,128)S(1)} %copy-done.3), channel_id=1, source_target_pairs={{0,1},{1,2},{2,3},{3,4},{4,5},{5,6},{6,7},{7,8},{8,9},{9,10},{10,1... | collective-permute-start | bytes 1179656 | tf_op jit(solution)/shard_map/ppermute | solution.py:33
  68.6 25.2 %collective-permute-start.5 = (f32[3,32768]{1,0:T(4,128)S(1)}, f32[3,32768]{1,0:T(4,128)S(1)}, u32[]{:S(2)}, u32[]{:S(2)}) collective-permute-start(f32[3,32768]{1,0:T(4,128)S(1)} %copy-done.3), channel_id=1, source_target_pairs={{0,2},{1,3},{2,4},{3,5},{4,6},{5,7},{6,8},{7,9},{8,10},{9,11},{10,... | collective-permute-start | bytes 1179656 | tf_op jit(solution)/shard_map/ppermute | solution.py:33
  70.5 23.3 %collective-permute-start.6 = (f32[3,32768]{1,0:T(4,128)S(1)}, f32[3,32768]{1,0:T(4,128)S(1)}, u32[]{:S(2)}, u32[]{:S(2)}) collective-permute-start(f32[3,32768]{1,0:T(4,128)S(1)} %copy-done.3), channel_id=1, source_target_pairs={{2,0},{3,1},{4,2},{5,3},{6,4},{7,5},{8,6},{9,7},{10,8},{11,9},{12,... | collective-permute-start | bytes 1179656 | tf_op jit(solution)/shard_map/ppermute | solution.py:33
  93.7 77.0 %copy-start.7 = (s32[512]{0:T(512)S(1)}, s32[512]{0:T(512)}, u32[]{:S(2)}) copy-start(s32[512]{0:T(512)} %param.17) | copy-start | bytes 6148
  93.7 77.0 %copy-start.8 = (s32[512]{0:T(512)S(1)}, s32[512]{0:T(512)}, u32[]{:S(2)}) copy-start(s32[512]{0:T(512)} %param.18) | copy-start | bytes 6148
  93.8 21.1 %copy-start.9 = (f32[3,32768]{1,0:T(4,128)}, f32[3,32768]{1,0:T(4,128)S(1)}, u32[]{:S(2)}) copy-start(f32[3,32768]{1,0:T(4,128)S(1)} %collective-permute-done.4.refs_1_) | copy-start | bytes 1179652
  93.8 21.1 %copy-start.10 = (f32[3,32768]{1,0:T(4,128)}, f32[3,32768]{1,0:T(4,128)S(1)}, u32[]{:S(2)}) copy-start(f32[3,32768]{1,0:T(4,128)S(1)} %collective-permute-done.5.refs_0_) | copy-start | bytes 1179652
  93.8 21.1 %copy-start.11 = (f32[3,32768]{1,0:T(4,128)}, f32[3,32768]{1,0:T(4,128)S(1)}, u32[]{:S(2)}) copy-start(f32[3,32768]{1,0:T(4,128)S(1)} %collective-permute-done.6.refs_4_) | copy-start | bytes 1179652
  93.8 12.0 %collective-permute-start.8 = (f32[4,32768]{1,0:T(4,128)S(1)}, f32[4,32768]{1,0:T(4,128)S(1)}, u32[]{:S(2)}, u32[]{:S(2)}) collective-permute-start(f32[4,32768]{1,0:T(4,128)S(1)} %get-tuple-element.25), channel_id=1, source_target_pairs={{1,0},{2,1},{3,2},{4,3},{5,4},{6,5},{7,6},{8,7},{9,8},{10,9},{11,1... | collective-permute-start | bytes 1572872 | tf_op jit(solution)/shard_map/ppermute | solution.py:33
  99.1 14.7 %collective-permute-start.7 = (f32[4,32768]{1,0:T(4,128)S(1)}, f32[4,32768]{1,0:T(4,128)S(1)}, u32[]{:S(2)}, u32[]{:S(2)}) collective-permute-start(f32[4,32768]{1,0:T(4,128)S(1)} %get-tuple-element.26), channel_id=1, source_target_pairs={{0,1},{1,2},{2,3},{3,4},{4,5},{5,6},{6,7},{7,8},{8,9},{9,10},{10,1... | collective-permute-start | bytes 1572872 | tf_op jit(solution)/shard_map/ppermute | solution.py:33
  154.2 20.4 %copy-start.6 = (f32[3,32768]{1,0:T(4,128)}, f32[3,32768]{1,0:T(4,128)S(1)}, u32[]{:S(2)}) copy-start(f32[3,32768]{1,0:T(4,128)S(1)} %multiply_add_fusion.refs_7_) | copy-start | bytes 1179652
  154.2 15.8 %collective-permute-start.10 = (f32[3,32768]{1,0:T(4,128)S(1)}, f32[3,32768]{1,0:T(4,128)S(1)}, u32[]{:S(2)}, u32[]{:S(2)}) collective-permute-start(f32[3,32768]{1,0:T(4,128)S(1)} %multiply_add_fusion.refs_7_), channel_id=1, source_target_pairs={{1,2},{2,1},{3,4},{4,3},{5,6},{6,5},{7,8},{8,7},{9,10},{10,9},{11,... | collective-permute-start | bytes 1179656 | tf_op jit(solution)/shard_map/ppermute | solution.py:40
  158.0 13.4 %collective-permute-start.11 = (f32[3,32768]{1,0:T(4,128)S(1)}, f32[3,32768]{1,0:T(4,128)S(1)}, u32[]{:S(2)}, u32[]{:S(2)}) collective-permute-start(f32[3,32768]{1,0:T(4,128)S(1)} %multiply_add_fusion.refs_7_), channel_id=1, source_target_pairs={{0,1},{1,0},{2,3},{3,2},{4,5},{5,4},{6,7},{7,6},{8,9},{9,8},{10,11... | collective-permute-start | bytes 1179656 | tf_op jit(solution)/shard_map/ppermute | solution.py:40
  158.1 16.5 %collective-permute-start.9 = (f32[3,32768]{1,0:T(4,128)S(1)}, f32[3,32768]{1,0:T(4,128)S(1)}, u32[]{:S(2)}, u32[]{:S(2)}) collective-permute-start(f32[3,32768]{1,0:T(4,128)S(1)} %multiply_add_fusion.refs_7_), channel_id=1, source_target_pairs={{0,2},{2,4},{3,1},{4,6},{5,3},{6,8},{7,5},{8,10},{9,7},{10,12},{11... | collective-permute-start | bytes 1179656 | tf_op jit(solution)/shard_map/ppermute | solution.py:40
  170.0 4.5 %copy-start.12 = (f32[3,32768]{1,0:T(4,128)}, f32[3,32768]{1,0:T(4,128)S(1)}, u32[]{:S(2)}) copy-start(f32[3,32768]{1,0:T(4,128)S(1)} %collective-permute-done.10.refs_6_) | copy-start | bytes 1179652
  170.0 4.5 %collective-permute-start.12 = (f32[3,32768]{1,0:T(4,128)S(1)}, f32[3,32768]{1,0:T(4,128)S(1)}, u32[]{:S(2)}, u32[]{:S(2)}) collective-permute-start(f32[3,32768]{1,0:T(4,128)S(1)} %collective-permute-done.10.refs_6_), channel_id=1, source_target_pairs={{0,1},{1,0},{2,3},{3,2},{4,5},{5,4},{6,7},{7,6},{8,9},{9,8},{10,11... | collective-permute-start | bytes 1179656 | tf_op jit(solution)/shard_map/ppermute | solution.py:40
  171.4 3.2 %copy-start.13 = (f32[3,32768]{1,0:T(4,128)}, f32[3,32768]{1,0:T(4,128)S(1)}, u32[]{:S(2)}) copy-start(f32[3,32768]{1,0:T(4,128)S(1)} %collective-permute-done.11.refs_8_) | copy-start | bytes 1179652
  (5 other events, 4.7 us)

commit v10 on v9

--- a/solution.py
+++ b/solution.py
@@ -558,16 +558,17 @@
     first = total[:3] + diagonal * ctrl_disp
     first_beside = total_beside[:3] + diagonal_beside * beside
     later, first = lax.optimization_barrier((ctrl_points, first))
-    for offset in (1, 2, -2):
-        geo[offset] = from_behind(later, "nodes", offset)
+    geo[1] = from_behind(later, "nodes", 1)
     own_part, right_part = images(1, first, first_beside, *tiles)
-    own_part, right_part, geo[1], geo[2], geo[-2] = lax.optimization_barrier(
-        (own_part, right_part, geo[1], geo[2], geo[-2])
-    )
+    own_part, right_part, geo[1] = lax.optimization_barrier((own_part, right_part, geo[1]))
     total, total_beside = exchanged(own_part, right_part)
     second = total[:3] + diagonal * first
     second_beside = total_beside[:3] + diagonal_beside * first_beside
+    later, second = lax.optimization_barrier((ctrl_points, second))
+    for offset in (2, -2):
+        geo[offset] = from_behind(later, "nodes", offset)
     (quad,) = images(2, second, second_beside, *tiles)
+    quad, geo[2], geo[-2] = lax.optimization_barrier((quad, geo[2], geo[-2]))
     moments = jnp.concatenate(
         [
             comp_sum(ctrl_disp, ctrl_disp),

time: 208 us -> 202 us (0.971)
  the two profiles are of different devices: /device:TPU:32 before, /device:TPU:31 now
where the time goes in v10:
time: 202 us; the launch traced here: 203 us
  Pallas kernels  110 us (54%)
  starting transfers between devices  40.9 us (20%)
  waiting for transfers between devices  23.6 us (12%)
  blocking collectives  15.9 us (8%)
  local copies, waits for them, and re-layouts  5.24 us (3%)
  other arithmetic  4.08 us (2%)
  between operations  2.37 us (1%)
    pallas_call x4, Pallas kernels, pair_call(): pl.pallas_call(functools.partial(pair_body, step), out_shape=tuple((shape...  80.9 us
    ppermute x9, starting transfers between devices, from_behind(): return lax.ppermute(block, axis, route)  32.9 us
    pallas_call x1, Pallas kernels, volume_call(): pl.pallas_call(volume_body, out_shape=jax.ShapeDtypeStruct((3, VB * TILE)...  29.5 us
    all_to_all x1, blocking collectives, body(): lax.all_to_all(sent, 'nodes', 0, 0, tiled=True)  15.9 us
    ppermute x9, waiting for transfers between devices, from_behind(): return lax.ppermute(block, axis, route)  12.6 us
    ppermute x4, waiting for transfers between devices, send(): lax.ppermute(value, axis, [(i, target(i)) for i in devices if target(i) i...  11 us
    ppermute x4, starting transfers between devices, send(): lax.ppermute(value, axis, [(i, target(i)) for i in devices if target(i) i...  8.02 us
    unnamed x30, local copies, waits for them, and re-layouts  4.51 us
  transfers between devices with their start and end apart: 13, of which 6 were waited for; matrix products, arithmetic and copies ran while one was open for 2% of the time, Pallas kernels for 24%

profile of v10, /device:TPU:31, one launch (start us, length us, event | category | flops | bytes accessed | tf_op | source)
XLA Modules:
  0.0 202.5 jit_solution(8467692116284709479)
XLA Ops:
  0.6 2.6 %collective-permute-start = (f32[3,32768]{1,0:T(4,128)}, f32[3,32768]{1,0:T(4,128)S(1)}, u32[]{:S(2)}, u32[]{:S(2)}) collective-permute-start(f32[3,32768]{1,0:T(4,128)} %refs_0_.3), channel_id=1, source_target_pairs={{1,0},{2,1},{3,2},{4,3},{5,4},{6,5},{7,6},{8,7},{9,8},{10,9},{11,1... | collective-permute-start | bytes 1179656 | tf_op jit(solution)/shard_map/ppermute | solution.py:33
  3.2 2.2 %collective-permute-start.1 = (f32[3,32768]{1,0:T(4,128)}, f32[3,32768]{1,0:T(4,128)S(1)}, u32[]{:S(2)}, u32[]{:S(2)}) collective-permute-start(f32[3,32768]{1,0:T(4,128)} %refs_2_.3), channel_id=1, source_target_pairs={{1,0},{2,1},{3,2},{4,3},{5,4},{6,5},{7,6},{8,7},{9,8},{10,9},{11,1... | collective-permute-start | bytes 1179656 | tf_op jit(solution)/shard_map/ppermute | solution.py:33
  7.2 1.0 copy-done
  8.3 14.0 %pair_tiles_diag.1 = (f32[4,32768]{1,0:T(4,128)S(1)}, bf16[16,16,128,128]{3,2,1,0:T(8,128)(2,1)}) custom-call(s32[1]{0:T(128)} %bitcast.me, s32[1]{0:T(128)S(6)} %mul.371.groups, s32[256]{0:T(256)S(1)} %fusion.41.diag_list, s32[768]{0:T(1024)S(1)} %fusion.13.pair_list, f32[3,32768]{1,0:T(4,128)S(1)} %copy-done, f32[3,32768]{1,0:T(4,128)} %refs_2_.3, ...), custom_call_target="tpu_custom_call" | custom-call | flops 2000000000 | bytes 100000000 | tf_op jit(solution)/shard_map/pair_tiles_diag/pallas_call | solution.py:413
  22.3 1.0 copy-done.4
  23.3 32.2 %pair_tiles_pairs.1 = (f32[4,32768]{1,0:T(4,128)S(1)}, f32[4,32768]{1,0:T(4,128)S(1)}, bf16[48,16,128,128]{3,2,1,0:T(8,128)(2,1)}) custom-call(s32[1]{0:T(128)} %bitcast.me, s32[1]{0:T(128)S(6)} %mul.371.groups, s32[256]{0:T(256)S(1)} %fusion.41.diag_list, s32[768]{0:T(1024)S(1)} %fusion.13.pair_list, f32[3,32768]{1,0:T(4,128)S(1)} %copy-done, ...), custom_call_target="tpu_custom_call" | custom-call | flops 2000000000 | bytes 100000000 | tf_op jit(solution)/shard_map/pair_tiles_pairs/pallas_call | solution.py:413
  55.5 1.9 collective-permute-start.3
  57.4 7.9 %collective-permute-start.2 = (f32[4,32768]{1,0:T(4,128)S(1)}, f32[4,32768]{1,0:T(4,128)S(1)}, u32[]{:S(2)}, u32[]{:S(2)}) collective-permute-start(f32[4,32768]{1,0:T(4,128)S(1)} %get-tuple-element.21), channel_id=1, source_target_pairs={{0,1},{1,2},{2,3},{3,4},{4,5},{5,6},{6,7},{7,8},{8,9},{9,10},{10,1... | collective-permute-start | bytes 1572872 | tf_op jit(solution)/shard_map/ppermute | solution.py:33
  65.3 4.9 %collective-permute-done.3 = f32[4,32768]{1,0:T(4,128)S(1)} collective-permute-done((f32[4,32768]{1,0:T(4,128)S(1)}, f32[4,32768]{1,0:T(4,128)S(1)}, u32[]{:S(2)}, u32[]{:S(2)}) %collective-permute-start.3) | collective-permute-done | bytes 524320 | tf_op jit(solution)/shard_map/ppermute | solution.py:33
  71.9 8.6 %collective-permute-start.4 = (f32[3,32768]{1,0:T(4,128)}, f32[3,32768]{1,0:T(4,128)S(1)}, u32[]{:S(2)}, u32[]{:S(2)}) collective-permute-start(f32[3,32768]{1,0:T(4,128)} %refs_2_.3), channel_id=1, source_target_pairs={{0,1},{1,2},{2,3},{3,4},{4,5},{5,6},{6,7},{7,8},{8,9},{9,10},{10,1... | collective-permute-start | bytes 1179656 | tf_op jit(solution)/shard_map/ppermute | solution.py:33
  80.7 19.0 %pair_tiles_1.1 = (f32[4,32768]{1,0:T(4,128)S(1)}, f32[4,32768]{1,0:T(4,128)S(1)}) custom-call(s32[1]{0:T(128)} %bitcast.me, s32[1]{0:T(128)S(6)} %mul.371.groups, s32[256]{0:T(256)S(1)} %fusion.41.diag_list, s32[768]{0:T(1024)S(1)} %fusion.13.pair_list, f32[3,32768]{1,0:T(4,128)S(1)} %slice_add_fusion.3.refs_0_, f32[3,32768]{1,0:T(4,128)S(1)} %slice_add_fusion.2.refs_1_, ...), custom_call_target="tpu_custom_call" | custom-call | flops 2000000000 | bytes 100000000 | tf_op jit(solution)/shard_map/pair_tiles_1/pallas_call | solution.py:413
  99.8 2.1 %collective-permute-start.5 = (f32[4,32768]{1,0:T(4,128)S(1)}, f32[4,32768]{1,0:T(4,128)S(1)}, u32[]{:S(2)}, u32[]{:S(2)}) collective-permute-start(f32[4,32768]{1,0:T(4,128)S(1)} %get-tuple-element.29), channel_id=1, source_target_pairs={{0,1},{1,2},{2,3},{3,4},{4,5},{5,6},{6,7},{7,8},{8,9},{9,10},{10,1... | collective-permute-start | bytes 1572872 | tf_op jit(solution)/shard_map/ppermute | solution.py:33
  101.8 2.4 %collective-permute-start.6 = (f32[4,32768]{1,0:T(4,128)S(1)}, f32[4,32768]{1,0:T(4,128)S(1)}, u32[]{:S(2)}, u32[]{:S(2)}) collective-permute-start(f32[4,32768]{1,0:T(4,128)S(1)} %get-tuple-element.28), channel_id=1, source_target_pairs={{1,0},{2,1},{3,2},{4,3},{5,4},{6,5},{7,6},{8,7},{9,8},{10,9},{11,1... | collective-permute-start | bytes 1572872 | tf_op jit(solution)/shard_map/ppermute | solution.py:33
  104.2 3.7 %collective-permute-done.5 = f32[4,32768]{1,0:T(4,128)S(1)} collective-permute-done((f32[4,32768]{1,0:T(4,128)S(1)}, f32[4,32768]{1,0:T(4,128)S(1)}, u32[]{:S(2)}, u32[]{:S(2)}) %collective-permute-start.5) | collective-permute-done | bytes 524320 | tf_op jit(solution)/shard_map/ppermute | solution.py:33
  108.2 1.9 collective-permute-start.7
  110.1 3.4 %collective-permute-start.8 = (f32[3,32768]{1,0:T(4,128)}, f32[3,32768]{1,0:T(4,128)S(1)}, u32[]{:S(2)}, u32[]{:S(2)}) collective-permute-start(f32[3,32768]{1,0:T(4,128)} %refs_2_.3), channel_id=1, source_target_pairs={{2,0},{3,1},{4,2},{5,3},{6,4},{7,5},{8,6},{9,7},{10,8},{11,9},{12,... | collective-permute-start | bytes 1179656 | tf_op jit(solution)/shard_map/ppermute | solution.py:33
  113.5 3.0 %collective-permute-done.6 = f32[4,32768]{1,0:T(4,128)S(1)} collective-permute-done((f32[4,32768]{1,0:T(4,128)S(1)}, f32[4,32768]{1,0:T(4,128)S(1)}, u32[]{:S(2)}, u32[]{:S(2)}) %collective-permute-start.6) | collective-permute-done | bytes 524320 | tf_op jit(solution)/shard_map/ppermute | solution.py:33
  116.8 15.8 %pair_tiles_2.1 = f32[8,128]{1,0:T(8,128)S(1)} custom-call(s32[1]{0:T(128)} %bitcast.me, s32[1]{0:T(128)S(6)} %mul.371.groups, s32[256]{0:T(256)S(1)} %fusion.41.diag_list, s32[768]{0:T(1024)S(1)} %fusion.13.pair_list, f32[3,32768]{1,0:T(4,128)S(1)} %fusion.2.refs_0_, f32[3,32768]{1,0:T(4,128)S(1)} %fusion.1.refs_1_, ...), custom_call_target="tpu_custom_call" | custom-call | flops 2000000000 | bytes 100000000 | tf_op jit(solution)/shard_map/pair_tiles_2/pallas_call | solution.py:413
  134.6 15.9 %all_to_all.5 = f32[128,1,128]{2,1,0:T(1,128)S(1)} all-to-all(f32[128,1,128]{2,1,0:T(1,128)S(1)} %broadcast_in_dim.37), channel_id=1, replica_groups=mesh['nodes'=128] {'nodes'}, dimensions={0} | all-to-all | bytes 131072 | tf_op jit(solution)/shard_map/all_to_all | solution.py:585
  151.0 6.0 %collective-permute-start.10 = (f32[3,32768]{1,0:T(4,128)S(1)}, f32[3,32768]{1,0:T(4,128)S(1)}, u32[]{:S(2)}, u32[]{:S(2)}) collective-permute-start(f32[3,32768]{1,0:T(4,128)S(1)} %multiply_add_fusion.refs_7_), channel_id=1, source_target_pairs={{1,2},{2,1},{3,4},{4,3},{5,6},{6,5},{7,8},{8,7},{9,10},{10,9},{11,... | collective-permute-start | bytes 1179656 | tf_op jit(solution)/shard_map/ppermute | solution.py:40
  157.2 1.9 collective-permute-start.9
  159.1 6.7 %collective-permute-done.10.refs_6_ = f32[3,32768]{1,0:T(4,128)S(1)} collective-permute-done((f32[3,32768]{1,0:T(4,128)S(1)}, f32[3,32768]{1,0:T(4,128)S(1)}, u32[]{:S(2)}, u32[]{:S(2)}) %collective-permute-start.10) | collective-permute-done | bytes 393248 | tf_op jit(solution)/shard_map/ppermute | solution.py:40
  167.1 4.3 %collective-permute-done.9.refs_5_ = f32[3,32768]{1,0:T(4,128)S(1)} collective-permute-done((f32[3,32768]{1,0:T(4,128)S(1)}, f32[3,32768]{1,0:T(4,128)S(1)}, u32[]{:S(2)}, u32[]{:S(2)}) %collective-permute-start.9) | collective-permute-done | bytes 393248 | tf_op jit(solution)/shard_map/ppermute | solution.py:40
  173.0 29.5 %volume_tiles.1 = f32[3,32768]{1,0:T(4,128)} custom-call(s32[1]{0:T(128)} %bitcast.me, s32[1]{0:T(128)S(6)} %select_n.129.groups, s32[512]{0:T(512)} %or_select_fusion.vol_list, f32[3,32768]{1,0:T(4,128)} %vol_geo.1, f32[3,32768]{1,0:T(4,128)} %copy-done.9, f32[3,32768]{1,0:T(4,128)} %copy-done.8, f32[3,32768]{1,0:T(4,128)} %refs_2_.3, ...), custom_call_target="tpu_custom_call" | custom-call | flops 2000000000 | bytes 100000000 | tf_op jit(solution)/shard_map/volume_tiles/pallas_call | solution.py:466
  (66 shorter events, 8.2 us)
Async XLA Ops:
  0.6 21.6 %collective-permute-start = (f32[3,32768]{1,0:T(4,128)}, f32[3,32768]{1,0:T(4,128)S(1)}, u32[]{:S(2)}, u32[]{:S(2)}) collective-permute-start(f32[3,32768]{1,0:T(4,128)} %refs_0_.3), channel_id=1, source_target_pairs={{1,0},{2,1},{3,2},{4,3},{5,4},{6,5},{7,6},{8,7},{9,8},{10,9},{11,1... | collective-permute-start | bytes 1179656 | tf_op jit(solution)/shard_map/ppermute | solution.py:33
  3.2 19.1 %collective-permute-start.1 = (f32[3,32768]{1,0:T(4,128)}, f32[3,32768]{1,0:T(4,128)S(1)}, u32[]{:S(2)}, u32[]{:S(2)}) collective-permute-start(f32[3,32768]{1,0:T(4,128)} %refs_2_.3), channel_id=1, source_target_pairs={{1,0},{2,1},{3,2},{4,3},{5,4},{6,5},{7,6},{8,7},{9,8},{10,9},{11,1... | collective-permute-start | bytes 1179656 | tf_op jit(solution)/shard_map/ppermute | solution.py:33
  8.3 91.4 %copy-start.2 = (f32[125,8,128]{2,1,0:T(8,128)}, f32[125,8,128]{2,1,0:T(8,128)S(1)}, u32[]{:S(2)}) copy-start(f32[125,8,128]{2,1,0:T(8,128)S(1)} %broadcast_in_dim.34.refs_2_.refs_4_.refs_10_) | copy-start | bytes 1536004
  22.3 85.9 %copy-start.3 = (f32[3,32768]{1,0:T(4,128)}, f32[3,32768]{1,0:T(4,128)S(1)}, u32[]{:S(2)}) copy-start(f32[3,32768]{1,0:T(4,128)S(1)} %collective-permute-done.1.refs_3_) | copy-start | bytes 1179652
  22.3 1.0 copy-start.4
  55.5 14.7 %collective-permute-start.3 = (f32[4,32768]{1,0:T(4,128)S(1)}, f32[4,32768]{1,0:T(4,128)S(1)}, u32[]{:S(2)}, u32[]{:S(2)}) collective-permute-start(f32[4,32768]{1,0:T(4,128)S(1)} %get-tuple-element.20), channel_id=1, source_target_pairs={{1,0},{2,1},{3,2},{4,3},{5,4},{6,5},{7,6},{8,7},{9,8},{10,9},{11,1... | collective-permute-start | bytes 1572872 | tf_op jit(solution)/shard_map/ppermute | solution.py:33
  57.4 14.0 %collective-permute-start.2 = (f32[4,32768]{1,0:T(4,128)S(1)}, f32[4,32768]{1,0:T(4,128)S(1)}, u32[]{:S(2)}, u32[]{:S(2)}) collective-permute-start(f32[4,32768]{1,0:T(4,128)S(1)} %get-tuple-element.21), channel_id=1, source_target_pairs={{0,1},{1,2},{2,3},{3,4},{4,5},{5,6},{6,7},{7,8},{8,9},{9,10},{10,1... | collective-permute-start | bytes 1572872 | tf_op jit(solution)/shard_map/ppermute | solution.py:33
  71.9 27.8 %collective-permute-start.4 = (f32[3,32768]{1,0:T(4,128)}, f32[3,32768]{1,0:T(4,128)S(1)}, u32[]{:S(2)}, u32[]{:S(2)}) collective-permute-start(f32[3,32768]{1,0:T(4,128)} %refs_2_.3), channel_id=1, source_target_pairs={{0,1},{1,2},{2,3},{3,4},{4,5},{5,6},{6,7},{7,8},{8,9},{9,10},{10,1... | collective-permute-start | bytes 1179656 | tf_op jit(solution)/shard_map/ppermute | solution.py:33
  99.7 32.9 %copy-start.1 = (f32[3,32768]{1,0:T(4,128)S(1)}, f32[3,32768]{1,0:T(4,128)}, u32[]{:S(2)}) copy-start(f32[3,32768]{1,0:T(4,128)} %refs_0_.3) | copy-start | bytes 1179652
  99.7 66.7 %copy-start.6 = (s32[512]{0:T(512)S(1)}, s32[512]{0:T(512)}, u32[]{:S(2)}) copy-start(s32[512]{0:T(512)} %param.17) | copy-start | bytes 6148
  99.7 66.7 %copy-start.7 = (s32[512]{0:T(512)S(1)}, s32[512]{0:T(512)}, u32[]{:S(2)}) copy-start(s32[512]{0:T(512)} %param.18) | copy-start | bytes 6148
  99.8 71.6 %copy-start.8 = (f32[3,32768]{1,0:T(4,128)}, f32[3,32768]{1,0:T(4,128)S(1)}, u32[]{:S(2)}) copy-start(f32[3,32768]{1,0:T(4,128)S(1)} %collective-permute-done.4.refs_1_) | copy-start | bytes 1179652
  99.8 8.2 %collective-permute-start.5 = (f32[4,32768]{1,0:T(4,128)S(1)}, f32[4,32768]{1,0:T(4,128)S(1)}, u32[]{:S(2)}, u32[]{:S(2)}) collective-permute-start(f32[4,32768]{1,0:T(4,128)S(1)} %get-tuple-element.29), channel_id=1, source_target_pairs={{0,1},{1,2},{2,3},{3,4},{4,5},{5,6},{6,7},{7,8},{8,9},{9,10},{10,1... | collective-permute-start | bytes 1572872 | tf_op jit(solution)/shard_map/ppermute | solution.py:33
  101.8 14.7 %collective-permute-start.6 = (f32[4,32768]{1,0:T(4,128)S(1)}, f32[4,32768]{1,0:T(4,128)S(1)}, u32[]{:S(2)}, u32[]{:S(2)}) collective-permute-start(f32[4,32768]{1,0:T(4,128)S(1)} %get-tuple-element.28), channel_id=1, source_target_pairs={{1,0},{2,1},{3,2},{4,3},{5,4},{6,5},{7,6},{8,7},{9,8},{10,9},{11,1... | collective-permute-start | bytes 1572872 | tf_op jit(solution)/shard_map/ppermute | solution.py:33
  108.2 25.3 %collective-permute-start.7 = (f32[3,32768]{1,0:T(4,128)}, f32[3,32768]{1,0:T(4,128)S(1)}, u32[]{:S(2)}, u32[]{:S(2)}) collective-permute-start(f32[3,32768]{1,0:T(4,128)} %refs_2_.3), channel_id=1, source_target_pairs={{0,2},{1,3},{2,4},{3,5},{4,6},{5,7},{6,8},{7,9},{8,10},{9,11},{10,... | collective-permute-start | bytes 1179656 | tf_op jit(solution)/shard_map/ppermute | solution.py:33
  110.1 24.2 %collective-permute-start.8 = (f32[3,32768]{1,0:T(4,128)}, f32[3,32768]{1,0:T(4,128)S(1)}, u32[]{:S(2)}, u32[]{:S(2)}) collective-permute-start(f32[3,32768]{1,0:T(4,128)} %refs_2_.3), channel_id=1, source_target_pairs={{2,0},{3,1},{4,2},{5,3},{6,4},{7,5},{8,6},{9,7},{10,8},{11,9},{12,... | collective-permute-start | bytes 1179656 | tf_op jit(solution)/shard_map/ppermute | solution.py:33
  134.3 37.1 %copy-start.10 = (f32[3,32768]{1,0:T(4,128)}, f32[3,32768]{1,0:T(4,128)S(1)}, u32[]{:S(2)}) copy-start(f32[3,32768]{1,0:T(4,128)S(1)} %collective-permute-done.8.refs_4_) | copy-start | bytes 1179652
  151.0 20.4 %copy-start.5 = (f32[3,32768]{1,0:T(4,128)}, f32[3,32768]{1,0:T(4,128)S(1)}, u32[]{:S(2)}) copy-start(f32[3,32768]{1,0:T(4,128)S(1)} %multiply_add_fusion.refs_7_) | copy-start | bytes 1179652
  151.0 14.7 %collective-permute-start.10 = (f32[3,32768]{1,0:T(4,128)S(1)}, f32[3,32768]{1,0:T(4,128)S(1)}, u32[]{:S(2)}, u32[]{:S(2)}) collective-permute-start(f32[3,32768]{1,0:T(4,128)S(1)} %multiply_add_fusion.refs_7_), channel_id=1, source_target_pairs={{1,2},{2,1},{3,4},{4,3},{5,6},{6,5},{7,8},{8,7},{9,10},{10,9},{11,... | collective-permute-start | bytes 1179656 | tf_op jit(solution)/shard_map/ppermute | solution.py:40
  157.1 10.0 %collective-permute-start.11 = (f32[3,32768]{1,0:T(4,128)S(1)}, f32[3,32768]{1,0:T(4,128)S(1)}, u32[]{:S(2)}, u32[]{:S(2)}) collective-permute-start(f32[3,32768]{1,0:T(4,128)S(1)} %multiply_add_fusion.refs_7_), channel_id=1, source_target_pairs={{0,1},{1,0},{2,3},{3,2},{4,5},{5,4},{6,7},{7,6},{8,9},{9,8},{10,11... | collective-permute-start | bytes 1179656 | tf_op jit(solution)/shard_map/ppermute | solution.py:40
  157.2 14.2 %collective-permute-start.9 = (f32[3,32768]{1,0:T(4,128)S(1)}, f32[3,32768]{1,0:T(4,128)S(1)}, u32[]{:S(2)}, u32[]{:S(2)}) collective-permute-start(f32[3,32768]{1,0:T(4,128)S(1)} %multiply_add_fusion.refs_7_), channel_id=1, source_target_pairs={{0,2},{2,4},{3,1},{4,6},{5,3},{6,8},{7,5},{8,10},{9,7},{10,12},{11... | collective-permute-start | bytes 1179656 | tf_op jit(solution)/shard_map/ppermute | solution.py:40
  165.8 5.6 %copy-start.11 = (f32[3,32768]{1,0:T(4,128)}, f32[3,32768]{1,0:T(4,128)S(1)}, u32[]{:S(2)}) copy-start(f32[3,32768]{1,0:T(4,128)S(1)} %collective-permute-done.10.refs_6_) | copy-start | bytes 1179652
  165.8 5.6 %collective-permute-start.12 = (f32[3,32768]{1,0:T(4,128)S(1)}, f32[3,32768]{1,0:T(4,128)S(1)}, u32[]{:S(2)}, u32[]{:S(2)}) collective-permute-start(f32[3,32768]{1,0:T(4,128)S(1)} %collective-permute-done.10.refs_6_), channel_id=1, source_target_pairs={{0,1},{1,0},{2,3},{3,2},{4,5},{5,4},{6,7},{7,6},{8,9},{9,8},{10,11... | collective-permute-start | bytes 1179656 | tf_op jit(solution)/shard_map/ppermute | solution.py:40
  167.1 4.3 %copy-start.12 = (f32[3,32768]{1,0:T(4,128)}, f32[3,32768]{1,0:T(4,128)S(1)}, u32[]{:S(2)}) copy-start(f32[3,32768]{1,0:T(4,128)S(1)} %collective-permute-done.11.refs_8_) | copy-start | bytes 1179652
  (4 other events, 3.5 us)

commit v11 on v9

--- a/solution.py
+++ b/solution.py
@@ -114,12 +114,12 @@
 
         def fill(first):
             rows = []
-            for block in three_rows(ref, first, CHUNK):
+            for block in three_rows(ref, first, 2 * CHUNK):
                 high, low = split(block)
                 rows.append(high + pltpu.roll(low, 4, 0) + unit)
-            vec_ref[pl.ds((at if places is None else places[at]) * CB + first, CHUNK)] = jnp.stack(rows)
-
-        each_chunk(CB, fill, CHUNK)
+            vec_ref[pl.ds((at if places is None else places[at]) * CB + first, 2 * CHUNK)] = jnp.stack(rows)
+
+        each_chunk(CB, fill, 2 * CHUNK)
     vec_ref[len(refs) * CB] = jnp.zeros((8, TILE), f32)
 
 

time: 208 us -> 206 us (level)
  Pallas kernels: 95.5 us -> 111 us
  blocking collectives: 26 us -> 11.9 us
  starting transfers between devices: 43.4 us -> 40.6 us
    pallas_call x4, Pallas kernels: 64.2 us -> 79.5 us  [pair_call(): pl.pallas_call(functools.partial(pair_body, step), out_shape=tuple((shape...]
    all_to_all x1, blocking collectives: 26 us -> 11.9 us  [body(): lax.all_to_all(sent, 'nodes', 0, 0, tiled=True)]
    ppermute x9, starting transfers between devices: 37.7 us -> 34.8 us  [from_behind(): return lax.ppermute(block, axis, route)]
  transfers between devices with their start and end apart: 13 -> 13, of which waited for: 5 -> 5; matrix products, arithmetic and copies ran while one was open for 1% -> 1% of each run, Pallas kernels for 13% -> 16%
where the time goes in v11:
time: 206 us; the launch traced here: 205 us
  Pallas kernels  111 us (54%)
  starting transfers between devices  40.6 us (20%)
  waiting for transfers between devices  30.2 us (15%)
  blocking collectives  11.9 us (6%)
  local copies, waits for them, and re-layouts  5.48 us (3%)
  other arithmetic  3.9 us (2%)
  between operations  2.4 us (1%)
    pallas_call x4, Pallas kernels, pair_call(): pl.pallas_call(functools.partial(pair_body, step), out_shape=tuple((shape...  79.5 us
    ppermute x9, starting transfers between devices, from_behind(): return lax.ppermute(block, axis, route)  34.8 us
    pallas_call x1, Pallas kernels, volume_call(): pl.pallas_call(volume_body, out_shape=jax.ShapeDtypeStruct((3, VB * TILE)...  31 us
    ppermute x9, waiting for transfers between devices, from_behind(): return lax.ppermute(block, axis, route)  17 us
    ppermute x4, waiting for transfers between devices, send(): lax.ppermute(value, axis, [(i, target(i)) for i in devices if target(i) i...  13.2 us
    all_to_all x1, blocking collectives, body(): lax.all_to_all(sent, 'nodes', 0, 0, tiled=True)  11.9 us
    ppermute x4, starting transfers between devices, send(): lax.ppermute(value, axis, [(i, target(i)) for i in devices if target(i) i...  5.78 us
    unnamed x32, local copies, waits for them, and re-layouts  4.74 us
  transfers between devices with their start and end apart: 13, of which 5 were waited for; matrix products, arithmetic and copies ran while one was open for 1% of the time, Pallas kernels for 16%

profile of v11, /device:TPU:32, one launch (start us, length us, event | category | flops | bytes accessed | tf_op | source)
XLA Modules:
  0.0 205.0 jit_solution(18402014607238810640)
XLA Ops:
  0.6 6.1 %collective-permute-start = (f32[3,32768]{1,0:T(4,128)}, f32[3,32768]{1,0:T(4,128)S(1)}, u32[]{:S(2)}, u32[]{:S(2)}) collective-permute-start(f32[3,32768]{1,0:T(4,128)} %refs_0_.3), channel_id=1, source_target_pairs={{1,0},{2,1},{3,2},{4,3},{5,4},{6,5},{7,6},{8,7},{9,8},{10,9},{11,1... | collective-permute-start | bytes 1179656 | tf_op jit(solution)/shard_map/ppermute | solution.py:33
  6.7 2.6 %collective-permute-start.1 = (f32[3,32768]{1,0:T(4,128)}, f32[3,32768]{1,0:T(4,128)S(1)}, u32[]{:S(2)}, u32[]{:S(2)}) collective-permute-start(f32[3,32768]{1,0:T(4,128)} %refs_2_.3), channel_id=1, source_target_pairs={{1,0},{2,1},{3,2},{4,3},{5,4},{6,5},{7,6},{8,7},{9,8},{10,9},{11,1... | collective-permute-start | bytes 1179656 | tf_op jit(solution)/shard_map/ppermute | solution.py:33
  12.2 1.0 copy-done.3
  13.2 13.2 %pair_tiles_diag.1 = (f32[4,32768]{1,0:T(4,128)S(1)}, bf16[16,16,128,128]{3,2,1,0:T(8,128)(2,1)}) custom-call(s32[1]{0:T(128)} %bitcast.me, s32[1]{0:T(128)S(6)} %mul.371.groups, s32[256]{0:T(256)S(1)} %fusion.41.diag_list, s32[768]{0:T(1024)S(1)} %fusion.13.pair_list, f32[3,32768]{1,0:T(4,128)S(1)} %copy-done, f32[3,32768]{1,0:T(4,128)S(1)} %copy-done.3, ...), custom_call_target="tpu_custom_call" | custom-call | flops 2000000000 | bytes 100000000 | tf_op jit(solution)/shard_map/pair_tiles_diag/pallas_call | solution.py:413
  26.5 1.0 copy-done.5
  27.5 31.6 %pair_tiles_pairs.1 = (f32[4,32768]{1,0:T(4,128)S(1)}, f32[4,32768]{1,0:T(4,128)S(1)}, bf16[48,16,128,128]{3,2,1,0:T(8,128)(2,1)}) custom-call(s32[1]{0:T(128)} %bitcast.me, s32[1]{0:T(128)S(6)} %mul.371.groups, s32[256]{0:T(256)S(1)} %fusion.41.diag_list, s32[768]{0:T(1024)S(1)} %fusion.13.pair_list, f32[3,32768]{1,0:T(4,128)S(1)} %copy-done, ...), custom_call_target="tpu_custom_call" | custom-call | flops 2000000000 | bytes 100000000 | tf_op jit(solution)/shard_map/pair_tiles_pairs/pallas_call | solution.py:413
  59.1 1.9 collective-permute-start.2
  61.0 7.9 %collective-permute-start.3 = (f32[4,32768]{1,0:T(4,128)S(1)}, f32[4,32768]{1,0:T(4,128)S(1)}, u32[]{:S(2)}, u32[]{:S(2)}) collective-permute-start(f32[4,32768]{1,0:T(4,128)S(1)} %get-tuple-element.17), channel_id=1, source_target_pairs={{1,0},{2,1},{3,2},{4,3},{5,4},{6,5},{7,6},{8,7},{9,8},{10,9},{11,1... | collective-permute-start | bytes 1572872 | tf_op jit(solution)/shard_map/ppermute | solution.py:33
  68.9 4.9 %collective-permute-done.2 = f32[4,32768]{1,0:T(4,128)S(1)} collective-permute-done((f32[4,32768]{1,0:T(4,128)S(1)}, f32[4,32768]{1,0:T(4,128)S(1)}, u32[]{:S(2)}, u32[]{:S(2)}) %collective-permute-start.2) | collective-permute-done | bytes 524320 | tf_op jit(solution)/shard_map/ppermute | solution.py:33
  74.3 1.9 collective-permute-start.4
  76.2 1.9 collective-permute-start.5
  78.2 8.1 %collective-permute-start.6 = (f32[3,32768]{1,0:T(4,128)S(1)}, f32[3,32768]{1,0:T(4,128)S(1)}, u32[]{:S(2)}, u32[]{:S(2)}) collective-permute-start(f32[3,32768]{1,0:T(4,128)S(1)} %copy-done.3), channel_id=1, source_target_pairs={{2,0},{3,1},{4,2},{5,3},{6,4},{7,5},{8,6},{9,7},{10,8},{11,9},{12,... | collective-permute-start | bytes 1179656 | tf_op jit(solution)/shard_map/ppermute | solution.py:33
  86.8 19.0 %pair_tiles_1.1 = (f32[4,32768]{1,0:T(4,128)S(1)}, f32[4,32768]{1,0:T(4,128)S(1)}) custom-call(s32[1]{0:T(128)} %bitcast.me, s32[1]{0:T(128)S(6)} %mul.371.groups, s32[256]{0:T(256)S(1)} %fusion.41.diag_list, s32[768]{0:T(1024)S(1)} %fusion.13.pair_list, f32[3,32768]{1,0:T(4,128)S(1)} %slice_add_fusion.3.refs_0_, f32[3,32768]{1,0:T(4,128)S(1)} %slice_add_fusion.2.refs_1_, ...), custom_call_target="tpu_custom_call" | custom-call | flops 2000000000 | bytes 100000000 | tf_op jit(solution)/shard_map/pair_tiles_1/pallas_call | solution.py:413
  105.9 1.9 collective-permute-start.8
  107.8 2.4 %collective-permute-start.7 = (f32[4,32768]{1,0:T(4,128)S(1)}, f32[4,32768]{1,0:T(4,128)S(1)}, u32[]{:S(2)}, u32[]{:S(2)}) collective-permute-start(f32[4,32768]{1,0:T(4,128)S(1)} %get-tuple-element.26), channel_id=1, source_target_pairs={{0,1},{1,2},{2,3},{3,4},{4,5},{5,6},{6,7},{7,8},{8,9},{9,10},{10,1... | collective-permute-start | bytes 1572872 | tf_op jit(solution)/shard_map/ppermute | solution.py:33
  110.2 4.3 %collective-permute-done.8 = f32[4,32768]{1,0:T(4,128)S(1)} collective-permute-done((f32[4,32768]{1,0:T(4,128)S(1)}, f32[4,32768]{1,0:T(4,128)S(1)}, u32[]{:S(2)}, u32[]{:S(2)}) %collective-permute-start.8) | collective-permute-done | bytes 524320 | tf_op jit(solution)/shard_map/ppermute | solution.py:33
  114.7 7.8 %collective-permute-done.7 = f32[4,32768]{1,0:T(4,128)S(1)} collective-permute-done((f32[4,32768]{1,0:T(4,128)S(1)}, f32[4,32768]{1,0:T(4,128)S(1)}, u32[]{:S(2)}, u32[]{:S(2)}) %collective-permute-start.7) | collective-permute-done | bytes 524320 | tf_op jit(solution)/shard_map/ppermute | solution.py:33
  123.6 15.8 %pair_tiles_2.1 = f32[8,128]{1,0:T(8,128)S(1)} custom-call(s32[1]{0:T(128)} %bitcast.me, s32[1]{0:T(128)S(6)} %mul.371.groups, s32[256]{0:T(256)S(1)} %fusion.41.diag_list, s32[768]{0:T(1024)S(1)} %fusion.13.pair_list, f32[3,32768]{1,0:T(4,128)S(1)} %get-tuple-element.44.refs_0_, f32[3,32768]{1,0:T(4,128)S(1)} %fusion.1.refs_1_, ...), custom_call_target="tpu_custom_call" | custom-call | flops 2000000000 | bytes 100000000 | tf_op jit(solution)/shard_map/pair_tiles_2/pallas_call | solution.py:413
  139.6 11.9 %all_to_all.5 = f32[128,1,128]{2,1,0:T(1,128)S(1)} all-to-all(f32[128,1,128]{2,1,0:T(1,128)S(1)} %broadcast_in_dim.37), channel_id=1, replica_groups=mesh['nodes'=128] {'nodes'}, dimensions={0} | all-to-all | bytes 131072 | tf_op jit(solution)/shard_map/all_to_all | solution.py:584
  152.1 3.8 %collective-permute-start.10 = (f32[3,32768]{1,0:T(4,128)S(1)}, f32[3,32768]{1,0:T(4,128)S(1)}, u32[]{:S(2)}, u32[]{:S(2)}) collective-permute-start(f32[3,32768]{1,0:T(4,128)S(1)} %multiply_add_fusion.refs_7_), channel_id=1, source_target_pairs={{1,2},{2,1},{3,4},{4,3},{5,6},{6,5},{7,8},{8,7},{9,10},{10,9},{11,... | collective-permute-start | bytes 1179656 | tf_op jit(solution)/shard_map/ppermute | solution.py:40
  155.9 1.9 collective-permute-start.9
  157.9 10.0 %collective-permute-done.10.refs_6_ = f32[3,32768]{1,0:T(4,128)S(1)} collective-permute-done((f32[3,32768]{1,0:T(4,128)S(1)}, f32[3,32768]{1,0:T(4,128)S(1)}, u32[]{:S(2)}, u32[]{:S(2)}) %collective-permute-start.10) | collective-permute-done | bytes 393248 | tf_op jit(solution)/shard_map/ppermute | solution.py:40
  169.2 3.2 %collective-permute-done.9.refs_5_ = f32[3,32768]{1,0:T(4,128)S(1)} collective-permute-done((f32[3,32768]{1,0:T(4,128)S(1)}, f32[3,32768]{1,0:T(4,128)S(1)}, u32[]{:S(2)}, u32[]{:S(2)}) %collective-permute-start.9) | collective-permute-done | bytes 393248 | tf_op jit(solution)/shard_map/ppermute | solution.py:40
  174.0 31.0 %volume_tiles.1 = f32[3,32768]{1,0:T(4,128)} custom-call(s32[1]{0:T(128)} %bitcast.me, s32[1]{0:T(128)S(6)} %select_n.129.groups, s32[512]{0:T(512)} %or_select_fusion.vol_list, f32[3,32768]{1,0:T(4,128)} %vol_geo.1, f32[3,32768]{1,0:T(4,128)} %copy-done.10, f32[3,32768]{1,0:T(4,128)} %copy-done.9, f32[3,32768]{1,0:T(4,128)} %refs_2_.3, ...), custom_call_target="tpu_custom_call" | custom-call | flops 2000000000 | bytes 100000000 | tf_op jit(solution)/shard_map/volume_tiles/pallas_call | solution.py:466
  (67 shorter events, 7.4 us)
Async XLA Ops:
  0.6 25.8 %collective-permute-start = (f32[3,32768]{1,0:T(4,128)}, f32[3,32768]{1,0:T(4,128)S(1)}, u32[]{:S(2)}, u32[]{:S(2)}) collective-permute-start(f32[3,32768]{1,0:T(4,128)} %refs_0_.3), channel_id=1, source_target_pairs={{1,0},{2,1},{3,2},{4,3},{5,4},{6,5},{7,6},{8,7},{9,8},{10,9},{11,1... | collective-permute-start | bytes 1179656 | tf_op jit(solution)/shard_map/ppermute | solution.py:33
  6.7 19.7 %collective-permute-start.1 = (f32[3,32768]{1,0:T(4,128)}, f32[3,32768]{1,0:T(4,128)S(1)}, u32[]{:S(2)}, u32[]{:S(2)}) collective-permute-start(f32[3,32768]{1,0:T(4,128)} %refs_2_.3), channel_id=1, source_target_pairs={{1,0},{2,1},{3,2},{4,3},{5,4},{6,5},{7,6},{8,7},{9,8},{10,9},{11,1... | collective-permute-start | bytes 1179656 | tf_op jit(solution)/shard_map/ppermute | solution.py:33
  13.2 92.5 %copy-start.2 = (f32[125,8,128]{2,1,0:T(8,128)}, f32[125,8,128]{2,1,0:T(8,128)S(1)}, u32[]{:S(2)}) copy-start(f32[125,8,128]{2,1,0:T(8,128)S(1)} %broadcast_in_dim.34.refs_2_.refs_4_.refs_10_) | copy-start | bytes 1536004
  26.5 88.2 %copy-start.4 = (f32[3,32768]{1,0:T(4,128)}, f32[3,32768]{1,0:T(4,128)S(1)}, u32[]{:S(2)}) copy-start(f32[3,32768]{1,0:T(4,128)S(1)} %collective-permute-done.1.refs_3_) | copy-start | bytes 1179652
  27.5 95.0 %copy-start.1 = (f32[3,32768]{1,0:T(4,128)S(1)}, f32[3,32768]{1,0:T(4,128)}, u32[]{:S(2)}) copy-start(f32[3,32768]{1,0:T(4,128)} %refs_0_.3) | copy-start | bytes 1179652
  59.1 14.7 %collective-permute-start.2 = (f32[4,32768]{1,0:T(4,128)S(1)}, f32[4,32768]{1,0:T(4,128)S(1)}, u32[]{:S(2)}, u32[]{:S(2)}) collective-permute-start(f32[4,32768]{1,0:T(4,128)S(1)} %get-tuple-element.18), channel_id=1, source_target_pairs={{0,1},{1,2},{2,3},{3,4},{4,5},{5,6},{6,7},{7,8},{8,9},{9,10},{10,1... | collective-permute-start | bytes 1572872 | tf_op jit(solution)/shard_map/ppermute | solution.py:33
  61.0 25.3 %collective-permute-start.3 = (f32[4,32768]{1,0:T(4,128)S(1)}, f32[4,32768]{1,0:T(4,128)S(1)}, u32[]{:S(2)}, u32[]{:S(2)}) collective-permute-start(f32[4,32768]{1,0:T(4,128)S(1)} %get-tuple-element.17), channel_id=1, source_target_pairs={{1,0},{2,1},{3,2},{4,3},{5,4},{6,5},{7,6},{8,7},{9,8},{10,9},{11,1... | collective-permute-start | bytes 1572872 | tf_op jit(solution)/shard_map/ppermute | solution.py:33
  74.3 31.5 %collective-permute-start.4 = (f32[3,32768]{1,0:T(4,128)S(1)}, f32[3,32768]{1,0:T(4,128)S(1)}, u32[]{:S(2)}, u32[]{:S(2)}) collective-permute-start(f32[3,32768]{1,0:T(4,128)S(1)} %copy-done.3), channel_id=1, source_target_pairs={{0,1},{1,2},{2,3},{3,4},{4,5},{5,6},{6,7},{7,8},{8,9},{9,10},{10,1... | collective-permute-start | bytes 1179656 | tf_op jit(solution)/shard_map/ppermute | solution.py:33
  76.2 29.6 %collective-permute-start.5 = (f32[3,32768]{1,0:T(4,128)S(1)}, f32[3,32768]{1,0:T(4,128)S(1)}, u32[]{:S(2)}, u32[]{:S(2)}) collective-permute-start(f32[3,32768]{1,0:T(4,128)S(1)} %copy-done.3), channel_id=1, source_target_pairs={{0,2},{1,3},{2,4},{3,5},{4,6},{5,7},{6,8},{7,9},{8,10},{9,11},{10,... | collective-permute-start | bytes 1179656 | tf_op jit(solution)/shard_map/ppermute | solution.py:33
  78.2 27.7 %collective-permute-start.6 = (f32[3,32768]{1,0:T(4,128)S(1)}, f32[3,32768]{1,0:T(4,128)S(1)}, u32[]{:S(2)}, u32[]{:S(2)}) collective-permute-start(f32[3,32768]{1,0:T(4,128)S(1)} %copy-done.3), channel_id=1, source_target_pairs={{2,0},{3,1},{4,2},{5,3},{6,4},{7,5},{8,6},{9,7},{10,8},{11,9},{12,... | collective-permute-start | bytes 1179656 | tf_op jit(solution)/shard_map/ppermute | solution.py:33
  105.8 62.8 %copy-start.7 = (s32[512]{0:T(512)S(1)}, s32[512]{0:T(512)}, u32[]{:S(2)}) copy-start(s32[512]{0:T(512)} %param.17) | copy-start | bytes 6148
  105.8 62.8 %copy-start.8 = (s32[512]{0:T(512)S(1)}, s32[512]{0:T(512)}, u32[]{:S(2)}) copy-start(s32[512]{0:T(512)} %param.18) | copy-start | bytes 6148
  105.8 17.7 %copy-start.9 = (f32[3,32768]{1,0:T(4,128)}, f32[3,32768]{1,0:T(4,128)S(1)}, u32[]{:S(2)}) copy-start(f32[3,32768]{1,0:T(4,128)S(1)} %collective-permute-done.4.refs_1_) | copy-start | bytes 1179652
  105.8 17.7 %copy-start.10 = (f32[3,32768]{1,0:T(4,128)}, f32[3,32768]{1,0:T(4,128)S(1)}, u32[]{:S(2)}) copy-start(f32[3,32768]{1,0:T(4,128)S(1)} %collective-permute-done.5.refs_0_) | copy-start | bytes 1179652
  105.9 17.7 %copy-start.11 = (f32[3,32768]{1,0:T(4,128)}, f32[3,32768]{1,0:T(4,128)S(1)}, u32[]{:S(2)}) copy-start(f32[3,32768]{1,0:T(4,128)S(1)} %collective-permute-done.6.refs_4_) | copy-start | bytes 1179652
  105.9 8.6 %collective-permute-start.8 = (f32[4,32768]{1,0:T(4,128)S(1)}, f32[4,32768]{1,0:T(4,128)S(1)}, u32[]{:S(2)}, u32[]{:S(2)}) collective-permute-start(f32[4,32768]{1,0:T(4,128)S(1)} %get-tuple-element.25), channel_id=1, source_target_pairs={{1,0},{2,1},{3,2},{4,3},{5,4},{6,5},{7,6},{8,7},{9,8},{10,9},{11,1... | collective-permute-start | bytes 1572872 | tf_op jit(solution)/shard_map/ppermute | solution.py:33
  107.8 14.7 %collective-permute-start.7 = (f32[4,32768]{1,0:T(4,128)S(1)}, f32[4,32768]{1,0:T(4,128)S(1)}, u32[]{:S(2)}, u32[]{:S(2)}) collective-permute-start(f32[4,32768]{1,0:T(4,128)S(1)} %get-tuple-element.26), channel_id=1, source_target_pairs={{0,1},{1,2},{2,3},{3,4},{4,5},{5,6},{6,7},{7,8},{8,9},{9,10},{10,1... | collective-permute-start | bytes 1572872 | tf_op jit(solution)/shard_map/ppermute | solution.py:33
  152.1 20.4 %copy-start.6 = (f32[3,32768]{1,0:T(4,128)}, f32[3,32768]{1,0:T(4,128)S(1)}, u32[]{:S(2)}) copy-start(f32[3,32768]{1,0:T(4,128)S(1)} %multiply_add_fusion.refs_7_) | copy-start | bytes 1179652
  152.1 15.8 %collective-permute-start.10 = (f32[3,32768]{1,0:T(4,128)S(1)}, f32[3,32768]{1,0:T(4,128)S(1)}, u32[]{:S(2)}, u32[]{:S(2)}) collective-permute-start(f32[3,32768]{1,0:T(4,128)S(1)} %multiply_add_fusion.refs_7_), channel_id=1, source_target_pairs={{1,2},{2,1},{3,4},{4,3},{5,6},{6,5},{7,8},{8,7},{9,10},{10,9},{11,... | collective-permute-start | bytes 1179656 | tf_op jit(solution)/shard_map/ppermute | solution.py:40
  155.9 13.4 %collective-permute-start.11 = (f32[3,32768]{1,0:T(4,128)S(1)}, f32[3,32768]{1,0:T(4,128)S(1)}, u32[]{:S(2)}, u32[]{:S(2)}) collective-permute-start(f32[3,32768]{1,0:T(4,128)S(1)} %multiply_add_fusion.refs_7_), channel_id=1, source_target_pairs={{0,1},{1,0},{2,3},{3,2},{4,5},{5,4},{6,7},{7,6},{8,9},{9,8},{10,11... | collective-permute-start | bytes 1179656 | tf_op jit(solution)/shard_map/ppermute | solution.py:40
  155.9 16.5 %collective-permute-start.9 = (f32[3,32768]{1,0:T(4,128)S(1)}, f32[3,32768]{1,0:T(4,128)S(1)}, u32[]{:S(2)}, u32[]{:S(2)}) collective-permute-start(f32[3,32768]{1,0:T(4,128)S(1)} %multiply_add_fusion.refs_7_), channel_id=1, source_target_pairs={{0,2},{2,4},{3,1},{4,6},{5,3},{6,8},{7,5},{8,10},{9,7},{10,12},{11... | collective-permute-start | bytes 1179656 | tf_op jit(solution)/shard_map/ppermute | solution.py:40
  167.9 4.5 %copy-start.12 = (f32[3,32768]{1,0:T(4,128)}, f32[3,32768]{1,0:T(4,128)S(1)}, u32[]{:S(2)}) copy-start(f32[3,32768]{1,0:T(4,128)S(1)} %collective-permute-done.10.refs_6_) | copy-start | bytes 1179652
  167.9 4.5 %collective-permute-start.12 = (f32[3,32768]{1,0:T(4,128)S(1)}, f32[3,32768]{1,0:T(4,128)S(1)}, u32[]{:S(2)}, u32[]{:S(2)}) collective-permute-start(f32[3,32768]{1,0:T(4,128)S(1)} %collective-permute-done.10.refs_6_), channel_id=1, source_target_pairs={{0,1},{1,0},{2,3},{3,2},{4,5},{5,4},{6,7},{7,6},{8,9},{9,8},{10,11... | collective-permute-start | bytes 1179656 | tf_op jit(solution)/shard_map/ppermute | solution.py:40
  169.2 3.2 %copy-start.13 = (f32[3,32768]{1,0:T(4,128)}, f32[3,32768]{1,0:T(4,128)S(1)}, u32[]{:S(2)}) copy-start(f32[3,32768]{1,0:T(4,128)S(1)} %collective-permute-done.11.refs_8_) | copy-start | bytes 1179652
  (5 other events, 4.7 us)
